TPU v7x, 32 devices: a whole 2x2x4 slice. The times are simulated.
32 devices in a mesh: psg: 4 (over x, core), batch: 8 (over z, y).
Axes of the slice: x: 2, y: 2, z: 4, core: 2. Of those that a mesh axis runs over, the one named last changes fastest.
Arguments:
- decoder_in: bfloat16 [8, 128, 768], P('batch'), may hold values from -6 to 6
- encoded: bfloat16 [8, 3840, 768], P('batch', 'psg'), may hold values from -6 to 6
- cotangent: bfloat16 [8, 128, 768], P('batch'), may hold values from -6 to 6
- task_ids: int32 [8], P('batch'), may hold values from 0 to 2
- task_embed: bfloat16 [3, 768], P(None, ('psg', 'batch')), may hold values from -6 to 6
- gain_self: bfloat16 [768], P(('psg', 'batch')), may hold values from 0.5 to 1.5
- self_query: bfloat16 [768, 768], P(('psg', 'batch')), may hold values from -0.21875 to 0.21875
- self_key: bfloat16 [768, 768], P(('psg', 'batch')), may hold values from -0.21875 to 0.21875
- self_value: bfloat16 [768, 768], P(('psg', 'batch')), may hold values from -0.21875 to 0.21875
- self_output: bfloat16 [768, 768], P(('psg', 'batch')), may hold values from -0.875 to 0.875
- gain_cross: bfloat16 [768], P(('psg', 'batch')), may hold values from 0.5 to 1.5
- cross_query: bfloat16 [768, 768], P(('psg', 'batch')), may hold values from -0.21875 to 0.21875
- cross_key: bfloat16 [768, 768], P(('psg', 'batch')), may hold values from -0.21875 to 0.21875
- cross_value: bfloat16 [768, 768], P(('psg', 'batch')), may hold values from -0.21875 to 0.21875
- cross_output: bfloat16 [768, 768], P(('psg', 'batch')), may hold values from -6 to 6
- gain_hidden: bfloat16 [768], P(('psg', 'batch')), may hold values from 0.5 to 1.5
- hidden_in: bfloat16 [768, 3072], P('batch', 'psg'), may hold values from -0.21875 to 0.21875
- hidden_out: bfloat16 [3072, 768], P('psg', 'batch'), may hold values from -0.109375 to 0.109375
Outputs:
- block_out: bfloat16 [8, 128, 768], P('batch')
- grad_decoder: float32 [8, 128, 768], P('batch')
- grad_encoded: float32 [8, 3840, 768], P('batch', 'psg')
- grad_task_embed: float32 [3, 768], P(None, ('psg', 'batch'))
- grad_gain_self: float32 [768], P(('psg', 'batch'))
- grad_self_query: float32 [768, 768], P(('psg', 'batch'))
- grad_self_key: float32 [768, 768], P(('psg', 'batch'))
- grad_self_value: float32 [768, 768], P(('psg', 'batch'))
- grad_self_output: float32 [768, 768], P(('psg', 'batch'))
- grad_gain_cross: float32 [768], P(('psg', 'batch'))
- grad_cross_query: float32 [768, 768], P(('psg', 'batch'))
- grad_cross_key: float32 [768, 768], P(('psg', 'batch'))
- grad_cross_value: float32 [768, 768], P(('psg', 'batch'))
- grad_cross_output: float32 [768, 768], P(('psg', 'batch'))
- grad_gain_hidden: float32 [768], P(('psg', 'batch'))
- grad_hidden_in: float32 [768, 3072], P('batch', 'psg')
- grad_hidden_out: float32 [3072, 768], P('psg', 'batch')
All inputs are finite; a program needn't handle non-finite values.
Results may differ from a plain program's by a relative error of at most 0.023.
Values may be sent and summed in bfloat16 or wider, within the bound.
A program may use at most 192 MiB of HBM per device.

v0:
```python
import jax
import jax.numpy as jnp
from jax import lax
from jax.sharding import PartitionSpec as P

HEADS = 12
PASS_LEN = 192


EPSILON = 1e-06
MASKED = -1000000000.0


def rms_norm(values, scales):
    factor = lax.rsqrt(jnp.mean(values * values, -1, keepdims=True) + EPSILON)
    return (values * factor * scales, factor)


def rms_back(values, factor, scales, grad_out):
    scaled = grad_out * scales
    cubed = factor * factor * factor
    lower = factor * scaled - values * cubed * jnp.mean(scaled * values, -1, keepdims=True)
    return (lower, grad_out * values * factor)


def gelu_tanh(values):
    return jax.nn.gelu(values, approximate=True)


def matmul(former, latter):
    return jnp.dot(former, latter, preferred_element_type=jnp.float32)


def inner_rows(former, latter):
    return lax.dot_general(
        former, latter, (((0,), (0,)), ((), ())), preferred_element_type=jnp.float32
    )


def outer_cols(former, latter):
    return lax.dot_general(
        former, latter, (((1,), (1,)), ((), ())), preferred_element_type=jnp.float32
    )


def split_heads(values, questions):
    return values.reshape(questions, values.shape[0] // questions, HEADS, values.shape[1] // HEADS)


def key_blocks(values):
    questions, length, width = values.shape
    shaped = values.reshape(questions, length // PASS_LEN, PASS_LEN, HEADS, width // HEADS)
    return jnp.moveaxis(shaped, 1, 0)


def block_scores(queries, key_block):
    scale = queries.shape[-1] ** (-0.5)
    return (
        jnp.einsum("bqhe,bkhe->bhqk", queries, key_block, preferred_element_type=jnp.float32)
        * scale
    )


def score_stats(queries, keys):
    questions, tokens, heads, width = queries.shape
    initial = (
        jnp.full((questions, heads, tokens), -1e30, jnp.float32),
        jnp.zeros((questions, heads, tokens), jnp.float32),
    )

    def score_advance(running, key_block):
        scores = block_scores(queries, key_block)
        highest = jnp.maximum(running[0], jnp.max(scores, -1))
        totals = running[1] * jnp.exp(running[0] - highest) + jnp.sum(
            jnp.exp(scores - highest[..., None]), -1
        )
        return ((highest, totals), None)

    return lax.scan(score_advance, initial, key_blocks(keys))[0]


def weighted_values(queries, keys, values, log_total):

    def weighted_advance(running, blocks):
        chances = jnp.exp(block_scores(queries, blocks[0]) - log_total[..., None]).astype(
            jnp.bfloat16
        )
        return (
            running
            + jnp.einsum("bhqk,bkhe->bqhe", chances, blocks[1], preferred_element_type=jnp.float32),
            None,
        )

    return lax.scan(
        weighted_advance,
        jnp.zeros(queries.shape, jnp.float32),
        (key_blocks(keys), key_blocks(values)),
    )[0]


def grad_dots(queries, keys, values, log_total, grad_out):
    questions, tokens, heads, width = queries.shape

    def grad_advance(running, blocks):
        chances = jnp.exp(block_scores(queries, blocks[0]) - log_total[..., None])
        dchance = jnp.einsum(
            "bqhe,bkhe->bhqk", grad_out, blocks[1], preferred_element_type=jnp.float32
        )
        return (running + jnp.sum(chances * dchance, -1), None)

    initial = jnp.zeros((questions, heads, tokens), jnp.float32)
    return lax.scan(grad_advance, initial, (key_blocks(keys), key_blocks(values)))[0]


def cross_back(queries, keys, values, log_total, dots, grad_out, with_keys):
    scale = queries.shape[-1] ** (-0.5)

    def cross_advance(running, blocks):
        chances = jnp.exp(block_scores(queries, blocks[0]) - log_total[..., None])
        dchance = jnp.einsum(
            "bqhe,bkhe->bhqk", grad_out, blocks[1], preferred_element_type=jnp.float32
        )
        dscore = (chances * (dchance - dots[..., None])).astype(jnp.bfloat16)
        running = (
            running
            + jnp.einsum("bhqk,bkhe->bqhe", dscore, blocks[0], preferred_element_type=jnp.float32)
            * scale
        )
        if with_keys:
            dkey = (
                jnp.einsum("bhqk,bqhe->bkhe", dscore, queries, preferred_element_type=jnp.float32)
                * scale
            ).astype(jnp.bfloat16)
            dvalue = jnp.einsum(
                "bhqk,bqhe->bkhe",
                chances.astype(jnp.bfloat16),
                grad_out,
                preferred_element_type=jnp.float32,
            ).astype(jnp.bfloat16)
            return (running, (dkey, dvalue))
        return (running, None)

    query_grad, pieces = lax.scan(
        cross_advance, jnp.zeros(queries.shape, jnp.float32), (key_blocks(keys), key_blocks(values))
    )
    if not with_keys:
        return (query_grad, None)
    questions, length, width = keys.shape
    key_grad = jnp.moveaxis(pieces[0], 0, 1).reshape(questions, length, width)
    value_grad = jnp.moveaxis(pieces[1], 0, 1).reshape(questions, length, width)
    return (query_grad, (key_grad, value_grad))


def local(
    decoder_in,
    encoded,
    cotangent,
    task_ids,
    task_embed,
    gain_self,
    self_query,
    self_key,
    self_value,
    self_output,
    gain_cross,
    cross_query,
    cross_key,
    cross_value,
    cross_output,
    gain_hidden,
    hidden_in,
    hidden_out,
):
    gathered = (
        lax.all_gather(task_embed, ("psg", "batch"), axis=1, tiled=True),
        lax.all_gather(gain_self, ("psg", "batch"), axis=0, tiled=True),
        lax.all_gather(self_query, ("psg", "batch"), axis=0, tiled=True),
        lax.all_gather(self_key, ("psg", "batch"), axis=0, tiled=True),
        lax.all_gather(self_value, ("psg", "batch"), axis=0, tiled=True),
        lax.all_gather(self_output, ("psg", "batch"), axis=0, tiled=True),
        lax.all_gather(gain_cross, ("psg", "batch"), axis=0, tiled=True),
        lax.all_gather(cross_query, ("psg", "batch"), axis=0, tiled=True),
        lax.all_gather(cross_key, ("psg", "batch"), axis=0, tiled=True),
        lax.all_gather(cross_value, ("psg", "batch"), axis=0, tiled=True),
        lax.all_gather(cross_output, ("psg", "batch"), axis=0, tiled=True),
        lax.all_gather(gain_hidden, ("psg", "batch"), axis=0, tiled=True),
    )
    (
        wide_table,
        wide_gain_self,
        wide_self_query,
        wide_self_key,
        wide_self_value,
        wide_self_output,
        wide_gain_cross,
        wide_cross_query,
        wide_cross_key,
        wide_cross_value,
        wide_cross_output,
        wide_gain_hidden,
    ) = gathered
    pieces = (
        lax.all_gather(hidden_in, "batch", axis=0, tiled=True),
        lax.all_gather(hidden_out, "batch", axis=1, tiled=True),
    )
    wide_in, wide_out = (
        lax.all_gather(pieces[0], "psg", axis=1, tiled=True),
        lax.all_gather(pieces[1], "psg", axis=0, tiled=True),
    )
    questions, tokens, width = decoder_in.shape
    rows = questions * tokens
    groups = task_embed.shape[0]
    onehot = (task_ids[:, None] == jnp.arange(groups, dtype=jnp.int32)[None, :]).astype(jnp.float32)
    embed_rows = jnp.dot(onehot, wide_table.astype(jnp.float32), precision=lax.Precision.HIGHEST)
    residual_in = (decoder_in.astype(jnp.float32) + embed_rows[:, None, :]).reshape(rows, width)
    gain_one = wide_gain_self.astype(jnp.float32)
    gain_two = wide_gain_cross.astype(jnp.float32)
    gain_three = wide_gain_hidden.astype(jnp.float32)
    normed_value, factor_one = rms_norm(residual_in, gain_one)
    normed_self = normed_value.astype(jnp.bfloat16)
    query_self = split_heads(matmul(normed_self, wide_self_query).astype(jnp.bfloat16), questions)
    key_self = split_heads(matmul(normed_self, wide_self_key).astype(jnp.bfloat16), questions)
    value_self = split_heads(matmul(normed_self, wide_self_value).astype(jnp.bfloat16), questions)
    causal = jnp.arange(tokens)[:, None] >= jnp.arange(tokens)[None, :]
    scores_self = jnp.where(causal, block_scores(query_self, key_self), MASKED)
    expo = jnp.exp(scores_self - jnp.max(scores_self, -1, keepdims=True))
    chances_self = expo / jnp.sum(expo, -1, keepdims=True)
    chances_low = chances_self.astype(jnp.bfloat16)
    mixed_self = (
        jnp.einsum("bhqk,bkhe->bqhe", chances_low, value_self, preferred_element_type=jnp.float32)
        .astype(jnp.bfloat16)
        .reshape(rows, width)
    )
    after_self = residual_in + matmul(mixed_self, wide_self_output)
    normed_value, factor_two = rms_norm(after_self, gain_two)
    normed_cross = normed_value.astype(jnp.bfloat16)
    query_cross = split_heads(
        matmul(normed_cross, wide_cross_query).astype(jnp.bfloat16), questions
    )
    encoder_rows = encoded.reshape(-1, width)
    key_cross = matmul(encoder_rows, wide_cross_key).astype(jnp.bfloat16).reshape(encoded.shape)
    value_cross = matmul(encoder_rows, wide_cross_value).astype(jnp.bfloat16).reshape(encoded.shape)
    length = encoded.shape[1]
    all_keys, all_values = (
        lax.all_gather(key_cross, "psg", axis=1, tiled=True),
        lax.all_gather(value_cross, "psg", axis=1, tiled=True),
    )
    highest, totals = score_stats(query_cross, all_keys)
    log_total = highest + jnp.log(totals)
    mixed = weighted_values(query_cross, all_keys, all_values, log_total)
    mixed_cross = mixed.astype(jnp.bfloat16).reshape(rows, width)
    after_cross = after_self + matmul(mixed_cross, wide_cross_output)
    normed_value, factor_three = rms_norm(after_cross, gain_three)
    normed_hidden = normed_value.astype(jnp.bfloat16)
    pre_act = matmul(normed_hidden, wide_in)
    activation, gelu_pull = jax.vjp(gelu_tanh, pre_act)
    act_low = activation.astype(jnp.bfloat16)
    hidden_part = matmul(act_low, wide_out)
    result = after_cross + hidden_part
    block_out = result.astype(jnp.bfloat16).reshape(decoder_in.shape)
    psg_count = lax.axis_size("psg")
    row_share = rows // psg_count
    first_row = lax.axis_index("psg") * row_share

    def own(values):
        return lax.dynamic_slice_in_dim(values, first_row, row_share, 0)

    grad_top = cotangent.reshape(rows, width)
    dhidden = outer_cols(grad_top, wide_out)
    dpre = gelu_pull(dhidden)[0].astype(jnp.bfloat16)
    term_out = inner_rows(own(act_low), own(grad_top))
    term_in = inner_rows(own(normed_hidden), own(dpre))
    dnorm_hidden = outer_cols(dpre, wide_in)
    lower, gterm_three = rms_back(after_cross, factor_three, gain_three, dnorm_hidden)
    grad_after_cross = grad_top.astype(jnp.float32) + lower
    dcross = grad_after_cross.astype(jnp.bfloat16)
    term_cross_output = inner_rows(own(mixed_cross), own(dcross))
    dmixed_cross = split_heads(
        outer_cols(dcross, wide_cross_output).astype(jnp.bfloat16), questions
    )
    dots_cross = grad_dots(query_cross, all_keys, all_values, log_total, dmixed_cross)
    query_own, key_pair = cross_back(
        query_cross, key_cross, value_cross, log_total, dots_cross, dmixed_cross, True
    )
    begin = (lax.axis_index("psg") + 1) * length
    span = (psg_count - 1) * length
    other_keys = lax.dynamic_slice_in_dim(jnp.concatenate([all_keys, all_keys], 1), begin, span, 1)
    other_values = lax.dynamic_slice_in_dim(
        jnp.concatenate([all_values, all_values], 1), begin, span, 1
    )
    query_rest = cross_back(
        query_cross, other_keys, other_values, log_total, dots_cross, dmixed_cross, False
    )[0]
    query_grad = query_own + query_rest
    dquery_cross = query_grad.astype(jnp.bfloat16).reshape(rows, width)
    dkey_rows = key_pair[0].reshape(-1, width)
    dvalue_rows = key_pair[1].reshape(-1, width)
    grad_encoded = (
        outer_cols(dkey_rows, wide_cross_key) + outer_cols(dvalue_rows, wide_cross_value)
    ).reshape(encoded.shape)
    term_cross_key = inner_rows(encoder_rows, dkey_rows)
    term_cross_value = inner_rows(encoder_rows, dvalue_rows)
    term_cross_query = inner_rows(own(normed_cross), own(dquery_cross))
    dnorm_cross = outer_cols(dquery_cross, wide_cross_query)
    lower, gterm_two = rms_back(after_self, factor_two, gain_two, dnorm_cross)
    grad_after_self = grad_after_cross + lower
    dself = grad_after_self.astype(jnp.bfloat16)
    term_self_output = inner_rows(own(mixed_self), own(dself))
    dmixed_self = split_heads(outer_cols(dself, wide_self_output).astype(jnp.bfloat16), questions)
    dchance = jnp.einsum(
        "bqhe,bkhe->bhqk", dmixed_self, value_self, preferred_element_type=jnp.float32
    )
    dots_self = jnp.sum(chances_self * dchance, -1, keepdims=True)
    dscore = (chances_self * (dchance - dots_self)).astype(jnp.bfloat16)
    scale = query_self.shape[-1] ** (-0.5)
    dquery_self = (
        (
            jnp.einsum("bhqk,bkhe->bqhe", dscore, key_self, preferred_element_type=jnp.float32)
            * scale
        )
        .astype(jnp.bfloat16)
        .reshape(rows, width)
    )
    dkey_self = (
        (
            jnp.einsum("bhqk,bqhe->bkhe", dscore, query_self, preferred_element_type=jnp.float32)
            * scale
        )
        .astype(jnp.bfloat16)
        .reshape(rows, width)
    )
    dvalue_self = (
        jnp.einsum("bhqk,bqhe->bkhe", chances_low, dmixed_self, preferred_element_type=jnp.float32)
        .astype(jnp.bfloat16)
        .reshape(rows, width)
    )
    dnorm_self = (
        outer_cols(dquery_self, wide_self_query)
        + outer_cols(dkey_self, wide_self_key)
        + outer_cols(dvalue_self, wide_self_value)
    )
    normed_own = own(normed_self)
    term_self_query = inner_rows(normed_own, own(dquery_self))
    term_self_key = inner_rows(normed_own, own(dkey_self))
    term_self_value = inner_rows(normed_own, own(dvalue_self))
    lower, gterm_one = rms_back(residual_in, factor_one, gain_one, dnorm_self)
    grad_decoder = grad_after_self + lower
    row_hot = jnp.repeat(onehot, tokens, 0)
    term_table = lax.dot_general(
        own(row_hot), own(grad_decoder), (((0,), (0,)), ((), ())), precision=lax.Precision.HIGHEST
    )
    sums = (
        lax.psum_scatter(term_table, ("psg", "batch"), scatter_dimension=1, tiled=True),
        lax.psum_scatter(
            jnp.sum(own(gterm_one), 0), ("psg", "batch"), scatter_dimension=0, tiled=True
        ),
        lax.psum_scatter(term_self_query, ("psg", "batch"), scatter_dimension=0, tiled=True),
        lax.psum_scatter(term_self_key, ("psg", "batch"), scatter_dimension=0, tiled=True),
        lax.psum_scatter(term_self_value, ("psg", "batch"), scatter_dimension=0, tiled=True),
        lax.psum_scatter(term_self_output, ("psg", "batch"), scatter_dimension=0, tiled=True),
        lax.psum_scatter(
            jnp.sum(own(gterm_two), 0), ("psg", "batch"), scatter_dimension=0, tiled=True
        ),
        lax.psum_scatter(term_cross_query, ("psg", "batch"), scatter_dimension=0, tiled=True),
        lax.psum_scatter(term_cross_key, ("psg", "batch"), scatter_dimension=0, tiled=True),
        lax.psum_scatter(term_cross_value, ("psg", "batch"), scatter_dimension=0, tiled=True),
        lax.psum_scatter(term_cross_output, ("psg", "batch"), scatter_dimension=0, tiled=True),
        lax.psum_scatter(
            jnp.sum(own(gterm_three), 0), ("psg", "batch"), scatter_dimension=0, tiled=True
        ),
    )
    hidden_pair = (
        lax.psum_scatter(
            term_in.astype(jnp.bfloat16), "psg", scatter_dimension=1, tiled=True
        ).astype(jnp.float32),
        lax.psum_scatter(
            term_out.astype(jnp.bfloat16), "psg", scatter_dimension=0, tiled=True
        ).astype(jnp.float32),
    )
    hidden_grads = (
        lax.psum_scatter(hidden_pair[0], "batch", scatter_dimension=0, tiled=True),
        lax.psum_scatter(hidden_pair[1], "batch", scatter_dimension=1, tiled=True),
    )
    return (
        block_out,
        grad_decoder.reshape(decoder_in.shape),
        grad_encoded,
        sums[0],
        sums[1],
        sums[2],
        sums[3],
        sums[4],
        sums[5],
        sums[6],
        sums[7],
        sums[8],
        sums[9],
        sums[10],
        sums[11],
        hidden_grads[0],
        hidden_grads[1],
    )


def solution(mesh):
    return jax.shard_map(
        local,
        mesh=mesh,
        in_specs=(
            P("batch", None, None),
            P("batch", "psg", None),
            P("batch", None, None),
            P("batch"),
            P(None, ("psg", "batch")),
            P(("psg", "batch")),
            P(("psg", "batch"), None),
            P(("psg", "batch"), None),
            P(("psg", "batch"), None),
            P(("psg", "batch"), None),
            P(("psg", "batch")),
            P(("psg", "batch"), None),
            P(("psg", "batch"), None),
            P(("psg", "batch"), None),
            P(("psg", "batch"), None),
            P(("psg", "batch")),
            P("batch", "psg"),
            P("psg", "batch"),
        ),
        out_specs=(
            P("batch", None, None),
            P("batch", None, None),
            P("batch", "psg", None),
            P(None, ("psg", "batch")),
            P(("psg", "batch")),
            P(("psg", "batch"), None),
            P(("psg", "batch"), None),
            P(("psg", "batch"), None),
            P(("psg", "batch"), None),
            P(("psg", "batch")),
            P(("psg", "batch"), None),
            P(("psg", "batch"), None),
            P(("psg", "batch"), None),
            P(("psg", "batch"), None),
            P(("psg", "batch")),
            P("batch", "psg"),
            P("psg", "batch"),
        ),
        check_vma=False,
    )
```

profile of v0, /device:TPU:0, one launch (start us, length us, event | category | flops | bytes accessed | tf_op | source)
XLA Modules:
  0.0 1939.4 jit_solution(16193223210875318872)
XLA Ops:
  13.4 54.4 %all-gather.28.cloned.1.call-done = bf16[768,768]{1,0:T(8,128)(2,1)} async-done(((bf16[24,768]{1,0:T(8,128)(2,1)}), bf16[768,768]{1,0:T(8,128)(2,1)}) %all-gather.28.cloned.1.call-update) | async-done | bytes 1179664 | tf_op jit(solution)/shard_map/all_gather | solution.py:183
  71.6 52.2 %all-gather.26.cloned.1.call-done = bf16[768,768]{1,0:T(8,128)(2,1)} async-done(((bf16[24,768]{1,0:T(8,128)(2,1)}), bf16[768,768]{1,0:T(8,128)(2,1)}) %all-gather.26.cloned.1.call-update) | async-done | bytes 1179664 | tf_op jit(solution)/shard_map/all_gather | solution.py:184
  128.3 37.7 %all-gather.34.cloned.1.call-done = bf16[768,768]{1,0:T(8,128)(2,1)} async-done(((bf16[96,768]{1,0:T(8,128)(2,1)}), bf16[768,768]{1,0:T(8,128)(2,1)}) %all-gather.34.cloned.1.call-update) | async-done | bytes 1179664 | tf_op jit(solution)/shard_map/all_gather | solution.py:203
  166.9 39.3 %all-reduce.8 = (bf16[768]{0:T(1024)(128)(2,1)S(1)}, bf16[768]{0:T(1024)(128)(2,1)S(1)}, bf16[768]{0:T(1024)(128)(2,1)S(1)}) all-reduce(bf16[768]{0:T(1024)(128)(2,1)S(1)} %dynamic-update-slice, bf16[768]{0:T(1024)(128)(2,1)S(1)} %dynamic-update-slice.1, ...), channel_id=1, replica_groups=mesh['psg'=4,'batch'=8] {'psg','batch'}, use_global_device_ids=true, to_apply=%add | all-reduce | flops 2304 | bytes 9216
  206.2 65.6 %all-gather.2 = bf16[32,24,3]{1,2,0:T(4,128)(2,1)S(1)} all-gather(bf16[1,24,3]{1,2,0:T(4,128)(2,1)S(1)} %bitcast.381), channel_id=1, replica_groups=mesh['psg'=4,'batch'=8] {'psg','batch'}, dimensions={0}, use_global_device_ids=true | all-gather | bytes 4752 | tf_op jit(solution)/shard_map/all_gather | solution.py:175
  286.3 33.2 %all-gather.20.cloned.1.call-done = bf16[768,768]{1,0:T(8,128)(2,1)} async-done(((bf16[24,768]{1,0:T(8,128)(2,1)}), bf16[768,768]{1,0:T(8,128)(2,1)}) %all-gather.20.cloned.1.call-update) | async-done | bytes 1179664 | tf_op jit(solution)/shard_map/all_gather | solution.py:177
  321.3 54.2 %all-gather.22.cloned.1.call-done = bf16[768,768]{1,0:T(8,128)(2,1)} async-done(((bf16[24,768]{1,0:T(8,128)(2,1)}), bf16[768,768]{1,0:T(8,128)(2,1)}) %all-gather.22.cloned.1.call-update) | async-done | bytes 1179664 | tf_op jit(solution)/shard_map/all_gather | solution.py:178
  379.3 52.3 %all-gather.24.cloned.1.call-done = bf16[768,768]{1,0:T(8,128)(2,1)} async-done(((bf16[24,768]{1,0:T(8,128)(2,1)}), bf16[768,768]{1,0:T(8,128)(2,1)}) %all-gather.24.cloned.1.call-update) | async-done | bytes 1179664 | tf_op jit(solution)/shard_map/all_gather | solution.py:180
  434.1 53.4 %all-gather.30.cloned.1.call-done = bf16[768,768]{1,0:T(8,128)(2,1)} async-done(((bf16[24,768]{1,0:T(8,128)(2,1)}), bf16[768,768]{1,0:T(8,128)(2,1)}) %all-gather.30.cloned.1.call-update) | async-done | bytes 1179664 | tf_op jit(solution)/shard_map/all_gather | solution.py:182
  501.6 30.4 %all-gather.44.cloned.1.call-done = bf16[3840,768]{1,0:T(8,128)(2,1)} async-done(((bf16[960,768]{1,0:T(8,128)(2,1)}), bf16[3840,768]{1,0:T(8,128)(2,1)}) %all-gather.44.cloned.1.call-update) | async-done | bytes 5898256 | tf_op jit(solution)/shard_map/all_gather | solution.py:245
  532.0 18.5 reshape.443
  550.5 19.4 copy.106
  569.9 33.2 %while.61 = (s32[]{:T(128)}, f32[1,12,128]{2,1,0:T(8,128)S(1)}, f32[1,12,128]{2,1,0:T(8,128)S(1)}, bf16[20,1,192,12,64]{2,4,3,1,0:T(8,128)(2,1)}, bf16[1,128,12,...) while((s32[]{:T(128)}, f32[1,12,128]{2,1,0:T(8,128)S(1)}, f32[1,12,128]{2,1,0:T(8,128)S(1)}, ...), condition=%wide.region_7.8_spmd.clone, body=%wide.region_4.7_spmd.clone.sunk | while | flops 38936064 | bytes 3029092 | solution.py:79
  603.1 18.5 reshape.442
  621.5 19.4 %copy.105 = bf16[20,1,192,12,64]{2,4,3,1,0:T(8,128)(2,1)} copy(bf16[20,1,192,12,64]{4,3,2,0,1:T(8,128)(2,1)} %reshape.442) | data formatting | bytes 11796480
  641.0 35.6 %while.62 = (s32[]{:T(128)}, f32[1,128,12,64]{1,3,2,0:T(8,128)S(1)}, bf16[20,1,192,12,64]{2,4,3,1,0:T(8,128)(2,1)}, bf16[20,1,192,12,64]{2,4,3,1,0:T(8,128)(2,1)...) while((s32[]{:T(128)}, ...), condition=%wide.region_9.10_spmd.clone, body=%wide.region_8.9_spmd.clone.sunk | while | flops 76578816 | bytes 1777254 | solution.py:94
  684.0 27.6 %all-gather.40.cloned.1.call-done = bf16[3072,768]{0,1:T(8,128)(2,1)} async-done(((bf16[768,768]{0,1:T(8,128)(2,1)}), bf16[3072,768]{0,1:T(8,128)(2,1)}) %all-gather.40.cloned.1.call-update) | async-done | bytes 4718608 | tf_op jit(solution)/shard_map/all_gather | solution.py:208
  744.5 15.0 copy.116
  773.6 15.0 copy.117
  798.2 58.8 %while.63 = (s32[]{:T(128)}, f32[1,12,128]{2,1,0:T(8,128)S(1)}, bf16[20,1,192,12,64]{2,4,3,1,0:T(8,128)(2,1)}, bf16[1,128,12,64]{1,3,2,0:T(8,128)(2,1)S(1)}, f32...) while((s32[]{:T(128)}, f32[1,12,128]{2,1,0:T(8,128)S(1)}, ...), condition=%wide.region_14.15_spmd.clone, body=%wide.region_12.14_spmd.clone.sunk | while | flops 76678656 | bytes 3569783 | solution.py:112
  857.0 48.6 %while.65 = (s32[]{:T(128)}, f32[1,128,12,64]{1,3,2,0:T(8,128)S(1)}, bf16[15,1,192,12,64]{2,4,3,1,0:T(8,128)(2,1)}, bf16[1,128,12,64]{1,3,2,0:T(8,128)(2,1)S(1)}...) while((s32[]{:T(128)}, ...), condition=%wide.region_18.19_spmd.clone, body=%wide.region_17.18_spmd.clone.sunk | while | flops 115015680 | bytes 4732538 | solution.py:143
  906.5 42.4 %while.64 = (s32[]{:T(128)}, f32[1,128,12,64]{1,3,2,0:T(8,128)}, bf16[5,1,192,12,64]{2,4,3,1,0:T(8,128)(2,1)}, bf16[5,1,192,12,64]{2,4,3,1,0:T(8,128)(2,1)}, bf1...) while((s32[]{:T(128)}, f32[1,128,12,64]{1,3,2,0:T(8,128)}, ...), condition=%wide.region_16.17_spmd.clone, body=%wide.region_15.16_spmd.clone.sunk | while | flops 191250432 | bytes 8859803 | solution.py:143
  1025.2 39.9 %all-reduce.7 = (f32[3,768]{1,0:T(4,128)S(1)}, f32[768]{0:T(1024)S(1)}, f32[768]{0:T(1024)S(1)}, f32[768]{0:T(1024)S(1)}) all-reduce(f32[3,768]{1,0:T(4,128)S(1)} %fusion.130, f32[768]{0:T(1024)S(1)} %fusion.129, f32[768]{0:T(1024)S(1)} %fusion.127, f32[768]{0:T(1024)S(1)} %fusion.125), channel_id=4, replica_groups=mesh['psg'=4,'batch'=8] {'psg','batch'}, use_global_device_ids=true, to_apply=%region_22.23.clone | all-reduce | flops 4608 | bytes 36864
  1079.0 83.3 %reduce-scatter.22.cloned.1.call-done = f32[24,768]{1,0:T(8,128)} async-done(((f32[768,768]{1,0:T(8,128)}), f32[24,768]{1,0:T(8,128)}) %reduce-scatter.22.cloned.1.call-update) | async-done | bytes 73744 | tf_op jit(solution)/shard_map/reduce_scatter | solution.py:358
  1162.4 103.9 %reduce-scatter.24.cloned.1.call-done = f32[24,768]{1,0:T(8,128)} async-done(((f32[768,768]{1,0:T(8,128)}), f32[24,768]{1,0:T(8,128)}) %reduce-scatter.24.cloned.1.call-update) | async-done | bytes 73744 | tf_op jit(solution)/shard_map/reduce_scatter | solution.py:359
  1266.3 104.6 %reduce-scatter.26.cloned.1.call-done = f32[24,768]{1,0:T(8,128)} async-done(((f32[768,768]{1,0:T(8,128)}), f32[24,768]{1,0:T(8,128)}) %reduce-scatter.26.cloned.1.call-update) | async-done | bytes 73744 | tf_op jit(solution)/shard_map/reduce_scatter | solution.py:360
  1370.8 103.9 %reduce-scatter.28.cloned.1.call-done = f32[24,768]{1,0:T(8,128)} async-done(((f32[768,768]{1,0:T(8,128)}), f32[24,768]{1,0:T(8,128)}) %reduce-scatter.28.cloned.1.call-update) | async-done | bytes 73744 | tf_op jit(solution)/shard_map/reduce_scatter | solution.py:364
  1474.7 104.8 %reduce-scatter.38.cloned.1.call-done = f32[24,768]{1,0:T(8,128)} async-done(((f32[768,768]{1,0:T(8,128)}), f32[24,768]{1,0:T(8,128)}) %reduce-scatter.38.cloned.1.call-update) | async-done | bytes 73744
  1579.6 103.9 %reduce-scatter.40.cloned.1.call-done = f32[24,768]{1,0:T(8,128)} async-done(((f32[768,768]{1,0:T(8,128)}), f32[24,768]{1,0:T(8,128)}) %reduce-scatter.40.cloned.1.call-update) | async-done | bytes 73744
  1683.5 104.6 %reduce-scatter.30.cloned.1.call-done = f32[24,768]{1,0:T(8,128)} async-done(((f32[768,768]{1,0:T(8,128)}), f32[24,768]{1,0:T(8,128)}) %reduce-scatter.30.cloned.1.call-update) | async-done | bytes 73744 | tf_op jit(solution)/shard_map/reduce_scatter | solution.py:367
  1788.1 72.3 %reduce-scatter.34.cloned.1.call-done = f32[96,768]{1,0:T(8,128)} async-done(((f32[768,768]{1,0:T(8,128)}), f32[96,768]{1,0:T(8,128)}) %reduce-scatter.34.cloned.1.call-update) | async-done | bytes 294928 | tf_op jit(solution)/shard_map/reduce_scatter | solution.py:381
  1860.4 72.2 %reduce-scatter.42.cloned.1.call-done = f32[96,768]{1,0:T(8,128)} async-done(((f32[768,768]{1,0:T(8,128)}), f32[96,768]{1,0:T(8,128)}) %reduce-scatter.42.cloned.1.call-update) | async-done | bytes 294928
  (497 shorter events, 420.4 us)
Async XLA Ops:
  7.2 60.7 %copy-start = (bf16[1,960,768]{2,1,0:T(8,128)(2,1)S(1)}, bf16[1,960,768]{2,1,0:T(8,128)(2,1)}, u32[]{:S(2)}) copy-start(bf16[1,960,768]{2,1,0:T(8,128)(2,1)} %param.29) | copy-start | bytes 4423684
  7.2 60.7 %all-gather.28.cloned.1.call-start = ((), (), s32[]{:S(2)}) async-start(), calls=%async_computation.17 | async-start | bytes 1216512 | tf_op jit(solution)/shard_map/all_gather | solution.py:183
  7.9 115.9 %all-gather.26.cloned.1.call-start = ((), (), s32[]{:S(2)}) async-start(), calls=%async_computation.16 | async-start | bytes 1216512 | tf_op jit(solution)/shard_map/all_gather | solution.py:184
  8.7 157.3 %all-gather.34.cloned.1.call-start = ((), (), s32[]{:S(2)}) async-start(), calls=%async_computation.20 | async-start | bytes 1327104 | tf_op jit(solution)/shard_map/all_gather | solution.py:203
  9.4 263.6 %all-gather.38.cloned.1.call-start = ((), (), s32[]{:S(2)}) async-start(), calls=%async_computation.22 | async-start | bytes 1327104 | tf_op jit(solution)/shard_map/all_gather | solution.py:204
  10.0 274.5 %all-gather.18.cloned.1.call-start = ((), (), s32[]{:S(2)}) async-start(), calls=%async_computation.12 | async-start | bytes 1216512 | tf_op jit(solution)/shard_map/all_gather | solution.py:179
  10.6 308.9 %all-gather.20.cloned.1.call-start = ((), (), s32[]{:S(2)}) async-start(), calls=%async_computation.13 | async-start | bytes 1216512 | tf_op jit(solution)/shard_map/all_gather | solution.py:177
  11.2 364.4 %all-gather.22.cloned.1.call-start = ((), (), s32[]{:S(2)}) async-start(), calls=%async_computation.14 | async-start | bytes 1216512 | tf_op jit(solution)/shard_map/all_gather | solution.py:178
  11.9 419.6 %all-gather.24.cloned.1.call-start = ((), (), s32[]{:S(2)}) async-start(), calls=%async_computation.15 | async-start | bytes 1216512 | tf_op jit(solution)/shard_map/all_gather | solution.py:180
  12.7 474.9 %all-gather.30.cloned.1.call-start = ((), (), s32[]{:S(2)}) async-start(), calls=%async_computation.18 | async-start | bytes 1216512 | tf_op jit(solution)/shard_map/all_gather | solution.py:182
  13.4 518.6 %all-gather.44.cloned.1.call-start = ((), (), s32[]{:S(2)}) async-start(), calls=%async_computation.34 | async-start | bytes 7372800 | tf_op jit(solution)/shard_map/all_gather | solution.py:245
  71.6 531.5 %all-gather.42.cloned.1.call-start = ((), (), s32[]{:S(2)}) async-start(), calls=%async_computation.33 | async-start | bytes 7372800 | tf_op jit(solution)/shard_map/all_gather | solution.py:246
  127.6 78.6 %copy-start.42 = (bf16[3,24]{1,0:T(4,128)(2,1)S(1)}, bf16[3,24]{1,0:T(4,128)(2,1)}, u32[]{:S(2)}) copy-start(bf16[3,24]{1,0:T(4,128)(2,1)} %param.32) | copy-start | bytes 436
  127.6 145.1 %copy-start.7 = (bf16[1,128,768]{2,1,0:T(8,128)(2,1)S(1)}, bf16[1,128,768]{2,1,0:T(8,128)(2,1)}, u32[]{:S(2)}) copy-start(bf16[1,128,768]{2,1,0:T(8,128)(2,1)} %param.28) | copy-start | bytes 589828
  127.7 549.0 %all-gather.32.cloned.1.call-start = ((), (), s32[]{:S(2)}) async-start(), calls=%async_computation.19 | async-start | bytes 1216512 | tf_op jit(solution)/shard_map/all_gather | solution.py:185
  128.2 550.4 %all-gather.36.cloned.1.call-start = ((), (), s32[]{:S(2)}) async-start(), calls=%async_computation.21 | async-start | bytes 5898240 | tf_op jit(solution)/shard_map/all_gather | solution.py:207
  166.1 545.5 %all-gather.40.cloned.1.call-start = ((), (), s32[]{:S(2)}) async-start(), calls=%async_computation.23 | async-start | bytes 5898240 | tf_op jit(solution)/shard_map/all_gather | solution.py:208
  273.0 102.5 %copy-start.14 = (bf16[128,768]{1,0:T(8,128)(2,1)}, bf16[128,768]{1,0:T(8,128)(2,1)S(1)}, u32[]{:S(2)}) copy-start(bf16[128,768]{1,0:T(8,128)(2,1)S(1)} %multiply_convert_fusion.4) | copy-start | bytes 589828
  273.1 740.2 %reduce-scatter.32.cloned.1.call-start = ((), (), s32[]{:S(2)}) async-start(), calls=%async_computation.30 | async-start | bytes 5898240 | tf_op jit(solution)/shard_map/reduce_scatter | solution.py:373
  286.3 92.3 %copy-start.39 = (bf16[128,768]{0,1:T(8,128)(2,1)}, bf16[128,768]{0,1:T(8,128)(2,1)S(1)}, u32[]{:S(2)}) copy-start(bf16[128,768]{0,1:T(8,128)(2,1)S(1)} %copy.97) | copy-start | bytes 589828
  434.1 61.2 %copy-start.26 = (bf16[128,768]{1,0:T(8,128)(2,1)}, bf16[128,768]{1,0:T(8,128)(2,1)S(1)}, u32[]{:S(2)}) copy-start(bf16[128,768]{1,0:T(8,128)(2,1)S(1)} %multiply_convert_fusion.3) | copy-start | bytes 589828
  793.2 223.1 %reduce-scatter.36.cloned.1.call-start = ((), (), s32[]{:S(2)}) async-start(), calls=%async_computation.32 | async-start | bytes 5898240 | tf_op jit(solution)/shard_map/reduce_scatter | solution.py:376
  857.0 222.0 %reduce-scatter.20.cloned.1.call-start = ((), (), s32[]{:S(2)}) async-start(), calls=%async_computation.24 | async-start | bytes 2433024 | tf_op jit(solution)/shard_map/reduce_scatter | solution.py:357
  958.7 203.7 %reduce-scatter.22.cloned.1.call-start = ((), (), s32[]{:S(2)}) async-start(), calls=%async_computation.25 | async-start | bytes 2433024 | tf_op jit(solution)/shard_map/reduce_scatter | solution.py:358
  962.0 304.2 %reduce-scatter.24.cloned.1.call-start = ((), (), s32[]{:S(2)}) async-start(), calls=%async_computation.26 | async-start | bytes 2433024 | tf_op jit(solution)/shard_map/reduce_scatter | solution.py:359
  968.2 402.7 %reduce-scatter.26.cloned.1.call-start = ((), (), s32[]{:S(2)}) async-start(), calls=%async_computation.27 | async-start | bytes 2433024 | tf_op jit(solution)/shard_map/reduce_scatter | solution.py:360
  971.9 502.9 %reduce-scatter.28.cloned.1.call-start = ((), (), s32[]{:S(2)}) async-start(), calls=%async_computation.28 | async-start | bytes 2433024 | tf_op jit(solution)/shard_map/reduce_scatter | solution.py:364
  974.7 604.9 %reduce-scatter.38.cloned.1.call-start = ((), (), s32[]{:S(2)}) async-start(), calls=%async_computation.35 | async-start | bytes 2433024
  992.4 691.1 %reduce-scatter.40.cloned.1.call-start = ((), (), s32[]{:S(2)}) async-start(), calls=%async_computation.36 | async-start | bytes 2433024
  1009.6 778.5 %reduce-scatter.30.cloned.1.call-start = ((), (), s32[]{:S(2)}) async-start(), calls=%async_computation.29 | async-start | bytes 2433024 | tf_op jit(solution)/shard_map/reduce_scatter | solution.py:367
  1013.2 847.2 %reduce-scatter.34.cloned.1.call-start = ((), (), s32[]{:S(2)}) async-start(), calls=%async_computation.31 | async-start | bytes 2654208 | tf_op jit(solution)/shard_map/reduce_scatter | solution.py:381
  1016.2 916.4 %reduce-scatter.42.cloned.1.call-start = ((), (), s32[]{:S(2)}) async-start(), calls=%async_computation.37 | async-start | bytes 2654208
  (41 other events, 480.6 us)
Sparse Core Ops, SparseCore 0:
  10.9 56.8 all-gather.27
  70.8 53.0 all-gather.25
  126.1 39.9 all-gather.33
  168.1 39.7 all-gather.37
  210.6 53.0 all-gather.17
  266.4 53.0 all-gather.19
  322.4 53.0 all-gather.21
  378.4 53.0 all-gather.23
  434.5 53.0 all-gather.29
  489.0 43.0 all-gather.43
  533.6 44.1 all-gather.41
  580.5 54.1 all-gather.31
  636.3 36.3 all-gather.35
  674.1 37.4 all-gather.39
  793.3 47.8 reduce-scatter.31
  857.1 47.7 reduce-scatter.35
  958.8 98.8 reduce-scatter.19
  1064.3 98.0 reduce-scatter.21
  1168.2 97.9 reduce-scatter.23
  1272.8 97.9 reduce-scatter.25
  1376.7 97.9 reduce-scatter.27
  1481.5 98.0 reduce-scatter.37
  1585.4 97.9 reduce-scatter.39
  1690.1 98.0 reduce-scatter.29
  1792.2 68.1 reduce-scatter.33
  1864.4 68.2 reduce-scatter.41
where the time goes:
time: 1950 us; the launch traced here: 1940 us
  waiting for transfers between devices  1260 us (65%)
  matrix products  298 us (15%)
  local copies, waits for them, and re-layouts  198 us (10%)
  blocking collectives  145 us (7%)
  other arithmetic  21.2 us (1%)
    unnamed x29, waiting for transfers between devices  287 us
    reduce_scatter x1, waiting for transfers between devices, local(): lax.psum_scatter(term_cross_output, ('psg', 'batch'), scatter_dimension=0...  105 us
    reduce_scatter x1, waiting for transfers between devices, local(): lax.psum_scatter(term_self_output, ('psg', 'batch'), scatter_dimension=0,...  105 us
    reduce_scatter x1, waiting for transfers between devices, local(): lax.psum_scatter(term_cross_query, ('psg', 'batch'), scatter_dimension=0,...  104 us
    reduce_scatter x1, waiting for transfers between devices, local(): lax.psum_scatter(term_self_value, ('psg', 'batch'), scatter_dimension=0,...  104 us
    unnamed x114, local copies, waits for them, and re-layouts  100 us
    dot_general x60, matrix products, block_scores(): jnp.einsum('bqhe,bkhe->bhqk', queries, key_block, preferred_element_type=...  84.6 us
    reduce_scatter x1, waiting for transfers between devices, local(): lax.psum_scatter(term_self_key, ('psg', 'batch'), scatter_dimension=0, ti...  83.3 us
  transfers between devices with their start and end apart: 26, of which 18 were waited for; matrix products, arithmetic and copies ran while one was open for 22% of the time, Pallas kernels for 0%

commit v1 on v0

v1 whole, which is shorter than its diff:
```python
import functools

import jax
import jax.numpy as jnp
from jax import lax
from jax.experimental import pallas as pl
from jax.experimental.pallas import tpu as pltpu
from jax.sharding import PartitionSpec as P

HEADS = 12
EPSILON = 1e-06
MASKED = -1000000000.0
LANES = 128
SMALL_ROWS = 16
MAX_BLOCKS = 32
MIB = 2**20

F32 = jnp.float32
BF16 = jnp.bfloat16
ID = pl.DeviceIdType.MESH
VMEM = pl.BlockSpec(memory_space=pltpu.VMEM)
ANY = pl.BlockSpec(memory_space=pl.ANY)


def nn(former, latter):
    return jnp.dot(former, latter, preferred_element_type=F32)


def nt(former, latter):
    return lax.dot_general(former, latter, (((1,), (1,)), ((), ())), preferred_element_type=F32)


def rms_factor(values):
    return lax.rsqrt(jnp.mean(values * values, -1, keepdims=True) + EPSILON)


def rms_back(values, factor, scales, grad_out):
    scaled = grad_out * scales
    cubed = factor * factor * factor
    return factor * scaled - values * cubed * jnp.mean(scaled * values, -1, keepdims=True)


def lane_is_low():
    return lax.broadcasted_iota(jnp.int32, (1, LANES), 1) < LANES // 2


def stack_heads(pair):
    low = lane_is_low()
    zero = jnp.zeros_like(pair)
    return jnp.concatenate([jnp.where(low, pair, zero), jnp.where(low, zero, pair)], 0)


def merge_heads(stacked):
    half = stacked.shape[0] // 2
    return jnp.where(lane_is_low(), stacked[:half], stacked[half:])


def stack_stat(stats, pair):
    return jnp.concatenate([stats[:, 2 * pair : 2 * pair + 1], stats[:, 2 * pair + 1 : 2 * pair + 2]], 0)


def spread_stat(stats, pair):
    return jnp.where(
        lane_is_low(), stats[:, 2 * pair : 2 * pair + 1], stats[:, 2 * pair + 1 : 2 * pair + 2]
    )


def remote(src, dst, send, recv, device):
    return pltpu.make_async_remote_copy(
        src_ref=src, dst_ref=dst, send_sem=send, recv_sem=recv, device_id=device, device_id_type=ID
    )


def place():
    index, question = lax.axis_index("psg"), lax.axis_index("batch")
    return index, question


def line_barrier(spans, extra):
    index, question = place()
    far, near = question // 2, question % 2
    barrier = pltpu.get_barrier_semaphore()

    @pl.when(far < spans - 1)
    def _():
        pl.semaphore_signal(barrier, inc=1, device_id=(index, question + 2), device_id_type=ID)

    @pl.when(far > 0)
    def _():
        pl.semaphore_signal(barrier, inc=1, device_id=(index, question - 2), device_id_type=ID)

    others = [(index, far * 2 + 1 - near)] + extra
    for other in others:
        pl.semaphore_signal(barrier, inc=1, device_id=other, device_id_type=ID)
    line = jnp.where(far < spans - 1, 1, 0) + jnp.where(far > 0, 1, 0)
    pl.semaphore_wait(barrier, line + len(others))


def gather_kernel(spans, a_ref, f_ref, s_ref, a_out, f_out, s_out, own_sem, *sems):
    a_recv, a_up, a_down, a_y, a_x, a_c, s_recv, s_up, s_down, s_y, s_x, s_c, f_recv, f_up, f_down, f_y = sems
    index, question = place()
    far, near = question // 2, question % 2
    side, core = index // 2, index % 2
    count = spans * 2
    x_peer = (1 - side) * 2 + core
    c_peer = side * 2 + 1 - core
    line_barrier(spans, [(x_peer, question), (c_peer, question)])

    own = [
        pltpu.make_async_copy(a_ref, a_out.at[index, question], own_sem.at[0]),
        pltpu.make_async_copy(s_ref, s_out.at[index, question], own_sem.at[1]),
        pltpu.make_async_copy(f_ref, f_out.at[question], own_sem.at[2]),
    ]
    for copy in own:
        copy.start()

    def ways(block, mine, up, down, across, wide):
        z = block // 2
        kinds = (
            (a_ref, a_out.at[index, block], a_recv.at[index * count + block], a_up, a_down, a_y),
            (s_ref, s_out.at[index, block], s_recv.at[index * count + block], s_up, s_down, s_y),
            (f_ref, f_out.at[block], f_recv.at[block], f_up, f_down, f_y),
        )
        out = []
        for own_ref, spot, recv, sem_up, sem_down, sem_y in kinds:
            src = own_ref if mine else spot
            if up:
                out.append((far < spans - 1, remote(src, spot, sem_up.at[z], recv, (index, question + 2))))
            if down:
                out.append((far > 0, remote(src, spot, sem_down.at[z], recv, (index, question - 2))))
            if across:
                out.append((None, remote(src, spot, sem_y.at[z], recv, (index, far * 2 + 1 - near))))
        return out

    def wides(owner, block, mine, to_x, to_core):
        kinds = (
            (a_ref, a_out.at[owner, block], a_recv.at[owner * count + block], a_x, a_c),
            (s_ref, s_out.at[owner, block], s_recv.at[owner * count + block], s_x, s_c),
        )
        out = []
        for own_ref, spot, recv, sem_x, sem_c in kinds:
            src = own_ref if mine else spot
            if to_x:
                out.append((None, remote(src, spot, sem_x.at[block], recv, (x_peer, question))))
            if to_core:
                out.append((None, remote(src, spot, sem_c.at[(owner // 2) * count + block], recv, (c_peer, question))))
        return out

    def each(copies, act):
        for when, copy in copies:
            if when is None:
                act(copy)
            else:
                pl.when(when)(functools.partial(act, copy))

    def start(copies):
        each(copies, lambda copy: copy.start())

    def arrived(owner, block, with_f):
        spot = a_out.at[owner, block]
        remote(spot, spot, a_c.at[0], a_recv.at[owner * count + block], (c_peer, question)).wait_recv()
        spot = s_out.at[owner, block]
        remote(spot, spot, s_c.at[0], s_recv.at[owner * count + block], (c_peer, question)).wait_recv()
        if with_f:
            spot = f_out.at[block]
            remote(spot, spot, f_y.at[0], f_recv.at[block], (c_peer, question)).wait_recv()

    start(ways(question, True, True, True, True, True))
    start(wides(index, question, True, True, True))

    def from_y(z):
        block = z * 2 + 1 - near
        arrived(index, block, True)
        start(wides(index, block, False, True, True))

    def from_x(block):
        arrived(x_peer, block, False)
        start(wides(x_peer, block, False, False, True))

    from_y(far)
    from_x(question)
    for step in range(1, spans):
        for sign in (-1, 1):
            z = far + sign * step
            block = z * 2 + near

            @pl.when((z >= 0) & (z < spans))
            def _(z=z, block=block, sign=sign):
                arrived(index, block, True)
                start(ways(block, False, sign < 0, sign > 0, True, True))
                start(wides(index, block, False, True, True))

        for sign in (-1, 1):
            z = far + sign * step

            @pl.when((z >= 0) & (z < spans))
            def _(z=z):
                from_y(z)

        if step == 1:
            from_x(far * 2 + 1 - near)
        for sign in (-1, 1):
            z = far + sign * step

            @pl.when((z >= 0) & (z < spans))
            def _(z=z):
                from_x(z * 2 + near)

    for step in range(1, spans):
        for sign in (-1, 1):
            z = far + sign * step

            @pl.when((z >= 0) & (z < spans))
            def _(z=z):
                from_x(z * 2 + 1 - near)

    for block in range(count):
        arrived(c_peer, block, False)
        arrived((1 - side) * 2 + 1 - core, block, False)

    for copy in own:
        copy.wait()

    def done(copies):
        each(copies, lambda copy: copy.wait_send())

    done(ways(question, True, True, True, True, True))
    done(wides(index, question, True, True, True))
    for step in range(1, spans):
        for sign in (-1, 1):
            z = far + sign * step

            @pl.when((z >= 0) & (z < spans))
            def _(z=z, sign=sign):
                done(ways(z * 2 + near, False, sign < 0, sign > 0, True, True))
                done(wides(index, z * 2 + near, False, True, True))

    for z in range(spans):
        done(wides(index, z * 2 + 1 - near, False, True, True))
    for block in range(count):
        done(wides(x_peer, block, False, False, True))


def gather_all(attn, hidden, small, psg, batch):
    if not regular(attn.shape[0] // 8, psg, batch):
        return (
            lax.all_gather(lax.all_gather(attn, "batch"), "psg"),
            lax.all_gather(hidden, "batch"),
            lax.all_gather(lax.all_gather(small, "batch"), "psg"),
        )
    spans = batch // 2
    dma = pltpu.SemaphoreType.DMA
    wide = [dma((psg * batch,))] + [dma((spans,))] * 3 + [dma((batch,)), dma((2 * batch,))]
    return pl.pallas_call(
        functools.partial(gather_kernel, spans),
        out_shape=(
            jax.ShapeDtypeStruct((psg, batch) + attn.shape, attn.dtype),
            jax.ShapeDtypeStruct((batch,) + hidden.shape, hidden.dtype),
            jax.ShapeDtypeStruct((psg, batch) + small.shape, small.dtype),
        ),
        in_specs=[ANY] * 3,
        out_specs=[ANY] * 3,
        scratch_shapes=[dma((3,))] + wide + wide + [dma((batch,))] + [dma((spans,))] * 3,
        compiler_params=pltpu.CompilerParams(collective_id=0, has_side_effects=True),
        name="gather_weights",
    )(attn, hidden, small)


def regular(owned, psg, batch):
    return psg == 4 and batch % 2 == 0 and psg * batch <= MAX_BLOCKS and owned % 8 == 0


def psg_start(psg, parts, send, recv):
    me, question = place()
    for hop in range(1, psg):
        peer = lax.rem(me + hop, psg)
        for row, (src, dst, scatter) in enumerate(parts):
            source = src.at[peer] if scatter else src
            remote(source, dst.at[me], send.at[row, hop], recv.at[row, me], (peer, question)).start()


def psg_wait(psg, parts, send, recv):
    me, question = place()
    for hop in range(1, psg):
        peer = lax.rem(me + hop, psg)
        for row, (src, dst, scatter) in enumerate(parts):
            source = src.at[peer] if scatter else src
            remote(source, dst.at[peer], send.at[row, hop], recv.at[row, peer], (peer, question)).wait_recv()
    for hop in range(1, psg):
        peer = lax.rem(me + hop, psg)
        for row, (src, dst, scatter) in enumerate(parts):
            source = src.at[peer] if scatter else src
            remote(source, dst.at[me], send.at[row, hop], recv.at[row, me], (peer, question)).wait_send()


def psg_barrier(psg):
    me, question = place()
    barrier = pltpu.get_barrier_semaphore()
    for hop in range(1, psg):
        pl.semaphore_signal(
            barrier, inc=1, device_id=(lax.rem(me + hop, psg), question), device_id_type=ID
        )
    pl.semaphore_wait(barrier, psg - 1)


def reduce_kernel(spans, kv_ref, a_ref, f_ref, s_ref, kv_out, a_out, f_out, s_out,
                  kv_core, kv_x, kv_mid, kv_acc, s_buf, s_recv, x_sem, s_sem, *rest):
    names = ("from_y", "acc", "from_up", "from_down", "y_send", "y_recv", "line_send", "up_recv", "down_recv")
    kv_kit, a_kit, f_kit = [dict(zip(names, rest[i * len(names) :])) for i in range(3)]
    index, question = place()
    far, near = question // 2, question % 2
    side, core = index // 2, index % 2
    x_peer = (1 - side) * 2 + core
    c_peer = side * 2 + 1 - core
    y_peer = far * 2 + 1 - near
    barrier = pltpu.get_barrier_semaphore()
    column = [(index, lax.rem(far + hop, spans) * 2 + near) for hop in range(1, spans)]
    greeted = column + [(index, y_peer), (x_peer, question), (c_peer, question)]
    for other in greeted:
        pl.semaphore_signal(barrier, inc=1, device_id=other, device_id_type=ID)
    pl.semaphore_wait(barrier, len(greeted))

    def y_copy(src, kit, z):
        return remote(
            src.at[z * 2 + 1 - near], kit["from_y"].at[z], kit["y_send"].at[z], kit["y_recv"].at[z], (index, y_peer)
        )

    def line(kit, z, up):
        slot, recv = (kit["from_up"], kit["up_recv"]) if up else (kit["from_down"], kit["down_recv"])
        return remote(
            kit["acc"].at[z], slot.at[z], kit["line_send"].at[z], recv.at[z],
            (index, question + 2 if up else question - 2),
        )

    def own_sum(src, kit, z):
        y_copy(src, kit, z).wait_recv()
        return src[z * 2 + near].astype(F32) + kit["from_y"][z].astype(F32)

    def along(src, kit):
        for step in range(spans):
            for up, z in ((False, step), (True, spans - 1 - step)):
                behind = far > 0 if up else far < spans - 1

                @pl.when(z > far if up else z < far)
                def _(z=z, up=up, behind=behind):
                    total = own_sum(src, kit, z)

                    @pl.when(behind)
                    def _():
                        line(kit, z, up).wait_recv()
                        slot = kit["from_up"] if up else kit["from_down"]
                        kit["acc"][z] = (total + slot[z].astype(F32)).astype(BF16)

                    @pl.when(jnp.logical_not(behind))
                    def _():
                        kit["acc"][z] = total.astype(BF16)

                    line(kit, z, up).start()

    def finish(src, kit, out):
        out[...] = own_sum(src, kit, far)

        @pl.when(far < spans - 1)
        def _():
            line(kit, far, False).wait_recv()
            out[...] = out[...] + kit["from_down"][far].astype(F32)

        @pl.when(far > 0)
        def _():
            line(kit, far, True).wait_recv()
            out[...] = out[...] + kit["from_up"][far].astype(F32)

    def sent(src, kit):
        for z in range(spans):
            y_copy(src, kit, z).wait_send()
            pl.when(z < far)(lambda z=z: line(kit, z, False).wait_send())
            pl.when(z > far)(lambda z=z: line(kit, z, True).wait_send())

    order = [z for step in range((spans + 1) // 2) for z in sorted({step, spans - 1 - step})]

    def y_start(src, kit):
        for z in order:
            y_copy(src, kit, z).start()

    def pair(slot, device):
        return remote(s_buf.at[slot], s_recv.at[slot], s_sem.at[0, slot], s_sem.at[1, slot], device)

    def small(z, mine):
        return remote(s_buf.at[3], s_recv.at[3 + mine], s_sem.at[2, z], s_sem.at[3, mine], (index, z * 2 + near))

    s_core, s_x, s_y = pair(0, (c_peer, question)), pair(1, (x_peer, question)), pair(2, (index, y_peer))
    core_copy = remote(kv_ref.at[1 - core], kv_core, x_sem.at[0], x_sem.at[1], (c_peer, question))
    core_copy.start()
    s_buf[0] = s_ref[...]
    s_core.start()
    y_start(f_ref, f_kit)
    y_start(a_ref, a_kit)

    core_copy.wait()
    kv_mid[...] = (kv_ref[core, 1 - side].astype(F32) + kv_core[1 - side].astype(F32)).astype(BF16)
    x_copy = remote(kv_mid, kv_x, x_sem.at[2], x_sem.at[3], (x_peer, question))
    x_copy.start()
    s_core.wait()
    s_buf[1] = s_buf[0] + s_recv[0]
    s_x.start()
    x_copy.wait()
    kv_acc[...] = (
        kv_ref[core, side].astype(F32) + kv_core[side].astype(F32) + kv_x[...].astype(F32)
    ).astype(BF16)
    y_start(kv_acc, kv_kit)
    s_x.wait()
    s_buf[2] = s_buf[1] + s_recv[1]
    s_y.start()

    along(f_ref, f_kit)
    s_y.wait()
    s_buf[3] = s_buf[2] + s_recv[2]
    for hop in range(1, spans):
        small(lax.rem(far + hop, spans), far).start()
    along(a_ref, a_kit)
    along(kv_acc, kv_kit)
    finish(f_ref, f_kit, f_out)
    finish(a_ref, a_kit, a_out)
    finish(kv_acc, kv_kit, kv_out)
    s_out[...] = s_buf[3]
    for hop in range(1, spans):
        z = lax.rem(far + hop, spans)
        small(z, z).wait_recv()
        s_out[...] = s_out[...] + s_recv[3 + z]
    for hop in range(1, spans):
        small(lax.rem(far + hop, spans), far).wait_send()
    for src, kit in ((f_ref, f_kit), (a_ref, a_kit), (kv_acc, kv_kit)):
        sent(src, kit)


def reduce_all(kv, attn, hidden, small, psg, batch):
    width = attn.shape[-1]
    if not regular(attn.shape[1] // 6, psg, batch):
        both = ("psg", "batch")
        return (
            lax.psum_scatter(kv.reshape((-1,) + kv.shape[2:]).astype(F32), both, tiled=True)[0],
            lax.psum_scatter(attn.astype(F32), "batch", tiled=True)[0],
            lax.psum_scatter(hidden.astype(F32), "batch", tiled=True)[0],
            lax.psum(small, both),
        )
    spans = batch // 2
    dma = pltpu.SemaphoreType.DMA

    def kit(rows):
        return [pltpu.VMEM((spans, rows, width), BF16)] * 4 + [dma((spans,))] * 5

    rows = [value.shape[-2] for value in (kv, attn, hidden)]
    block = (batch, rows[0], width)
    cored = jnp.swapaxes(kv.reshape((psg // 2, 2) + block), 0, 1)
    return pl.pallas_call(
        functools.partial(reduce_kernel, spans),
        out_shape=tuple(jax.ShapeDtypeStruct((n, width), F32) for n in rows + [small.shape[0]]),
        in_specs=[VMEM] * 4,
        out_specs=[VMEM] * 4,
        scratch_shapes=[
            pltpu.VMEM((2,) + block, BF16),
            pltpu.VMEM(block, BF16),
            pltpu.VMEM(block, BF16),
            pltpu.VMEM(block, BF16),
            pltpu.VMEM((4,) + small.shape, F32),
            pltpu.VMEM((3 + spans,) + small.shape, F32),
            dma((4,)),
            dma((4, max(spans, 3))),
        ] + kit(rows[0]) + kit(rows[1]) + kit(rows[2]),
        compiler_params=pltpu.CompilerParams(collective_id=1, has_side_effects=True, vmem_limit_bytes=48 * MIB),
        name="reduce_grads",
    )(cored, attn, hidden, small)


def self_forward(dec, row, g1, wq, wk, wv, wo, g2, wcq, res, n1, q, k, v, probs, mix, after, n2, qc):
    x = dec[...].astype(F32) + row[...]
    res[...] = x
    normed = (x * rms_factor(x) * g1[...]).astype(BF16)
    n1[...] = normed
    q[...] = nn(normed, wq[...]).astype(BF16)
    k[...] = nn(normed, wk[...]).astype(BF16)
    v[...] = nn(normed, wv[...]).astype(BF16)
    tokens, width = x.shape
    scale = (width // HEADS) ** (-0.5)
    rows = lax.broadcasted_iota(jnp.int32, (2 * tokens, tokens), 0) % tokens
    causal = rows >= lax.broadcasted_iota(jnp.int32, (2 * tokens, tokens), 1)
    for pair in range(HEADS // 2):
        cols = slice(pair * LANES, (pair + 1) * LANES)
        scores = jnp.where(causal, nt(stack_heads(q[:, cols]), k[:, cols]) * scale, MASKED)
        expo = jnp.exp(scores - jnp.max(scores, -1, keepdims=True))
        chances = expo * (1.0 / jnp.sum(expo, -1, keepdims=True))
        probs[pair] = chances
        mix[:, cols] = merge_heads(nn(chances.astype(BF16), v[:, cols])).astype(BF16)
    y = x + nn(mix[...], wo[...])
    after[...] = y
    crossed = (y * rms_factor(y) * g2[...]).astype(BF16)
    n2[...] = crossed
    qc[...] = nn(crossed, wcq[...]).astype(BF16)


def cross_forward(enc, wk, wv, qc, key, val, probs, out, stat):
    tokens, width = qc.shape
    length = enc.shape[0]
    scale = (width // HEADS) ** (-0.5)
    step = 256
    for first in range(0, width, step):
        cols = slice(first, first + step)
        key[:, cols] = nn(enc[...], wk[:, cols]).astype(BF16)
        val[:, cols] = nn(enc[...], wv[:, cols]).astype(BF16)
    lane = lax.broadcasted_iota(jnp.int32, (tokens, LANES), 1)
    tops = jnp.zeros((tokens, LANES), F32)
    sums = jnp.ones((tokens, LANES), F32)
    for pair in range(HEADS // 2):
        cols = slice(pair * LANES, (pair + 1) * LANES)
        scores = nt(stack_heads(qc[:, cols]), key[:, cols]) * scale
        top = jnp.max(scores, -1, keepdims=True)
        expo = jnp.exp(scores - top)
        total = jnp.sum(expo, -1, keepdims=True)
        low = expo.astype(BF16)
        probs[pair] = low
        mixed = nn(low, val[:, cols]) * (1.0 / total)
        out[:, cols] = merge_heads(mixed).astype(BF16)
        for half in range(2):
            part = slice(half * tokens, (half + 1) * tokens)
            here = lane == 2 * pair + half
            tops = jnp.where(here, top[part], tops)
            sums = jnp.where(here, total[part], sums)
    stat[:, :LANES] = tops
    stat[:, LANES:] = sums


def cross_combine(psg, out, stat, after, wo, g3, both, log_total, mixed_rows, after_rows,
                  r_out, r_stat, buf, send, recv):
    me, question = place()
    psg_barrier(psg)
    parts = [(out, r_out, True), (stat, r_stat, True)]
    psg_start(psg, parts, send, recv)
    r_out[me] = out[me]
    r_stat[me] = stat[me]
    psg_wait(psg, parts, send, recv)
    tops = [r_stat[p, :, :LANES] for p in range(psg)]
    top = functools.reduce(jnp.maximum, tops)
    shares = [jnp.exp(tops[p] - top) * r_stat[p, :, LANES:] for p in range(psg)]
    total = functools.reduce(jnp.add, shares)
    log_total[me] = top + jnp.log(total)
    inverse = 1.0 / total
    shares = [share * inverse for share in shares]
    width = out.shape[-1]
    for pair in range(HEADS // 2):
        cols = slice(pair * LANES, (pair + 1) * LANES)
        mixed = jnp.zeros(shares[0].shape, F32)
        for p in range(psg):
            mixed = mixed + spread_stat(shares[p], pair) * r_out[p, :, cols].astype(F32)
        mixed_rows[:, cols] = mixed
        both[me, :, width + pair * LANES : width + (pair + 1) * LANES] = mixed.astype(BF16)
    y = after[me] + nn(mixed_rows[...].astype(BF16), wo[...])
    after_rows[...] = y
    both[me, :, :width] = (y * rms_factor(y) * g3[...]).astype(BF16)
    buf[...] = both[me]
    parts = [(buf, both, False), (log_total.at[me], log_total, False)]
    psg_start(psg, parts, send.at[2:4], recv.at[2:4])
    psg_wait(psg, parts, send.at[2:4], recv.at[2:4])


def feed_forward(normed, cot, w_in, w_out, out, dnorm, grads):
    x = normed[...]
    top = cot[...]
    pre = nn(x, w_in[...])
    root = (2.0 / jnp.pi) ** 0.5
    square = pre * pre
    bend = jnp.tanh(root * (pre + 0.044715 * (square * pre)))
    act = (0.5 * pre * (1.0 + bend)).astype(BF16)
    slope = 0.5 * (1.0 + bend) + 0.5 * pre * (1.0 - bend * bend) * (root * (1.0 + 3 * 0.044715 * square))
    out[...] = nt(act, w_out[...]).astype(BF16)
    dpre = (nn(top, w_out[...]) * slope).astype(BF16)
    dnorm[...] = nt(dpre, w_in[...]).astype(BF16)
    batch, double, _ = grads.shape
    rows = double // 2
    width = x.shape[1]
    x_turned = x.T
    top_turned = top.T
    step = 256 if width % 256 == 0 else width
    g_in = nn(x_turned, dpre).astype(BF16)
    g_out = nn(top_turned, act).astype(BF16)
    for b in range(batch):
        grads[b, :rows] = g_in[b * rows : (b + 1) * rows]
        grads[b, rows:] = g_out[b * rows : (b + 1) * rows]


def hidden_combine(psg, out, dnorm, cot, after_rows, mixed_rows, wo, g3, wide, dots, grad_after, gain,
                   r_out, r_dnorm, buf, send, recv):
    me, question = place()
    psg_barrier(psg)
    parts = [(dnorm, r_dnorm, True), (out, r_out, True)]
    psg_start(psg, parts, send, recv)
    r_out[me] = out[me]
    r_dnorm[me] = dnorm[me]
    y = after_rows[...]
    factor = rms_factor(y)
    psg_wait(psg, parts, send, recv)
    width = y.shape[1]
    upstream = functools.reduce(jnp.add, [r_dnorm[p].astype(F32) for p in range(psg)])
    hidden = functools.reduce(jnp.add, [r_out[p].astype(F32) for p in range(psg)])
    scales = g3[...]
    gain[...] = jnp.sum(upstream * y * factor, 0, keepdims=True)
    grad = cot[me].astype(F32) + rms_back(y, factor, scales, upstream)
    grad_after[...] = grad
    dcross = grad.astype(BF16)
    dmixed = nt(dcross, wo[...]).astype(BF16)
    product = dmixed.astype(F32) * mixed_rows[...]
    lane = lax.broadcasted_iota(jnp.int32, (product.shape[0], LANES), 1)
    sums = jnp.zeros(lane.shape, F32)
    low = lane_is_low()
    for pair in range(HEADS // 2):
        here = product[:, pair * LANES : (pair + 1) * LANES]
        sums = jnp.where(lane == 2 * pair, jnp.sum(jnp.where(low, here, 0.0), -1, keepdims=True), sums)
        sums = jnp.where(lane == 2 * pair + 1, jnp.sum(jnp.where(low, 0.0, here), -1, keepdims=True), sums)
    dots[me] = sums
    buf[:, :width] = dmixed
    buf[:, width : 2 * width] = dcross
    buf[:, 2 * width :] = (y + hidden).astype(BF16)
    wide[me] = buf[...]
    parts = [(buf, wide, False), (dots.at[me], dots, False)]
    psg_start(psg, parts, send.at[2:4], recv.at[2:4])
    psg_wait(psg, parts, send.at[2:4], recv.at[2:4])


def cross_backward(enc, key, val, wk, wv, qc, dmixed, probs, stat, log_total, dots,
                   grad_enc, g_key, g_val, dquery, dkey_t, dval_t):
    tokens, width = qc.shape
    scale = (width // HEADS) ** (-0.5)
    ratio = jnp.exp(stat[:, :LANES] - log_total[...])
    dot_all = dots[...]
    for pair in range(HEADS // 2):
        cols = slice(pair * LANES, (pair + 1) * LANES)
        q2 = stack_heads(qc[:, cols])
        d2 = stack_heads(dmixed[:, cols])
        chances = probs[pair].astype(F32) * stack_stat(ratio, pair)
        dchance = nt(d2, val[:, cols])
        dscore = (chances * (dchance - stack_stat(dot_all, pair))).astype(BF16)
        dquery[:, cols] = (merge_heads(nn(dscore, key[:, cols])) * scale).astype(BF16)
        dkey_t[cols, :] = (nn(q2.T, dscore) * scale).astype(BF16)
        dval_t[cols, :] = nn(d2.T, chances.astype(BF16)).astype(BF16)
    dkey = dkey_t[...].T
    dval = dval_t[...].T
    step = 256
    enc_t = enc[...].T
    for first in range(0, width, step):
        cols = slice(first, first + step)
        grad_enc[:, cols] = nt(dkey, wk[cols, :]) + nt(dval, wv[cols, :])
    g_key[...] = nn(enc_t, dkey).astype(BF16)
    g_val[...] = nn(enc_t, dval).astype(BF16)


def query_combine(psg, dquery, after, grad_cross, wcq, g2, dq_all, grad_all, gain, r_dq, buf, buf32, send, recv):
    me, question = place()
    psg_barrier(psg)
    parts = [(dquery, r_dq, True)]
    psg_start(psg, parts, send, recv)
    r_dq[me] = dquery[me]
    y = after[me]
    factor = rms_factor(y)
    psg_wait(psg, parts, send, recv)
    total = functools.reduce(jnp.add, [r_dq[p].astype(F32) for p in range(psg)]).astype(BF16)
    upstream = nt(total, wcq[...])
    gain[...] = jnp.sum(upstream * y * factor, 0, keepdims=True)
    grad = grad_cross[...] + rms_back(y, factor, g2[...], upstream)
    buf[...] = total
    buf32[...] = grad
    dq_all[me] = total
    grad_all[me] = grad
    parts = [(buf, dq_all, False), (buf32, grad_all, False)]
    psg_start(psg, parts, send.at[1:3], recv.at[1:3])
    psg_wait(psg, parts, send.at[1:3], recv.at[1:3])


def self_backward(res, n1, q, k, v, probs, mix, n2, g1, wq, wk, wv, wo, grad_after, dq_cross, dcross, mixc,
                  grad_dec, gain, terms, turned, dq, dk, dv):
    me = lax.axis_index("psg")
    grad = grad_after[...]
    tokens, width = grad.shape
    scale = (width // HEADS) ** (-0.5)
    dself = grad.astype(BF16)
    dmixed = nt(dself, wo[...]).astype(BF16)
    for pair in range(HEADS // 2):
        cols = slice(pair * LANES, (pair + 1) * LANES)
        q2 = stack_heads(q[:, cols])
        d2 = stack_heads(dmixed[:, cols])
        chances = probs[pair]
        dchance = nt(d2, v[:, cols])
        dscore = chances * (dchance - jnp.sum(chances * dchance, -1, keepdims=True))
        low = dscore.astype(BF16)
        dq[:, cols] = (merge_heads(nn(low, k[:, cols])) * scale).astype(BF16)
        dk[:, cols] = (nn(low.T, q2) * scale).astype(BF16)
        dv[:, cols] = nn(chances.astype(BF16).T, d2).astype(BF16)
    upstream = nt(dq[...], wq[...]) + nt(dk[...], wk[...]) + nt(dv[...], wv[...])
    x = res[...]
    factor = rms_factor(x)
    grad = grad + rms_back(x, factor, g1[...], upstream)
    grad_dec[...] = grad
    share = tokens // lax.axis_size("psg")
    mine = lax.broadcasted_iota(jnp.int32, (tokens, 1), 0) // share == me
    gain[0:1] = jnp.sum(jnp.where(mine, upstream * x * factor, 0.0), 0, keepdims=True)
    gain[1:2] = jnp.sum(jnp.where(mine, grad, 0.0), 0, keepdims=True)
    rows = terms.shape[1]
    own = pl.ds(pl.multiple_of(me * rows, 16), rows)
    for slot, (left, rights) in enumerate(
        ((n1, (dq, dk, dv)), (mix, (None,)), (n2, (dq_cross,)), (mixc, (dcross,)))
    ):
        turned[slot] = left[...].T
        part = turned[slot, own, :]
        base = (0, 3, 4, 5)[slot]
        for offset, right in enumerate(rights):
            terms[base + offset] = nn(part, dself if right is None else right[...]).astype(BF16)


def call(body, outs, args, scratch=(), limit=40, collective=None):
    params = {"vmem_limit_bytes": limit * MIB}
    if collective is not None:
        params.update(collective_id=collective, has_side_effects=True)
    name = (body.func if isinstance(body, functools.partial) else body).__name__
    return pl.pallas_call(
        body,
        out_shape=tuple(jax.ShapeDtypeStruct(shape, dtype) for shape, dtype in outs),
        in_specs=[VMEM] * len(args),
        out_specs=[VMEM] * len(outs),
        scratch_shapes=list(scratch),
        compiler_params=pltpu.CompilerParams(**params),
        name=name,
    )(*args)


def local(
    psg,
    batch,
    decoder_in,
    encoded,
    cotangent,
    task_ids,
    task_embed,
    gain_self,
    self_query,
    self_key,
    self_value,
    self_output,
    gain_cross,
    cross_query,
    cross_key,
    cross_value,
    cross_output,
    gain_hidden,
    hidden_in,
    hidden_out,
):
    _, tokens, width = decoder_in.shape
    length = encoded.shape[1]
    groups = task_embed.shape[0]
    owned = gain_self.shape[0]
    pairs = HEADS // 2
    decoder, encoder, top = decoder_in[0], encoded[0], cotangent[0]

    attn = jnp.concatenate(
        [self_query, self_key, self_value, self_output, cross_query, cross_output, cross_key, cross_value], 0
    )
    hidden = jnp.concatenate([hidden_in, hidden_out.T], 0)
    gains = jnp.stack([gain_self, gain_cross, gain_hidden])
    small = jnp.zeros((SMALL_ROWS, LANES), BF16)
    small = small.at[:groups, :owned].set(task_embed).at[groups : groups + 3, :owned].set(gains)
    attn, hidden, small = gather_all(attn, hidden, small, psg, batch)
    attn = jnp.moveaxis(attn.reshape(psg, batch, 8, owned, width), 2, 0).reshape(8, width, width)
    wq, wk, wv, wo, wcq, wco, wck, wcv = [attn[i] for i in range(8)]
    hidden = jnp.moveaxis(hidden.reshape(batch, 2, -1, hidden.shape[-1]), 1, 0).reshape(2, width, -1)
    w_in, w_out = hidden[0], hidden[1]
    table = jnp.moveaxis(small[:, :, :, :owned], 2, 0).reshape(SMALL_ROWS, width).astype(F32)
    row = lax.dynamic_slice_in_dim(table, task_ids[0], 1, 0)
    g1, g2, g3 = [table[groups + i : groups + i + 1] for i in range(3)]

    whole = (tokens, width)
    res, n1, q, k, v, probs, mix, after, n2, qc = call(
        self_forward,
        [(whole, F32)] + [(whole, BF16)] * 4 + [((pairs, 2 * tokens, tokens), F32), (whole, BF16), (whole, F32)]
        + [(whole, BF16)] * 2,
        [decoder, row, g1, wq, wk, wv, wo, g2, wcq],
    )
    key, val, cprobs, out, stat = call(
        cross_forward,
        [((length, width), BF16)] * 2 + [((pairs, 2 * tokens, length), BF16), (whole, BF16), ((tokens, 2 * LANES), F32)],
        [encoder, wck, wcv, qc],
    )
    share = tokens // psg
    rows = (psg, share, width)
    dma = pltpu.SemaphoreType.DMA
    both, log_total, mixed_rows, after_rows = call(
        functools.partial(cross_combine, psg),
        [((psg, share, 2 * width), BF16), ((psg, share, LANES), F32), ((share, width), F32), ((share, width), F32)],
        [out.reshape(rows), stat.reshape(psg, share, 2 * LANES), after.reshape(rows), wco, g3],
        [
            pltpu.VMEM(rows, BF16),
            pltpu.VMEM((psg, share, 2 * LANES), F32),
            pltpu.VMEM((share, 2 * width), BF16),
            dma((4, psg)),
            dma((4, psg)),
        ],
        collective=2,
    )
    both = both.reshape(tokens, 2 * width)
    n3, mixc = both[:, :width], both[:, width:]
    hid = w_in.shape[1]
    part, dnorm, hidden_grads = call(
        feed_forward,
        [(whole, BF16), (whole, BF16), ((batch, 2 * width // batch, hid), BF16)],
        [n3, top, w_in, w_out],
    )
    wide, dots, grad_rows, gain_three = call(
        functools.partial(hidden_combine, psg),
        [((psg, share, 3 * width), BF16), ((psg, share, LANES), F32), ((share, width), F32), ((1, width), F32)],
        [part.reshape(rows), dnorm.reshape(rows), top.reshape(rows), after_rows, mixed_rows, wco, g3],
        [
            pltpu.VMEM(rows, BF16),
            pltpu.VMEM(rows, BF16),
            pltpu.VMEM((share, 3 * width), BF16),
            dma((4, psg)),
            dma((4, psg)),
        ],
        collective=3,
    )
    wide = wide.reshape(tokens, 3 * width)
    dmixed, dcross, block_out = [wide[:, i * width : (i + 1) * width] for i in range(3)]
    grad_encoded, g_key, g_val, dquery = call(
        cross_backward,
        [((length, width), F32)] + [((width, width), BF16)] * 2 + [(whole, BF16)],
        [encoder, key, val, wck, wcv, qc, dmixed, cprobs, stat, log_total.reshape(tokens, LANES), dots.reshape(tokens, LANES)],
        [pltpu.VMEM((width, length), BF16)] * 2,
    )
    dq_cross, grad_after, gain_two = call(
        functools.partial(query_combine, psg),
        [(rows, BF16), (rows, F32), ((1, width), F32)],
        [dquery.reshape(rows), after.reshape(rows), grad_rows, wcq, g2],
        [
            pltpu.VMEM(rows, BF16),
            pltpu.VMEM((share, width), BF16),
            pltpu.VMEM((share, width), F32),
            dma((3, psg)),
            dma((3, psg)),
        ],
        collective=4,
    )
    grad_decoder, sums, terms = call(
        self_backward,
        [(whole, F32), ((2, width), F32), ((6, width // psg, width), BF16)],
        [res, n1, q, k, v, probs, mix, n2, g1, wq, wk, wv, wo, grad_after.reshape(whole),
         dq_cross.reshape(whole), dcross, mixc],
        [pltpu.VMEM((4, width, tokens), BF16)] + [pltpu.VMEM(whole, BF16)] * 3,
    )

    kv = jnp.concatenate([g.reshape(psg, batch, owned, width) for g in (g_key, g_val)], 2)
    terms = jnp.moveaxis(terms.reshape(6, batch, owned, width), 0, 1).reshape(batch, 6 * owned, width)
    onehot = (task_ids[0] == jnp.arange(groups, dtype=jnp.int32)).astype(F32)
    sums = jnp.concatenate(
        [onehot[:, None] * sums[1:2], sums[0:1], gain_two, gain_three, jnp.zeros((8 - groups - 3, width), F32)], 0
    )
    kv, terms, hidden_grads, sums = reduce_all(kv, terms, hidden_grads, sums, psg, batch)
    first = (lax.axis_index("psg") * batch + lax.axis_index("batch")) * owned
    sums = lax.dynamic_slice_in_dim(sums, first, owned, 1)
    g_self = [terms[i * owned : (i + 1) * owned] for i in range(6)]
    cut = hidden_grads.shape[0] // 2
    return (
        block_out[None],
        grad_decoder[None],
        grad_encoded[None],
        sums[:groups],
        sums[groups],
        g_self[0],
        g_self[1],
        g_self[2],
        g_self[3],
        sums[groups + 1],
        g_self[4],
        kv[:owned],
        kv[owned:],
        g_self[5],
        sums[groups + 2],
        hidden_grads[:cut],
        hidden_grads[cut:].T,
    )


def solution(mesh):
    line, spread = P("batch", None, None), P("batch", "psg", None)
    flat, rows = P(("psg", "batch")), P(("psg", "batch"), None)
    table, wide, tall = P(None, ("psg", "batch")), P("batch", "psg"), P("psg", "batch")
    return jax.shard_map(
        functools.partial(local, mesh.shape["psg"], mesh.shape["batch"]),
        mesh=mesh,
        in_specs=(line, spread, line, P("batch"), table) + ((flat,) + (rows,) * 4) * 2 + (flat, wide, tall),
        out_specs=(line, line, spread, table) + ((flat,) + (rows,) * 4) * 2 + (flat, wide, tall),
        check_vma=False,
    )
```

time: 1950 us -> 299 us (0.15)
  waiting for transfers between devices: 1260 us -> 0 us
  matrix products: 298 us -> 0 us
  Pallas kernels: 0 us -> 233 us
  blocking collectives: 145 us -> 0 us
  local copies, waits for them, and re-layouts: 198 us -> 58.9 us
    reduce_scatter x9 -> x0, waiting for transfers between devices: 573 us -> none  [the longest x1 105 us: local(): lax.psum_scatter(term_cross_output, ('psg', 'batch'), scatter_dimension=0...]
    all_gather x14 -> x0, waiting for transfers between devices: 396 us -> none  [the longest x1 54.4 us: local(): lax.all_gather(cross_key, ('psg', 'batch'), axis=0, tiled=True)]
    dot_general x172 -> x0, matrix products: 297 us -> none  [the longest x60 84.6 us: block_scores(): jnp.einsum('bqhe,bkhe->bhqk', queries, key_block, preferred_element_type=...]
    unnamed x29 -> x0, waiting for transfers between devices: 287 us -> none
    pallas_call x0 -> x10, Pallas kernels: none -> 233 us  [the longest x1 89.1 us: reduce_all(): pl.pallas_call(functools.partial(reduce_kernel, spans), out_shape=tuple((...]
    another operation x8 -> x0, local copies, waits for them, and re-layouts: 86.9 us -> none  [the longest x6 76.4 us: key_blocks(): return jnp.moveaxis(shaped, 1, 0)]
    unnamed x2 -> x0, blocking collectives: 79.2 us -> none
    unnamed x114 -> x125, local copies, waits for them, and re-layouts: 100 us -> 28.8 us
  transfers between devices with their start and end apart: 26 -> 0, of which waited for: 18 -> 0; matrix products, arithmetic and copies ran while one was open for 22% -> 0% of each run, Pallas kernels for 0% -> 0%
where the time goes in v1:
time: 299 us; the launch traced here: 296 us
  Pallas kernels  233 us (78%)
  local copies, waits for them, and re-layouts  58.9 us (20%)
    pallas_call x1, Pallas kernels, reduce_all(): pl.pallas_call(functools.partial(reduce_kernel, spans), out_shape=tuple((...  89.1 us
    pallas_call x1, Pallas kernels, gather_all(): pl.pallas_call(functools.partial(gather_kernel, spans), out_shape=(jax.Sh...  80.7 us
    pallas_call x8, Pallas kernels, call(): pl.pallas_call(body, out_shape=tuple((jax.ShapeDtypeStruct(shape, dtype)...  63.6 us
    unnamed x125, local copies, waits for them, and re-layouts  28.8 us
    reshape x1, local copies, waits for them, and re-layouts, local(): attn.reshape(psg, batch, 8, owned, width)  8.52 us
    slice x1, local copies, waits for them, and re-layouts, local(): wq, wk, wv, wo, wcq, wco, wck, wcv = [attn[i] for i in range(8)]  6.35 us

profile of v1, /device:TPU:0, one launch (start us, length us, event | category | flops | bytes accessed | tf_op | source)
XLA Modules:
  0.0 296.3 jit_solution(1711095463886487368)
XLA Ops:
  6.9 1.8 pad_maximum_fusion.1.f_ref
  9.7 80.7 %gather_weights.1 = (bf16[4,8,192,768]{3,2,1,0:T(8,128)(2,1)}, bf16[8,192,768]{2,1,0:T(8,128)(2,1)}, bf16[4,8,16,128]{3,2,1,0:T(8,128)(2,1)}) custom-call(bf16[192,768]{1,0:T(8,128)(2,1)} %copy-done.52, bf16[192,768]{1,0:T(8,128)(2,1)} %pad_maximum_fusion.1.f_ref, bf16[16,128]{1,0:T(8,128)(2,1)} %copy-done.54), custom_call_target="tpu_custom_call" | custom-call | tf_op jit(solution)/shard_map/gather_weights/pallas_call | solution.py:254
  90.4 8.5 %copy.49 = bf16[4,8,8,24,768]{4,3,1,0,2:T(8,128)(2,1)} copy(bf16[4,8,8,24,768]{4,3,2,1,0:T(8,128)(2,1)} %bitcast.108) | data formatting | bytes 18874368 | tf_op jit(solution)/shard_map/reshape | solution.py:770
  98.9 6.4 %fusion = (bf16[1,4,8,24,768]{4,3,2,1,0:T(8,128)(2,1)}, bf16[1,4,8,24,768]{4,3,2,1,0:T(8,128)(2,1)}, bf16[1,4,8,24,768]{4,3,2,1,0:T(8,128)(2,1)S(1)}, bf16[1,4,8...) fusion(bf16[8,4,8,24,768]{4,3,2,1,0:T(8,128)(2,1)} %bitcast.107), kind=kLoop, calls=%fused_computation.28 | loop fusion | bytes 18874368 | tf_op jit(solution)/shard_map/slice | solution.py:771
  106.8 1.7 convert_element_type.18
  109.9 1.8 slice_reduce_fusion
  112.5 0.8 slice.177.g2
  113.3 1.3 copy-done
  114.6 1.3 copy-done.6
  115.9 0.9 copy-done.33
  116.8 2.2 self_forward.1
  119.8 1.0 copy-done.23
  123.5 5.6 %cross_forward.1 = (bf16[960,768]{1,0:T(8,128)(2,1)S(1)}, bf16[960,768]{1,0:T(8,128)(2,1)S(1)}, bf16[6,256,960]{2,1,0:T(8,128)(2,1)S(1)}, bf16[128,768]{1,0:T(8,128)(2,1)S(1)}, f32[128,256]{1,0:T(8,128)S(1)}) custom-call(bf16[960,768]{1,0:T(8,128)(2,1)S(1)} %bitcast.84, bf16[768,768]{1,0:T(8,128)(2,1)S(1)} %bitcast.77, bf16[768,768]{1,0:T(8,128)(2,1)S(1)} %bitcast.75, ...), custom_call_target="tpu_custom_call" | custom-call | tf_op jit(solution)/shard_map/cross_forward/pallas_call | solution.py:722
  129.2 1.6 copy-done.13
  130.8 1.1 copy-done.19
  132.0 1.1 copy-done.21
  135.2 1.3 copy-done.8
  136.5 1.0 copy-done.17
  137.5 0.9 copy-done.29
  138.4 0.9 copy-done.35
  139.3 12.1 %cross_combine.1 = (bf16[4,32,1536]{2,1,0:T(8,128)(2,1)S(1)}, f32[4,32,128]{2,1,0:T(8,128)S(1)}, f32[32,768]{1,0:T(8,128)S(1)}, f32[32,768]{1,0:T(8,128)S(1)}) custom-call(bf16[4,32,768]{2,1,0:T(8,128)(2,1)S(1)} %bitcast.102, f32[4,32,256]{2,1,0:T(8,128)S(1)} %bitcast.96, f32[4,32,768]{2,1,0:T(8,128)S(1)} %bitcast.89, bf16[768,768]{1,0:T(8,128)(2,1)S(1)} %bitcast.81, ...), custom_call_target="tpu_custom_call" | custom-call | tf_op jit(solution)/shard_map/cross_combine/pallas_call | solution.py:722
  152.4 1.9 feed_forward.1
  154.3 1.4 copy-done.15
  155.7 15.7 %hidden_combine.1 = (bf16[4,32,2304]{2,1,0:T(8,128)(2,1)S(1)}, f32[4,32,128]{2,1,0:T(8,128)S(1)}, f32[32,768]{1,0:T(8,128)S(1)}, f32[1,768]{1,0:T(1,128)S(1)}) custom-call(bf16[4,32,768]{2,1,0:T(8,128)(2,1)S(1)} %bitcast.100, bf16[4,32,768]{2,1,0:T(8,128)(2,1)S(1)} %bitcast.101, bf16[4,32,768]{2,1,0:T(8,128)(2,1)S(1)} %bitcast.94, ...), custom_call_target="tpu_custom_call" | custom-call | tf_op jit(solution)/shard_map/hidden_combine/pallas_call | solution.py:722
  172.3 7.9 %cross_backward.1 = (f32[960,768]{1,0:T(8,128)}, bf16[768,768]{1,0:T(8,128)(2,1)S(1)}, bf16[768,768]{1,0:T(8,128)(2,1)S(1)}, bf16[128,768]{1,0:T(8,128)(2,1)S(1)}) custom-call(bf16[960,768]{1,0:T(8,128)(2,1)S(1)} %bitcast.85, bf16[960,768]{1,0:T(8,128)(2,1)S(1)} %copy-done.20, bf16[960,768]{1,0:T(8,128)(2,1)S(1)} %copy-done.22, ...), custom_call_target="tpu_custom_call" | custom-call | tf_op jit(solution)/shard_map/cross_backward/pallas_call | solution.py:722
  180.3 13.6 %query_combine.1 = (bf16[4,32,768]{2,1,0:T(8,128)(2,1)S(1)}, f32[4,32,768]{2,1,0:T(8,128)S(1)}, f32[1,768]{1,0:T(1,128)S(1)}) custom-call(bf16[4,32,768]{2,1,0:T(8,128)(2,1)S(1)} %bitcast.103, f32[4,32,768]{2,1,0:T(8,128)S(1)} %bitcast.90, f32[32,768]{1,0:T(8,128)S(1)} %get-tuple-element.111.grad_cross, bf16[768,768]{1,0:T(8,128)(2,1)S(1)} %bitcast.80, ...), custom_call_target="tpu_custom_call" | custom-call | tf_op jit(solution)/shard_map/query_combine/pallas_call | solution.py:722
  194.0 4.6 %self_backward.1 = (f32[128,768]{1,0:T(8,128)}, f32[2,768]{1,0:T(2,128)S(1)}, bf16[6,192,768]{2,1,0:T(8,128)(2,1)S(1)}) custom-call(f32[128,768]{1,0:T(8,128)S(1)} %copy-done.32, bf16[128,768]{1,0:T(8,128)(2,1)S(1)} %copy-done.37, bf16[128,768]{1,0:T(8,128)(2,1)S(1)} %copy-done.39, bf16[128,768]{1,0:T(8,128)(2,1)S(1)} %copy-done.41, ...), custom_call_target="tpu_custom_call" | custom-call | tf_op jit(solution)/shard_map/self_backward/pallas_call | solution.py:722
  198.8 1.3 copy.44
  200.9 1.5 copy-done.10
  203.1 89.1 %reduce_grads.1 = (f32[48,768]{1,0:T(8,128)S(1)}, f32[144,768]{1,0:T(8,128)S(1)}, f32[192,768]{1,0:T(8,128)S(1)}, f32[8,768]{1,0:T(8,128)S(1)}) custom-call(bf16[2,2,8,48,768]{4,3,2,1,0:T(8,128)(2,1)S(1)} %copy_bitcast_fusion.1.kv_ref, bf16[8,144,768]{2,1,0:T(8,128)(2,1)S(1)} %bitcast.83, bf16[8,192,768]{2,1,0:T(8,128)(2,1)} %copy-done.15, ...), custom_call_target="tpu_custom_call" | custom-call | tf_op jit(solution)/shard_map/reduce_grads/pallas_call | solution.py:455
  294.7 0.8 fusion.3
  295.5 0.8 slice_bitcast_fusion
  (134 shorter events, 21.6 us)
Async XLA Ops:
  0.7 8.1 %copy-start.55 = (bf16[3,24]{1,0:T(4,128)(2,1)S(1)}, bf16[3,24]{1,0:T(4,128)(2,1)}, u32[]{:S(2)}) copy-start(bf16[3,24]{1,0:T(4,128)(2,1)} %param.26) | copy-start | bytes 436
  0.7 8.1 %copy-start.56 = (bf16[24]{0:T(256)(128)(2,1)S(1)}, bf16[24]{0:T(256)(128)(2,1)}, u32[]{:S(2)}) copy-start(bf16[24]{0:T(256)(128)(2,1)} %param.37) | copy-start | bytes 148
  0.7 8.1 %copy-start.57 = (bf16[24]{0:T(256)(128)(2,1)S(1)}, bf16[24]{0:T(256)(128)(2,1)}, u32[]{:S(2)}) copy-start(bf16[24]{0:T(256)(128)(2,1)} %param.32) | copy-start | bytes 148
  0.7 8.1 %copy-start.58 = (bf16[24]{0:T(256)(128)(2,1)S(1)}, bf16[24]{0:T(256)(128)(2,1)}, u32[]{:S(2)}) copy-start(bf16[24]{0:T(256)(128)(2,1)} %param.27) | copy-start | bytes 148
  98.9 6.4 %copy-start.53 = (bf16[4,8,16,128]{3,2,1,0:T(8,128)(2,1)S(1)}, bf16[4,8,16,128]{3,2,1,0:T(8,128)(2,1)}, u32[]{:S(2)}) copy-start(bf16[4,8,16,128]{3,2,1,0:T(8,128)(2,1)} %get-tuple-element.85) | copy-start | bytes 393220
  116.8 6.7 %copy-start.2 = (bf16[1,4,8,24,768]{4,3,2,1,0:T(8,128)(2,1)S(1)}, bf16[1,4,8,24,768]{4,3,2,1,0:T(8,128)(2,1)}, u32[]{:S(2)}) copy-start(bf16[1,4,8,24,768]{4,3,2,1,0:T(8,128)(2,1)} %get-tuple-element.136) | copy-start | bytes 3538948
  116.8 6.7 %copy-start.4 = (bf16[1,4,8,24,768]{4,3,2,1,0:T(8,128)(2,1)S(1)}, bf16[1,4,8,24,768]{4,3,2,1,0:T(8,128)(2,1)}, u32[]{:S(2)}) copy-start(bf16[1,4,8,24,768]{4,3,2,1,0:T(8,128)(2,1)} %get-tuple-element.137) | copy-start | bytes 3538948
  116.8 6.7 %copy-start.11 = (bf16[1,960,768]{2,1,0:T(8,128)(2,1)S(1)}, bf16[1,960,768]{2,1,0:T(8,128)(2,1)}, u32[]{:S(2)}) copy-start(bf16[1,960,768]{2,1,0:T(8,128)(2,1)} %param.23) | copy-start | bytes 4423684
  123.5 5.7 %copy-start.25 = (bf16[128,768]{1,0:T(8,128)(2,1)}, bf16[128,768]{1,0:T(8,128)(2,1)S(1)}, u32[]{:S(2)}) copy-start(bf16[128,768]{1,0:T(8,128)(2,1)S(1)} %get-tuple-element.86.qc) | copy-start | bytes 589828
  123.5 5.7 %copy-start.31 = (f32[128,768]{1,0:T(8,128)}, f32[128,768]{1,0:T(8,128)S(1)}, u32[]{:S(2)}) copy-start(f32[128,768]{1,0:T(8,128)S(1)} %get-tuple-element.97.res) | copy-start | bytes 1179652
  123.5 5.7 %copy-start.36 = (bf16[128,768]{1,0:T(8,128)(2,1)}, bf16[128,768]{1,0:T(8,128)(2,1)S(1)}, u32[]{:S(2)}) copy-start(bf16[128,768]{1,0:T(8,128)(2,1)S(1)} %get-tuple-element.98.n1) | copy-start | bytes 589828
  123.5 5.7 %copy-start.38 = (bf16[128,768]{1,0:T(8,128)(2,1)}, bf16[128,768]{1,0:T(8,128)(2,1)S(1)}, u32[]{:S(2)}) copy-start(bf16[128,768]{1,0:T(8,128)(2,1)S(1)} %get-tuple-element.99.q) | copy-start | bytes 589828
  139.3 12.1 %copy-start.50 = (bf16[8,192,768]{2,1,0:T(8,128)(2,1)S(1)}, bf16[8,192,768]{2,1,0:T(8,128)(2,1)}, u32[]{:S(2)}) copy-start(bf16[8,192,768]{2,1,0:T(8,128)(2,1)} %get-tuple-element.91) | copy-start | bytes 7077892
  151.5 20.7 %copy-start.22 = (bf16[960,768]{1,0:T(8,128)(2,1)S(1)}, bf16[960,768]{1,0:T(8,128)(2,1)}, u32[]{:S(2)}) copy-start(bf16[960,768]{1,0:T(8,128)(2,1)} %copy-done.21) | copy-start | bytes 4423684
  151.7 20.5 %copy-start.14 = (bf16[6,256,960]{2,1,0:T(8,128)(2,1)S(1)}, bf16[6,256,960]{2,1,0:T(8,128)(2,1)}, u32[]{:S(2)}) copy-start(bf16[6,256,960]{2,1,0:T(8,128)(2,1)} %copy-done.13) | copy-start | bytes 8847364
  151.7 20.5 %copy-start.20 = (bf16[960,768]{1,0:T(8,128)(2,1)S(1)}, bf16[960,768]{1,0:T(8,128)(2,1)}, u32[]{:S(2)}) copy-start(bf16[960,768]{1,0:T(8,128)(2,1)} %copy-done.19) | copy-start | bytes 4423684
  152.4 19.8 %copy-start.12 = (bf16[1,960,768]{2,1,0:T(8,128)(2,1)S(1)}, bf16[1,960,768]{2,1,0:T(8,128)(2,1)}, u32[]{:S(2)}) copy-start(bf16[1,960,768]{2,1,0:T(8,128)(2,1)} %param.23) | copy-start | bytes 4423684
  155.7 16.5 %copy-start.3 = (bf16[1,4,8,24,768]{4,3,2,1,0:T(8,128)(2,1)S(1)}, bf16[1,4,8,24,768]{4,3,2,1,0:T(8,128)(2,1)}, u32[]{:S(2)}) copy-start(bf16[1,4,8,24,768]{4,3,2,1,0:T(8,128)(2,1)} %get-tuple-element.136) | copy-start | bytes 3538948
  155.7 16.5 %copy-start.5 = (bf16[1,4,8,24,768]{4,3,2,1,0:T(8,128)(2,1)S(1)}, bf16[1,4,8,24,768]{4,3,2,1,0:T(8,128)(2,1)}, u32[]{:S(2)}) copy-start(bf16[1,4,8,24,768]{4,3,2,1,0:T(8,128)(2,1)} %get-tuple-element.137) | copy-start | bytes 3538948
  155.7 16.5 %copy-start.26 = (bf16[128,768]{1,0:T(8,128)(2,1)S(1)}, bf16[128,768]{1,0:T(8,128)(2,1)}, u32[]{:S(2)}) copy-start(bf16[128,768]{1,0:T(8,128)(2,1)} %copy-done.25) | copy-start | bytes 589828
  155.7 16.5 %copy-start.30 = (f32[128,256]{1,0:T(8,128)S(1)}, f32[128,256]{1,0:T(8,128)}, u32[]{:S(2)}) copy-start(f32[128,256]{1,0:T(8,128)} %copy-done.28) | copy-start | bytes 393220
  172.3 8.1 %copy-start.7 = (bf16[1,4,8,24,768]{4,3,2,1,0:T(8,128)(2,1)S(1)}, bf16[1,4,8,24,768]{4,3,2,1,0:T(8,128)(2,1)}, u32[]{:S(2)}) copy-start(bf16[1,4,8,24,768]{4,3,2,1,0:T(8,128)(2,1)} %get-tuple-element.131) | copy-start | bytes 3538948
  172.3 8.1 %copy-start.18 = (f32[128,768]{1,0:T(8,128)S(1)}, f32[128,768]{1,0:T(8,128)}, u32[]{:S(2)}) copy-start(f32[128,768]{1,0:T(8,128)} %copy-done.16) | copy-start | bytes 1179652
  172.3 21.7 %copy-start.24 = (f32[6,256,128]{2,1,0:T(8,128)S(1)}, f32[6,256,128]{2,1,0:T(8,128)}, u32[]{:S(2)}) copy-start(f32[6,256,128]{2,1,0:T(8,128)} %copy-done.23) | copy-start | bytes 2359300
  172.3 21.7 %copy-start.39 = (bf16[128,768]{1,0:T(8,128)(2,1)S(1)}, bf16[128,768]{1,0:T(8,128)(2,1)}, u32[]{:S(2)}) copy-start(bf16[128,768]{1,0:T(8,128)(2,1)} %copy-done.38) | copy-start | bytes 589828
  172.3 21.7 %copy-start.41 = (bf16[128,768]{1,0:T(8,128)(2,1)S(1)}, bf16[128,768]{1,0:T(8,128)(2,1)}, u32[]{:S(2)}) copy-start(bf16[128,768]{1,0:T(8,128)(2,1)} %copy-done.40) | copy-start | bytes 589828
  172.3 21.7 %copy-start.43 = (bf16[128,768]{1,0:T(8,128)(2,1)S(1)}, bf16[128,768]{1,0:T(8,128)(2,1)}, u32[]{:S(2)}) copy-start(bf16[128,768]{1,0:T(8,128)(2,1)} %copy-done.42) | copy-start | bytes 589828
  172.3 21.7 %copy-start.45 = (bf16[128,768]{1,0:T(8,128)(2,1)S(1)}, bf16[128,768]{1,0:T(8,128)(2,1)}, u32[]{:S(2)}) copy-start(bf16[128,768]{1,0:T(8,128)(2,1)} %copy-done.44) | copy-start | bytes 589828
  172.3 21.7 %copy-start.47 = (bf16[128,768]{1,0:T(8,128)(2,1)S(1)}, bf16[128,768]{1,0:T(8,128)(2,1)}, u32[]{:S(2)}) copy-start(bf16[128,768]{1,0:T(8,128)(2,1)} %copy-done.46) | copy-start | bytes 589828
  180.3 13.7 %copy-start.1 = (bf16[1,4,8,24,768]{4,3,2,1,0:T(8,128)(2,1)S(1)}, bf16[1,4,8,24,768]{4,3,2,1,0:T(8,128)(2,1)}, u32[]{:S(2)}) copy-start(bf16[1,4,8,24,768]{4,3,2,1,0:T(8,128)(2,1)} %get-tuple-element.135) | copy-start | bytes 3538948
  180.3 13.7 %copy-start.32 = (f32[128,768]{1,0:T(8,128)S(1)}, f32[128,768]{1,0:T(8,128)}, u32[]{:S(2)}) copy-start(f32[128,768]{1,0:T(8,128)} %copy-done.31) | copy-start | bytes 1179652
  180.3 13.7 %copy-start.37 = (bf16[128,768]{1,0:T(8,128)(2,1)S(1)}, bf16[128,768]{1,0:T(8,128)(2,1)}, u32[]{:S(2)}) copy-start(bf16[128,768]{1,0:T(8,128)(2,1)} %copy-done.36) | copy-start | bytes 589828
  (27 other events, 29.2 us)

commit v2 on v0

--- a/solution.py
+++ b/solution.py
@@ -1,14 +1,997 @@
+import functools
+import types
+
 import jax
 import jax.numpy as jnp
 from jax import lax
+from jax.experimental import pallas as pl
+from jax.experimental.pallas import tpu as pltpu
 from jax.sharding import PartitionSpec as P
 
 HEADS = 12
 PASS_LEN = 192
-
-
 EPSILON = 1e-06
 MASKED = -1000000000.0
+LANES = 128
+MAX_BLOCKS = 32
+MIB = 2**20
+
+F32 = jnp.float32
+BF16 = jnp.bfloat16
+ID = pl.DeviceIdType.MESH
+
+CK, CV, CO, CQ, SO, SQ, SK, SV = range(8)
+GATHER = ((CK, 2, False), (SO, 4, False), (CO, 2, True))
+REDUCE = ((CO, 1), (CQ, 2), (SQ, 3), (CK, 2))
+
+
+def nn(former, latter):
+    return jnp.dot(former, latter, preferred_element_type=F32)
+
+
+def nt(former, latter):
+    return lax.dot_general(former, latter, (((1,), (1,)), ((), ())), preferred_element_type=F32)
+
+
+def rms_factor(values):
+    return lax.rsqrt(jnp.mean(values * values, -1, keepdims=True) + EPSILON)
+
+
+def norm_back(values, factor, scales, grad_out):
+    scaled = grad_out * scales
+    cubed = factor * factor * factor
+    return factor * scaled - values * cubed * jnp.mean(scaled * values, -1, keepdims=True)
+
+
+def lane_is_low():
+    return lax.broadcasted_iota(jnp.int32, (1, LANES), 1) < LANES // 2
+
+
+def stack_heads(pair):
+    low = lane_is_low()
+    zero = jnp.zeros_like(pair)
+    return jnp.concatenate([jnp.where(low, pair, zero), jnp.where(low, zero, pair)], 0)
+
+
+def merge_heads(stacked):
+    half = stacked.shape[0] // 2
+    return jnp.where(lane_is_low(), stacked[:half], stacked[half:])
+
+
+def stack_stat(stats, pair):
+    return jnp.concatenate([stats[:, 2 * pair : 2 * pair + 1], stats[:, 2 * pair + 1 : 2 * pair + 2]], 0)
+
+
+def spread_stat(stats, pair):
+    return jnp.where(
+        lane_is_low(), stats[:, 2 * pair : 2 * pair + 1], stats[:, 2 * pair + 1 : 2 * pair + 2]
+    )
+
+
+def column_tiles(width, size=256):
+    return [slice(first, min(first + size, width)) for first in range(0, width, size)]
+
+
+def pair_lanes(pair):
+    return slice(pair * LANES, (pair + 1) * LANES)
+
+
+def self_forward(dec, row, g1, wq, wk, wv, wo, g2, res, n1, q, k, v, probs, mix, after, n2):
+    x = dec + row
+    res[...] = x
+    normed = (x * rms_factor(x) * g1).astype(BF16)
+    n1[...] = normed
+    q[...] = nn(normed, wq).astype(BF16)
+    k[...] = nn(normed, wk).astype(BF16)
+    v[...] = nn(normed, wv).astype(BF16)
+    tokens, width = x.shape
+    scale = (width // HEADS) ** (-0.5)
+    rows = lax.broadcasted_iota(jnp.int32, (2 * tokens, tokens), 0) % tokens
+    causal = rows >= lax.broadcasted_iota(jnp.int32, (2 * tokens, tokens), 1)
+    for pair in range(HEADS // 2):
+        cols = pair_lanes(pair)
+        scores = jnp.where(causal, nt(stack_heads(q[:, cols]), k[:, cols]) * scale, MASKED)
+        expo = jnp.exp(scores - jnp.max(scores, -1, keepdims=True))
+        chances = expo * (1.0 / jnp.sum(expo, -1, keepdims=True))
+        probs[pair] = chances
+        mix[:, cols] = merge_heads(nn(chances.astype(BF16), v[:, cols])).astype(BF16)
+    y = x + nn(mix[...], wo)
+    after[...] = y
+    n2[...] = (y * rms_factor(y) * g2).astype(BF16)
+
+
+def cross_attend(qc, key, val, probs, stat, part):
+    tokens, width = qc.shape
+    share = tokens // 4
+    scale = (width // HEADS) ** (-0.5)
+    lane = lax.broadcasted_iota(jnp.int32, (tokens, LANES), 1)
+    tops = jnp.zeros((tokens, LANES), F32)
+    sums = jnp.ones((tokens, LANES), F32)
+    for pair in range(HEADS // 2):
+        cols = pair_lanes(pair)
+        scores = nt(stack_heads(qc[:, cols]), key[:, cols]) * scale
+        top = jnp.max(scores, -1, keepdims=True)
+        expo = jnp.exp(scores - top)
+        total = jnp.sum(expo, -1, keepdims=True)
+        low = expo.astype(BF16)
+        probs[pair] = low
+        mixed = merge_heads(nn(low, val[:, cols]) * (1.0 / total)).astype(BF16)
+        for p in range(4):
+            part[p // 2, p % 2, :, cols] = mixed[p * share : (p + 1) * share]
+        for half in range(2):
+            rows = slice(half * tokens, (half + 1) * tokens)
+            here = lane == 2 * pair + half
+            tops = jnp.where(here, top[rows], tops)
+            sums = jnp.where(here, total[rows], sums)
+    for p in range(4):
+        rows = slice(p * share, (p + 1) * share)
+        stat[p // 2, p % 2, :, :LANES] = tops[rows]
+        stat[p // 2, p % 2, :, LANES:] = sums[rows]
+
+
+def join_parts(o_a, s_a, o_b, s_b, out, stat):
+    top_a, top_b = s_a[:, :LANES], s_b[:, :LANES]
+    top = jnp.maximum(top_a, top_b)
+    w_a = jnp.exp(top_a - top) * s_a[:, LANES:]
+    w_b = jnp.exp(top_b - top) * s_b[:, LANES:]
+    total = w_a + w_b
+    inverse = 1.0 / total
+    w_a, w_b = w_a * inverse, w_b * inverse
+    for pair in range(HEADS // 2):
+        cols = pair_lanes(pair)
+        mixed = spread_stat(w_a, pair) * o_a[:, cols].astype(F32) + spread_stat(w_b, pair) * o_b[:, cols].astype(F32)
+        out[:, cols] = mixed.astype(out.dtype)
+    stat[:, :LANES] = top
+    stat[:, LANES:] = total
+
+
+def feed_forward(x, top, w_in, w_out):
+    pre = nn(x, w_in)
+    root = (2.0 / jnp.pi) ** 0.5
+    square = pre * pre
+    bend = jnp.tanh(root * (pre + 0.044715 * (square * pre)))
+    act = (0.5 * pre * (1.0 + bend)).astype(BF16)
+    slope = 0.5 * (1.0 + bend) + 0.5 * pre * (1.0 - bend * bend) * (root * (1.0 + 3 * 0.044715 * square))
+    dpre = (nn(top, w_out) * slope).astype(BF16)
+    return act, dpre
+
+
+def head_sums(product):
+    lane = lax.broadcasted_iota(jnp.int32, (product.shape[0], LANES), 1)
+    sums = jnp.zeros(lane.shape, F32)
+    low = lane_is_low()
+    for pair in range(HEADS // 2):
+        here = product[:, pair_lanes(pair)]
+        sums = jnp.where(lane == 2 * pair, jnp.sum(jnp.where(low, here, 0.0), -1, keepdims=True), sums)
+        sums = jnp.where(lane == 2 * pair + 1, jnp.sum(jnp.where(low, 0.0, here), -1, keepdims=True), sums)
+    return sums
+
+
+def cross_backward(pair, qc, dmixed, key, val, probs, ratio, dots, part):
+    tokens, width = qc.shape
+    share = tokens // 4
+    scale = (width // HEADS) ** (-0.5)
+    cols = pair_lanes(pair)
+    q2 = stack_heads(qc[:, cols])
+    d2 = stack_heads(dmixed[:, cols])
+    chances = probs[pair].astype(F32) * stack_stat(ratio, pair)
+    dchance = nt(d2, val[:, cols])
+    dscore = (chances * (dchance - stack_stat(dots, pair))).astype(BF16)
+    dquery = (merge_heads(nn(dscore, key[:, cols])) * scale).astype(BF16)
+    for p in range(4):
+        part[p // 2, p % 2, :, cols] = dquery[p * share : (p + 1) * share]
+    probs[pair, :LANES] = (nn(q2.T, dscore) * scale).astype(BF16)
+    probs[pair, LANES:] = nn(d2.T, chances.astype(BF16)).astype(BF16)
+
+
+def self_backward(dmixed, q, k, v, probs, dq, dk, dv):
+    width = q.shape[1]
+    scale = (width // HEADS) ** (-0.5)
+    for pair in range(HEADS // 2):
+        cols = pair_lanes(pair)
+        q2 = stack_heads(q[:, cols])
+        d2 = stack_heads(dmixed[:, cols])
+        chances = probs[pair]
+        dchance = nt(d2, v[:, cols])
+        dscore = chances * (dchance - jnp.sum(chances * dchance, -1, keepdims=True))
+        low = dscore.astype(BF16)
+        dq[:, cols] = (merge_heads(nn(low, k[:, cols])) * scale).astype(BF16)
+        dk[:, cols] = (nn(low.T, q2) * scale).astype(BF16)
+        dv[:, cols] = nn(chances.astype(BF16).T, d2).astype(BF16)
+
+
+INPUTS = ["tid", "dec", "cot", "enc", "table", "g_one", "g_two", "g_three", "sq", "sk", "sv", "so", "cq", "co", "ck", "cv", "h_in", "h_out"]
+OUTPUTS = ["block_out", "grad_dec", "grad_enc", "g_attn", "g_in", "g_out", "g_vec"]
+
+
+def buffers(psg, batch, tokens, length, width, owned, hidden):
+    spans, pairs, share, half = batch // 2, HEADS // 2, tokens // psg, width // 2
+    dma = pltpu.SemaphoreType.DMA
+    whole = (tokens, width)
+    quad = (2, 2, share)
+    band = 2 * owned
+    runs = len(GATHER)
+
+    def low(*shape):
+        return pltpu.VMEM(shape, BF16)
+
+    def full(*shape):
+        return pltpu.VMEM(shape, F32)
+
+    out = dict(
+        w=low(8, 2, 2 * batch * owned, width),
+        f=low(2, width, hidden // 2),
+        m_send=low(4, band, half),
+        m_recv=low(4, band, half),
+        v_buf=full(4, 8, width),
+        v_recv=full(3 + spans, 8, width),
+        cots=low(2, tokens, width),
+        key=low(length, width),
+        val=low(length, width),
+        c_probs=low(pairs, 2 * tokens, length),
+        s_probs=full(pairs, 2 * tokens, tokens),
+        res=full(*whole),
+        after=full(*whole),
+        n1=low(*whole),
+        n2=low(*whole),
+        q=low(*whole),
+        k=low(*whole),
+        v=low(*whole),
+        mix=low(*whole),
+        qc=low(*whole),
+        o_part=low(*quad, width),
+        o_stat=full(*quad, 2 * LANES),
+        o_core=low(2, share, width),
+        o_core_stat=full(2, share, 2 * LANES),
+        o_to=low(share, width),
+        o_to_stat=full(share, 2 * LANES),
+        o_mid=full(share, width),
+        o_mid_stat=full(share, 2 * LANES),
+        o_x=low(share, width),
+        o_x_stat=full(share, 2 * LANES),
+        mixed_rows=full(share, width),
+        stat_rows=full(share, 2 * LANES),
+        after_rows=full(share, width),
+        n3=low(2, *quad, width),
+        mixc=low(*quad, width),
+        log_total=full(*quad, LANES),
+        dn=low(2, *quad, width),
+        dn_core=low(2, 2, share, width),
+        dn_to=low(3, share, width),
+        dn_got=low(3, share, width),
+        hp=low(2, *quad, width),
+        hp_core=low(2, 2, share, width),
+        hp_to=low(3, share, width),
+        hp_got=low(3, share, width),
+        grad_rows=full(share, width),
+        dmixed=low(*quad, width),
+        dcross=low(*quad, width),
+        dots=full(*quad, LANES),
+        dq_part=low(*quad, width),
+        dq_core=low(2, share, width),
+        dq_to=low(share, width),
+        dq_x=low(share, width),
+        dqc=low(*quad, width),
+        dself=low(*quad, width),
+        dself_rest=low(*quad, width),
+        dq=low(*whole),
+        dk=low(*whole),
+        dv=low(*whole),
+        turned=low(4, width, tokens),
+        gf=low(2, width, hidden // 2),
+        gkv=low(2, 2, 2 * batch * owned, width),
+        kv_core=low(2, 2, batch * owned, width),
+        kv_to=low(2, batch * owned, width),
+        kv_x=low(2, batch * owned, width),
+        g=low(8, batch * owned, width),
+        gains=full(8, width),
+        t_buf=full(4, 8, width),
+        t_recv=full(3 + spans, 8, width),
+        f_swap=low(2, width // batch, hidden // 2),
+        f_swapped=low(2, width // batch, hidden // 2),
+        f_came=low(spans, 2, width // spans, hidden // 2),
+        f_sum=full(2, width // spans, hidden // 2),
+        r_sum=full(max(count for _, count in REDUCE), band, half),
+        one_send=dma((96,)),
+        one_recv=dma((96,)),
+        a_recv=dma((runs, psg * batch)),
+        a_up=dma((runs, spans)),
+        a_down=dma((runs, spans)),
+        a_y=dma((runs, spans)),
+        a_x=dma((runs, batch)),
+        a_c=dma((runs, 2 * batch)),
+        w_recv=dma((spans,)),
+        w_up=dma((spans,)),
+        w_down=dma((spans,)),
+        v_sems=dma((2, spans)),
+        t_sems=dma((2, spans)),
+        f_line=dma((2, spans)),
+    )
+    for number, (_, count) in enumerate(REDUCE):
+        out[f"r{number}_y"] = low(spans, count, band, half)
+        out[f"r{number}_came"] = low(spans, count, band, half)
+        out[f"r{number}_swap"] = low(count, owned, half)
+        out[f"r{number}_swapped"] = low(count, owned, half)
+        out[f"r{number}_sems"] = dma((4, spans))
+    return out
+
+
+def block_kernel(names, psg, batch, *refs):
+    r = types.SimpleNamespace(**dict(zip(names, refs, strict=True)))
+    spans = batch // 2
+    index, question = lax.axis_index("psg"), lax.axis_index("batch")
+    far, near = question // 2, question % 2
+    side, core = index // 2, index % 2
+    x_peer = ((1 - side) * 2 + core, question)
+    c_peer = (side * 2 + 1 - core, question)
+    y_peer = (index, far * 2 + 1 - near)
+    d_peer = ((1 - side) * 2 + core, far * 2 + 1 - near)
+    column = [(index, lax.rem(far + hop, spans) * 2 + near) for hop in range(1, spans)]
+    tokens, width = r.dec.shape
+    owned = r.sq.shape[0]
+    band, quarter, half = 2 * owned, batch * owned, width // 2
+    share = tokens // psg
+    fan = width // batch
+    shards = (r.ck, r.cv, r.co, r.cq, r.so, r.sq, r.sk, r.sv)
+    pairs = HEADS // 2
+
+    def aligned(value, to):
+        return value if isinstance(value, int) else pl.multiple_of(value, to)
+
+    def span(start, size, to):
+        return pl.ds(aligned(start, to), size)
+
+    def lanes(h):
+        return span(h * half, half, LANES)
+
+    sent = []
+
+    def go(copy, when=None):
+        if when is None:
+            copy.start()
+        else:
+            pl.when(when)(copy.start)
+        sent.append((copy, when))
+
+    def remote(src, dst, send, recv, device):
+        return pltpu.make_async_remote_copy(
+            src_ref=src, dst_ref=dst, send_sem=send, recv_sem=recv, device_id=device, device_id_type=ID
+        )
+
+    numbers = iter(range(96))
+
+    def pair(src, dst, device):
+        number = next(numbers)
+        copy = remote(src, dst, r.one_send.at[number], r.one_recv.at[number], device)
+        go(copy)
+        return copy
+
+    barrier = pltpu.get_barrier_semaphore()
+    greeted = column + [y_peer, x_peer, c_peer, d_peer]
+    for other in greeted:
+        pl.semaphore_signal(barrier, inc=1, device_id=other, device_id_type=ID)
+    pl.semaphore_wait(barrier, len(greeted))
+
+    def pack(number):
+        first, second = shards[2 * number], shards[2 * number + 1]
+        both = jnp.concatenate([first[:, lanes(1 - near)].astype(F32), second[:, lanes(1 - near)].astype(F32)], 0)
+        r.m_send[number] = both.astype(BF16)
+
+    def exchange(first, count):
+        for number in range(first, first + count):
+            pack(number)
+        return pair(r.m_send.at[first : first + count], r.m_recv.at[first : first + count], y_peer)
+
+    row = core * quarter + far * band
+
+    def join(number):
+        other = r.m_recv[number].astype(F32)
+        for part in range(2):
+            mine = shards[2 * number + part][:, lanes(near)].astype(F32)
+            theirs = other[part * owned : (part + 1) * owned]
+            block = jnp.where(near == 0, jnp.concatenate([mine, theirs], 0), jnp.concatenate([theirs, mine], 0))
+            r.w[2 * number + part, side, span(row, band, 16), lanes(near)] = block.astype(BF16)
+
+    def unit(run, x, c, z, h):
+        first, count, joined = GATHER[run]
+        rows = span(c * quarter + z * band, band, 16)
+        return r.w.at[first : first + count, slice(None) if joined else x, rows, lanes(h)]
+
+    def landing(run, x, c, z, h):
+        place = 0 if GATHER[run][2] else x
+        return r.a_recv.at[run, (place * 2 + c) * batch + z * 2 + h]
+
+    def hand(run, x, c, z, h, sem, device, when=None):
+        spot = unit(run, x, c, z, h)
+        go(remote(spot, spot, sem, landing(run, x, c, z, h), device), when)
+
+    def landed(run, x, c, z, h, when=None):
+        spot = unit(run, x, c, z, h)
+        copy = remote(spot, spot, r.a_up.at[0, 0], landing(run, x, c, z, h), c_peer)
+        if when is None:
+            copy.wait_recv()
+        else:
+            pl.when(when)(copy.wait_recv)
+
+    def wide(run, z, h, when=None):
+        if not GATHER[run][2]:
+            hand(run, side, core, z, h, r.a_x.at[run, z * 2 + h], x_peer, when)
+        hand(run, side, core, z, h, r.a_c.at[run, z * 2 + h], c_peer, when)
+
+    def offer(run):
+        hand(run, side, core, far, near, r.a_up.at[run, far], (index, question + 2), far < spans - 1)
+        hand(run, side, core, far, near, r.a_down.at[run, far], (index, question - 2), far > 0)
+        hand(run, side, core, far, near, r.a_y.at[run, far], y_peer)
+        wide(run, far, near)
+
+    def inside(z):
+        return (z >= 0) & (z < spans)
+
+    def from_y(run, step):
+        for sign in (-1, 1) if 0 < step < spans else (1,) if step == 0 else ():
+            z = far + sign * step
+            valid = inside(z) if step else None
+            landed(run, side, core, z, 1 - near, valid)
+            wide(run, z, 1 - near, valid)
+
+    def from_line(run, step):
+        for sign in (-1, 1) if step < spans else ():
+            z = far + sign * step
+            valid = inside(z)
+            landed(run, side, core, z, near, valid)
+            if sign < 0:
+                hand(run, side, core, z, near, r.a_up.at[run, z], (index, question + 2), valid & (far < spans - 1))
+            else:
+                hand(run, side, core, z, near, r.a_down.at[run, z], (index, question - 2), valid & (far > 0))
+            hand(run, side, core, z, near, r.a_y.at[run, z], y_peer, valid)
+            wide(run, z, near, valid)
+
+    def from_x(run, step):
+        for sign in (-1, 1) if 0 < step < spans else (1,) if step == 0 else ():
+            z = far + sign * step
+            valid = inside(z) if step else None
+            for h in (near, 1 - near):
+                landed(run, 1 - side, core, z, h, valid)
+                hand(run, 1 - side, core, z, h, r.a_c.at[run, batch + z * 2 + h], c_peer, valid)
+
+    def complete(run):
+        for z in range(spans):
+            for h in range(2):
+                landed(run, side, 1 - core, z, h)
+                if not GATHER[run][2]:
+                    landed(run, 1 - side, 1 - core, z, h)
+
+    def matrix(number):
+        return r.w[number].reshape(width, width)
+
+    m_kv = exchange(0, 1)
+    m_self = exchange(2, 2)
+    m_tail = exchange(1, 1)
+
+    def ladder(buf, recv, sems):
+        def first():
+            return pair(buf.at[0], recv.at[0], c_peer)
+
+        def second(copy):
+            copy.wait_recv()
+            buf[1] = (buf[0].astype(F32) + recv[0].astype(F32)).astype(buf.dtype)
+            return pair(buf.at[1], recv.at[1], x_peer)
+
+        def third(copy):
+            copy.wait_recv()
+            buf[2] = (buf[1].astype(F32) + recv[1].astype(F32)).astype(buf.dtype)
+            return pair(buf.at[2], recv.at[2], y_peer)
+
+        def fourth(copy):
+            copy.wait_recv()
+            buf[3] = (buf[2].astype(F32) + recv[2].astype(F32)).astype(buf.dtype)
+            for hop in range(1, spans):
+                z = lax.rem(far + hop, spans)
+                go(remote(buf.at[3], recv.at[3 + far], sems.at[0, z], sems.at[1, far], (index, z * 2 + near)))
+
+        def last():
+            total = buf[3].astype(F32)
+            for hop in range(1, spans):
+                z = lax.rem(far + hop, spans)
+                remote(buf.at[3], recv.at[3 + z], sems.at[0, z], sems.at[1, z], c_peer).wait_recv()
+                total = total + recv[3 + z].astype(F32)
+            return total
+
+        return first, second, third, fourth, last
+
+    device = index * batch + question
+    place = jnp.where(
+        lax.broadcasted_iota(jnp.int32, (owned, width), 1)
+        == lax.broadcasted_iota(jnp.int32, (owned, width), 0) + device * owned,
+        1.0,
+        0.0,
+    ).astype(BF16)
+    r.v_buf[0, 0:3] = nn(r.table[...], place)
+    for number, gain in enumerate((r.g_one, r.g_two, r.g_three)):
+        r.v_buf[0, 3 + number : 4 + number] = nn(gain[...], place)
+    r.v_buf[0, 6:8] = jnp.zeros((2, width), F32)
+    v_first, v_second, v_third, v_fourth, v_last = ladder(r.v_buf, r.v_recv, r.v_sems)
+    v_copy = v_first()
+
+    m_kv.wait_recv()
+    join(0)
+    offer(0)
+    m_self.wait_recv()
+    join(2)
+    join(3)
+    offer(1)
+    m_tail.wait_recv()
+    join(1)
+    own_tail = r.w.at[CO : CO + 2, side, span(row, band, 16), lanes(near)]
+    x_tail = pair(own_tail, own_tail, x_peer)
+    v_copy = v_second(v_copy)
+
+    cut = r.f.shape[2]
+    other_cols = span((1 - near) * cut, cut, LANES)
+    own_cols = span(near * cut, cut, LANES)
+    own_fan = span(question * fan, fan, 16)
+    h_copies = [
+        pair(r.h_in.at[:, other_cols], r.f.at[0, own_fan], y_peer),
+        pair(r.h_out.at[:, other_cols], r.f.at[1, own_fan], y_peer),
+    ]
+    r.f[0, own_fan] = r.h_in[:, own_cols]
+    r.f[1, own_fan] = r.h_out[:, own_cols]
+    r.cots[near] = r.cot[...]
+
+    def f_unit(z):
+        return r.f.at[:, span(z * 2 * fan, 2 * fan, 16), :]
+
+    def f_hand(z, sem, device, when):
+        go(remote(f_unit(z), f_unit(z), sem, r.w_recv.at[z], device), when)
+
+    def f_landed(step):
+        for sign in (-1, 1) if step < spans else ():
+            z = far + sign * step
+            pl.when(inside(z))(remote(f_unit(z), f_unit(z), r.w_up.at[0], r.w_recv.at[z], c_peer).wait_recv)
+            if sign < 0:
+                f_hand(z, r.w_up.at[z], (index, question + 2), inside(z) & (far < spans - 1))
+            else:
+                f_hand(z, r.w_down.at[z], (index, question - 2), inside(z) & (far > 0))
+
+    from_y(0, 0)
+    from_y(1, 0)
+    from_line(0, 1)
+    from_line(1, 1)
+    x_tail.wait_recv()
+    offer(2)
+    from_y(0, 1)
+    from_y(1, 1)
+    v_copy = v_third(v_copy)
+    from_x(0, 0)
+    from_x(1, 0)
+    from_line(0, 2)
+    from_line(1, 2)
+    from_y(2, 0)
+    from_line(2, 1)
+    for copy in h_copies:
+        copy.wait_recv()
+    f_hand(far, r.w_up.at[far], (index, question + 2), far < spans - 1)
+    f_hand(far, r.w_down.at[far], (index, question - 2), far > 0)
+    from_y(0, 2)
+    from_y(1, 2)
+    from_x(0, 1)
+    v_fourth(v_copy)
+    from_line(0, 3)
+    from_line(1, 3)
+    from_line(2, 2)
+    from_y(2, 1)
+    from_x(1, 1)
+    from_y(0, 3)
+    from_y(1, 3)
+    from_x(0, 2)
+    from_line(2, 3)
+    from_y(2, 2)
+    f_landed(1)
+    cot_copy = pair(r.cot, r.cots.at[near], y_peer)
+    from_x(1, 2)
+    from_x(0, 3)
+    from_y(2, 3)
+    complete(0)
+    vectors = v_last()
+    for cols in column_tiles(width):
+        r.key[:, cols] = nn(r.enc[...], r.w[CK, :, :, cols].reshape(width, -1)).astype(BF16)
+        r.val[:, cols] = nn(r.enc[...], r.w[CV, :, :, cols].reshape(width, -1)).astype(BF16)
+    f_landed(2)
+    from_x(1, 3)
+    complete(1)
+
+    gains = [vectors[3 + i : 4 + i] for i in range(3)]
+    chosen = r.tid[0]
+    row_embed = functools.reduce(
+        jnp.add, [vectors[i : i + 1] * jnp.where(chosen == i, 1.0, 0.0).astype(F32) for i in range(3)]
+    )
+    r.gains[0:3] = vectors[3:6]
+    self_forward(
+        r.dec[...].astype(F32), row_embed, gains[0], matrix(SQ), matrix(SK), matrix(SV), matrix(SO), gains[1],
+        r.res, r.n1, r.q, r.k, r.v, r.s_probs, r.mix, r.after, r.n2,
+    )
+    complete(2)
+    r.qc[...] = nn(r.n2[...], matrix(CQ)).astype(BF16)
+
+    cross_attend(r.qc, r.key, r.val, r.c_probs, r.o_stat, r.o_part)
+    first = [pair(r.o_part.at[:, 1 - core], r.o_core, c_peer), pair(r.o_stat.at[:, 1 - core], r.o_core_stat, c_peer)]
+    for copy in first:
+        copy.wait_recv()
+    join_parts(
+        r.o_part[1 - side, core], r.o_stat[1 - side, core], r.o_core[1 - side], r.o_core_stat[1 - side],
+        r.o_to, r.o_to_stat,
+    )
+    second = [pair(r.o_to, r.o_x, x_peer), pair(r.o_to_stat, r.o_x_stat, x_peer)]
+    join_parts(
+        r.o_part[side, core], r.o_stat[side, core], r.o_core[side], r.o_core_stat[side], r.o_mid, r.o_mid_stat
+    )
+    for copy in second:
+        copy.wait_recv()
+    join_parts(r.o_mid[...], r.o_mid_stat[...], r.o_x[...], r.o_x_stat[...], r.mixed_rows, r.stat_rows)
+    my_rows = span(index * share, share, 16)
+    r.log_total[side, core] = r.stat_rows[:, :LANES] + jnp.log(r.stat_rows[:, LANES:])
+    mixed_low = r.mixed_rows[...].astype(BF16)
+    r.mixc[side, core] = mixed_low
+    y = r.after[my_rows, :] + nn(mixed_low, matrix(CO))
+    r.after_rows[...] = y
+    r.n3[near, side, core] = (y * rms_factor(y) * r.gains[2:3]).astype(BF16)
+
+    def block8(h, x, c):
+        return r.n3.at[h, x, c]
+
+    def spread4(buf):
+        spot = buf.at[side, core]
+        over_x, over_c = pair(spot, spot, x_peer), pair(spot, spot, c_peer)
+
+        def then():
+            over_x.wait_recv()
+            onward = buf.at[1 - side, core]
+            last = pair(onward, onward, c_peer)
+
+            def end():
+                over_c.wait_recv()
+                last.wait_recv()
+
+            return end
+
+        return then
+
+    mine = block8(near, side, core)
+    to_y, to_x, to_d, to_c = [pair(mine, mine, peer) for peer in (y_peer, x_peer, d_peer, c_peer)]
+    log_then = spread4(r.log_total)
+    mixc_then = spread4(r.mixc)
+    onward = [to_c]
+    for copy, h, x in ((to_y, 1 - near, side), (to_x, near, 1 - side), (to_d, 1 - near, 1 - side)):
+        copy.wait_recv()
+        onward.append(pair(block8(h, x, core), block8(h, x, core), c_peer))
+    log_end = log_then()
+    f_landed(3)
+    cot_copy.wait_recv()
+    for copy in onward:
+        copy.wait_recv()
+
+    x = r.n3[...].reshape(2 * tokens, width)
+    top = r.cots[...].reshape(2 * tokens, width)
+    act, dpre = feed_forward(x, top, r.f[0], r.f[1])
+    r.dn[...] = nt(dpre, r.f[0]).astype(BF16).reshape(r.dn.shape)
+
+    def shrink8(part, got_c, to, got):
+        over_c = pair(part.at[:, :, 1 - core], got_c, c_peer)
+
+        def second():
+            over_c.wait_recv()
+
+            def total(h, x):
+                return part[h, x, core].astype(F32) + got_c[h, x].astype(F32)
+
+            copies = []
+            for slot, (h, x, peer) in enumerate(
+                ((1 - near, 1 - side, d_peer), (near, 1 - side, x_peer), (1 - near, side, y_peer))
+            ):
+                to[slot] = total(h, x).astype(BF16)
+                copies.append(pair(to.at[slot], got.at[slot], peer))
+
+            def last():
+                out = total(near, side)
+                for slot, copy in enumerate(copies):
+                    copy.wait_recv()
+                    out = out + got[slot].astype(F32)
+                return out
+
+            return last
+
+        return second
+
+    dn_second = shrink8(r.dn, r.dn_core, r.dn_to, r.dn_got)
+    r.hp[...] = nt(act, r.f[1]).astype(BF16).reshape(r.hp.shape)
+    dn_last = dn_second()
+    hp_second = shrink8(r.hp, r.hp_core, r.hp_to, r.hp_got)
+    r.gf[0] = nn(x.T, dpre).astype(BF16)
+    r.gf[1] = nn(top.T, act).astype(BF16)
+
+    others = [lax.rem(far + hop, spans) for hop in range(1, spans)]
+
+    def line_kit(came, src, sems):
+        def copy(z, slot):
+            return remote(src(z), came.at[slot], sems.at[0, z], sems.at[1, slot], (index, z * 2 + near))
+
+        def send(z):
+            go(copy(z, far))
+
+        def total(value, out):
+            out[...] = value
+            for z in others:
+                copy(far, z).wait_recv()
+                out[...] = out[...] + came[z].astype(F32)
+
+        return send, total
+
+    def f_piece(z):
+        return r.gf.at[:, span(z * 2 * fan, 2 * fan, 16), :]
+
+    f_send, f_total = line_kit(r.f_came, f_piece, r.f_line)
+    for z in others:
+        f_send(z)
+
+    upstream = dn_last()
+    y = r.after_rows[...]
+    factor = rms_factor(y)
+    scales = r.gains[2:3]
+    gain_three = jnp.sum(upstream * y * factor, 0, keepdims=True)
+    grad = r.cot[my_rows, :].astype(F32) + norm_back(y, factor, scales, upstream)
+    r.grad_rows[...] = grad
+    low = grad.astype(BF16)
+    r.dcross[side, core] = low
+    dmixed = nt(low, matrix(CO)).astype(BF16)
+    r.dmixed[side, core] = dmixed
+    dmixed_then = spread4(r.dmixed)
+    r.dots[side, core] = head_sums(dmixed.astype(F32) * r.mixed_rows[...])
+    dots_then = spread4(r.dots)
+    dcross_then = spread4(r.dcross)
+    mixc_end = mixc_then()
+    hp_last = hp_second()
+    dmixed_end = dmixed_then()
+    dots_end = dots_then()
+    dcross_end = dcross_then()
+    for end in (log_end, mixc_end, dmixed_end, dots_end, dcross_end):
+        end()
+
+    def rows_of(ref):
+        return ref[...].reshape(tokens, ref.shape[-1])
+
+    def reduce_kit(number):
+        first, count = REDUCE[number]
+        got_y, sems = getattr(r, f"r{number}_y"), getattr(r, f"r{number}_sems")
+
+        def piece(z, h):
+            return r.g.at[first : first + count, span(z * band, band, 16), lanes(h)]
+
+        def y_copy(z):
+            return remote(piece(z, 1 - near), got_y.at[z], sems.at[0, z], sems.at[1, z], y_peer)
+
+        send, total = line_kit(getattr(r, f"r{number}_came"), lambda z: got_y.at[z], sems.at[2:4])
+
+        def begin():
+            for z in others + [far]:
+                go(y_copy(z))
+
+        def value(z):
+            y_copy(z).wait_recv()
+            mine = r.g[first : first + count, span(z * band, band, 16), lanes(near)]
+            return mine.astype(F32) + got_y[z].astype(F32)
+
+        def forward():
+            for z in others:
+                got_y[z] = value(z).astype(BF16)
+                send(z)
+
+        swap, swapped = getattr(r, f"r{number}_swap"), getattr(r, f"r{number}_swapped")
+        out = r.g_attn.at[first : first + count]
+
+        def finish():
+            sums = r.r_sum.at[:count]
+
+            total(value(far), sums)
+            both = sums[...]
+            upper, lower = both[:, :owned], both[:, owned:]
+            swap[...] = jnp.where(near == 0, lower, upper).astype(BF16)
+            copy = pair(swap, swapped, y_peer)
+            out[:, :, lanes(near)] = jnp.where(near == 0, upper, lower)
+
+            def end():
+                copy.wait_recv()
+                out[:, :, lanes(1 - near)] = swapped[...].astype(F32)
+
+            return end
+
+        return begin, forward, finish
+
+    own_rows = span(index * quarter, quarter, 16)
+
+    def turn(slot, value):
+        r.turned[slot] = value.T
+        return r.turned[slot, own_rows, :]
+
+    co_begin, co_forward, co_finish = reduce_kit(0)
+    so_begin, so_forward, so_finish = reduce_kit(1)
+    late_begin, late_forward, late_finish = reduce_kit(2)
+    kv_begin, kv_forward, kv_finish = reduce_kit(3)
+    r.g[CO] = nn(turn(0, rows_of(r.mixc)), rows_of(r.dcross)).astype(BF16)
+    co_begin()
+
+    ratio = jnp.exp(rows_of(r.o_stat)[:, :LANES] - rows_of(r.log_total))
+    dots = rows_of(r.dots)
+    dmixed = rows_of(r.dmixed)
+    for number in range(pairs):
+        cross_backward(
+            number, r.qc, dmixed, r.key, r.val, r.c_probs, ratio, dots, r.dq_part
+        )
+    q_first = pair(r.dq_part.at[:, 1 - core], r.dq_core, c_peer)
+    r.key[...] = r.c_probs[:, :LANES].reshape(width, -1).T
+    q_first.wait_recv()
+    r.dq_to[...] = (r.dq_part[1 - side, core].astype(F32) + r.dq_core[1 - side].astype(F32)).astype(BF16)
+    q_second = pair(r.dq_to, r.dq_x, x_peer)
+    r.c_probs[:, :LANES] = r.enc[...].T.reshape(pairs, LANES, -1)
+    for cols in column_tiles(width):
+        r.gkv[0, :, :, cols] = nn(r.c_probs[:, :LANES].reshape(width, -1), r.key[:, cols]).astype(BF16).reshape(2, 2 * quarter, -1)
+    q_second.wait_recv()
+    dq_rows = (
+        r.dq_part[side, core].astype(F32) + r.dq_core[side].astype(F32) + r.dq_x[...].astype(F32)
+    ).astype(BF16)
+    r.dqc[side, core] = dq_rows
+    upstream = nt(dq_rows, matrix(CQ))
+    y = r.after[my_rows, :]
+    factor = rms_factor(y)
+    gain_two = jnp.sum(upstream * y * factor, 0, keepdims=True)
+    grad = r.grad_rows[...] + norm_back(y, factor, r.gains[1:2], upstream)
+    low = grad.astype(BF16)
+    r.dself[side, core] = low
+    dself_then = spread4(r.dself)
+    r.dself_rest[side, core] = (grad - low.astype(F32)).astype(BF16)
+    rest_then = spread4(r.dself_rest)
+    dqc_then = spread4(r.dqc)
+    r.val[...] = r.c_probs[:, LANES:].reshape(width, -1).T
+    for cols in column_tiles(width):
+        r.gkv[1, :, :, cols] = nn(r.c_probs[:, :LANES].reshape(width, -1), r.val[:, cols]).astype(BF16).reshape(2, 2 * quarter, -1)
+    kv_first = pair(r.gkv.at[:, :, span((1 - core) * quarter, quarter, 16), :], r.kv_core, c_peer)
+    dself_end = dself_then()
+    dqc_end = dqc_then()
+    rest_end = rest_then()
+    co_forward()
+    kv_first.wait_recv()
+    kv_own = span(core * quarter, quarter, 16)
+    r.kv_to[...] = (
+        r.gkv[:, 1 - side, kv_own, :].astype(F32) + r.kv_core[:, 1 - side].astype(F32)
+    ).astype(BF16)
+    kv_second = pair(r.kv_to, r.kv_x, x_peer)
+    dself_end()
+    dqc_end()
+
+    dself = rows_of(r.dself)
+    r.g[SO] = nn(turn(1, r.mix[...]), dself).astype(BF16)
+    r.g[CQ] = nn(turn(2, r.n2[...]), rows_of(r.dqc)).astype(BF16)
+    so_begin()
+    dmixed = nt(dself, matrix(SO)).astype(BF16)
+    self_backward(dmixed, r.q, r.k, r.v, r.s_probs, r.dq, r.dk, r.dv)
+    normed = turn(3, r.n1[...])
+    for number, ref in ((SQ, r.dq), (SK, r.dk), (SV, r.dv)):
+        r.g[number] = nn(normed, ref[...]).astype(BF16)
+    late_begin()
+    rest_end()
+    upstream = nt(r.dq[...], matrix(SQ)) + nt(r.dk[...], matrix(SK)) + nt(r.dv[...], matrix(SV))
+    x = r.res[...]
+    factor = rms_factor(x)
+    grad = dself.astype(F32) + rows_of(r.dself_rest).astype(F32) + norm_back(x, factor, r.gains[0:1], upstream)
+    r.grad_dec[...] = grad
+    mine = lax.broadcasted_iota(jnp.int32, (tokens, 1), 0) // share == index
+    task = jnp.sum(jnp.where(mine, grad, 0.0), 0, keepdims=True)
+    r.t_buf[0, 0:3] = jnp.concatenate([task * jnp.where(chosen == i, 1.0, 0.0).astype(F32) for i in range(3)], 0)
+    r.t_buf[0, 3:4] = jnp.sum(jnp.where(mine, upstream * x * factor, 0.0), 0, keepdims=True)
+    r.t_buf[0, 4:5] = gain_two
+    r.t_buf[0, 5:6] = gain_three
+    r.t_buf[0, 6:8] = jnp.zeros((2, width), F32)
+    t_first, t_second, t_third, t_fourth, t_last = ladder(r.t_buf, r.t_recv, r.t_sems)
+    t_copy = t_first()
+    hidden = hp_last()
+    r.block_out[side, core] = (r.after_rows[...] + hidden).astype(BF16)
+    out_then = spread4(r.block_out)
+    so_forward()
+    t_copy = t_second(t_copy)
+    for cols in column_tiles(width):
+        r.grad_enc[:, cols] = nt(r.key[...], matrix(CK)[cols]) + nt(r.val[...], matrix(CV)[cols])
+    late_forward()
+    kv_second.wait_recv()
+    r.g[CK : CK + 2] = (
+        r.gkv[:, side, kv_own, :].astype(F32) + r.kv_core[:, side].astype(F32) + r.kv_x[...].astype(F32)
+    ).astype(BF16)
+    kv_begin()
+    t_copy = t_third(t_copy)
+    out_end = out_then()
+
+    f_total(f_piece(far)[...].astype(F32), r.f_sum)
+    both = r.f_sum[...]
+    upper, lower = both[:, :fan], both[:, fan:]
+    r.f_swap[...] = jnp.where(near == 0, lower, upper).astype(BF16)
+    f_copy = pair(r.f_swap, r.f_swapped, y_peer)
+    kept = jnp.where(near == 0, upper, lower)
+    r.g_in[:, own_cols] = kept[0]
+    r.g_out[:, own_cols] = kept[1]
+    co_end = co_finish()
+    so_end = so_finish()
+    t_fourth(t_copy)
+    kv_forward()
+    late_end = late_finish()
+    f_copy.wait_recv()
+    r.g_in[:, other_cols] = r.f_swapped[0].astype(F32)
+    r.g_out[:, other_cols] = r.f_swapped[1].astype(F32)
+    kv_end = kv_finish()
+    r.g_vec[...] = t_last()
+    out_end()
+    co_end()
+    so_end()
+    late_end()
+    kv_end()
+    for copy, when in sent:
+        if when is None:
+            copy.wait_send()
+        else:
+            pl.when(when)(copy.wait_send)
+
+
+def regular(owned, psg, batch, tokens, width):
+    return psg == 4 and batch in (4, 6, 8) and owned % 8 == 0 and tokens % 128 == 0 and (width // 2) % LANES == 0
+
+
+def fused(psg, batch, decoder_in, encoded, cotangent, task_ids, task_embed, gain_self, self_query, self_key, self_value,
+          self_output, gain_cross, cross_query, cross_key, cross_value, cross_output, gain_hidden, hidden_in, hidden_out):
+    _, tokens, width = decoder_in.shape
+    length = encoded.shape[1]
+    groups, owned = task_embed.shape
+    hidden = hidden_in.shape[1]
+    scratch = buffers(psg, batch, tokens, length, width, owned, hidden)
+    names = INPUTS + OUTPUTS + list(scratch)
+    vmem = pl.BlockSpec(memory_space=pltpu.VMEM)
+    quad = (2, 2, tokens // psg, width)
+    block_out, grad_decoder, grad_encoded, g_attn, g_in, g_out, g_vec = pl.pallas_call(
+        functools.partial(block_kernel, names, psg, batch),
+        out_shape=(
+            jax.ShapeDtypeStruct(quad, BF16),
+            jax.ShapeDtypeStruct((tokens, width), F32),
+            jax.ShapeDtypeStruct((length, width), F32),
+            jax.ShapeDtypeStruct((8, owned, width), F32),
+            jax.ShapeDtypeStruct((width // batch, hidden), F32),
+            jax.ShapeDtypeStruct((width // batch, hidden), F32),
+            jax.ShapeDtypeStruct((8, width), F32),
+        ),
+        in_specs=[pl.BlockSpec(memory_space=pltpu.SMEM)] + [vmem] * (len(INPUTS) - 1),
+        out_specs=[vmem] * len(OUTPUTS),
+        scratch_shapes=list(scratch.values()),
+        compiler_params=pltpu.CompilerParams(collective_id=0, has_side_effects=True, vmem_limit_bytes=56 * MIB),
+        name="decoder_block",
+    )(task_ids, decoder_in[0], cotangent[0], encoded[0], task_embed, gain_self[None],
+      gain_cross[None], gain_hidden[None], self_query, self_key, self_value, self_output,
+      cross_query, cross_output, cross_key, cross_value, hidden_in, hidden_out.T)
+    first = (lax.axis_index("psg") * batch + lax.axis_index("batch")) * owned
+    mine = lax.dynamic_slice_in_dim(g_vec, first, owned, 1)
+    return (
+        block_out.reshape(decoder_in.shape),
+        grad_decoder[None],
+        grad_encoded[None],
+        mine[:groups],
+        mine[groups],
+        g_attn[SQ],
+        g_attn[SK],
+        g_attn[SV],
+        g_attn[SO],
+        mine[groups + 1],
+        g_attn[CQ],
+        g_attn[CK],
+        g_attn[CV],
+        g_attn[CO],
+        mine[groups + 2],
+        g_in,
+        g_out.T,
+    )
 
 
 def rms_norm(values, scales):
@@ -151,7 +1134,7 @@
     return (query_grad, (key_grad, value_grad))
 
 
-def local(
+def general(
     decoder_in,
     encoded,
     cotangent,
@@ -402,48 +1385,21 @@
     )
 
 
+def local(psg, batch, *arrays):
+    decoder_in, gain = arrays[0], arrays[5]
+    if regular(gain.shape[0], psg, batch, decoder_in.shape[1], decoder_in.shape[2]) and decoder_in.shape[0] == 1:
+        return fused(psg, batch, *arrays)
+    return general(*arrays)
+
+
 def solution(mesh):
+    line, spread = P("batch", None, None), P("batch", "psg", None)
+    flat, rows = P(("psg", "batch")), P(("psg", "batch"), None)
+    table, wide, tall = P(None, ("psg", "batch")), P("batch", "psg"), P("psg", "batch")
     return jax.shard_map(
-        local,
+        functools.partial(local, mesh.shape["psg"], mesh.shape["batch"]),
         mesh=mesh,
-        in_specs=(
-            P("batch", None, None),
-            P("batch", "psg", None),
-            P("batch", None, None),
-            P("batch"),
-            P(None, ("psg", "batch")),
-            P(("psg", "batch")),
-            P(("psg", "batch"), None),
-            P(("psg", "batch"), None),
-            P(("psg", "batch"), None),
-            P(("psg", "batch"), None),
-            P(("psg", "batch")),
-            P(("psg", "batch"), None),
-            P(("psg", "batch"), None),
-            P(("psg", "batch"), None),
-            P(("psg", "batch"), None),
-            P(("psg", "batch")),
-            P("batch", "psg"),
-            P("psg", "batch"),
-        ),
-        out_specs=(
-            P("batch", None, None),
-            P("batch", None, None),
-            P("batch", "psg", None),
-            P(None, ("psg", "batch")),
-            P(("psg", "batch")),
-            P(("psg", "batch"), None),
-            P(("psg", "batch"), None),
-            P(("psg", "batch"), None),
-            P(("psg", "batch"), None),
-            P(("psg", "batch")),
-            P(("psg", "batch"), None),
-            P(("psg", "batch"), None),
-            P(("psg", "batch"), None),
-            P(("psg", "batch"), None),
-            P(("psg", "batch")),
-            P("batch", "psg"),
-            P("psg", "batch"),
-        ),
+        in_specs=(line, spread, line, P("batch"), table) + ((flat,) + (rows,) * 4) * 2 + (flat, wide, tall),
+        out_specs=(line, line, spread, table) + ((flat,) + (rows,) * 4) * 2 + (flat, wide, tall),
         check_vma=False,
     )

time: 1950 us -> 156 us (0.08)
  waiting for transfers between devices: 1260 us -> 0 us
  matrix products: 298 us -> 0 us
  local copies, waits for them, and re-layouts: 198 us -> 12.3 us
  blocking collectives: 145 us -> 0 us
  Pallas kernels: 0 us -> 142 us
  other arithmetic: 21.2 us -> 0 us
    reduce_scatter x9 -> x0, waiting for transfers between devices: 573 us -> none  [the longest x1 105 us: local(): lax.psum_scatter(term_cross_output, ('psg', 'batch'), scatter_dimension=0...]
    all_gather x14 -> x0, waiting for transfers between devices: 396 us -> none  [the longest x1 54.4 us: local(): lax.all_gather(cross_key, ('psg', 'batch'), axis=0, tiled=True)]
    dot_general x172 -> x0, matrix products: 297 us -> none  [the longest x60 84.6 us: block_scores(): jnp.einsum('bqhe,bkhe->bhqk', queries, key_block, preferred_element_type=...]
    unnamed x29 -> x0, waiting for transfers between devices: 287 us -> none
    pallas_call x0 -> x1, Pallas kernels: none -> 142 us  [fused(): pl.pallas_call(functools.partial(block_kernel, names, psg, batch), out_sh...]
    unnamed x114 -> x9, local copies, waits for them, and re-layouts: 100 us -> 8.5 us
    another operation x8 -> x0, local copies, waits for them, and re-layouts: 86.9 us -> none  [the longest x6 76.4 us: key_blocks(): return jnp.moveaxis(shaped, 1, 0)]
    unnamed x2 -> x0, blocking collectives: 79.2 us -> none
  transfers between devices with their start and end apart: 26 -> 0, of which waited for: 18 -> 0; matrix products, arithmetic and copies ran while one was open for 22% -> 0% of each run, Pallas kernels for 0% -> 0%
where the time goes in v2:
time: 156 us
  Pallas kernels  142 us (91%)
  local copies, waits for them, and re-layouts  12.3 us (8%)
    pallas_call x1, Pallas kernels, fused(): pl.pallas_call(functools.partial(block_kernel, names, psg, batch), out_sh...  142 us
    unnamed x9, local copies, waits for them, and re-layouts  8.5 us

profile of v2, /device:TPU:0, one launch (start us, length us, event | category | flops | bytes accessed | tf_op | source)
XLA Modules:
  0.0 155.5 jit_solution(7608728914221305657)
XLA Ops:
  1.3 141.9 %decoder_block.1 = (bf16[2,2,32,768]{3,2,1,0:T(8,128)(2,1)}, f32[128,768]{1,0:T(8,128)}, f32[960,768]{1,0:T(8,128)}, f32[8,24,768]{2,1,0:T(8,128)}, f32[96,768]{...) custom-call(s32[1]{0:T(128)S(6)} %copy.40.refs_0_, bf16[128,768]{1,0:T(8,128)(2,1)} %bitcast.38, ...), custom_call_target="tpu_custom_call" | custom-call | tf_op jit(solution)/shard_map/decoder_block/pallas_call | solution.py:955
  143.2 0.8 constant_dynamic-slice_fusion
  144.0 0.5 slice_bitcast_fusion.8
  144.5 0.6 slice.36
  145.1 1.9 %slice_bitcast_fusion = (f32[24,768]{1,0:T(8,128)}, f32[24,768]{1,0:T(8,128)}, f32[24,768]{1,0:T(8,128)}, f32[24,768]{1,0:T(8,128)}, f32[24,768]{1,0:T(8,128)}, ...) fusion(f32[8,24,768]{2,1,0:T(8,128)} %get-tuple-element.28), kind=kLoop, calls=%fused_computation | loop fusion | bytes 1179648 | tf_op jit(solution)/shard_map/squeeze | solution.py:990
  147.0 1.6 %copy.41 = bf16[1,128,768]{2,1,0:T(8,128)(2,1)} copy(bf16[1,128,768]{2,1,0:T(8,128)(2,1)} %bitcast.37) | data formatting | bytes 393216
  148.6 1.8 %copy.42 = f32[1,128,768]{2,1,0:T(8,128)} copy(f32[1,128,768]{2,1,0:T(8,128)} %bitcast.35) | data formatting | bytes 786432
  150.4 0.0 copy-start.1
  150.4 0.0 copy-start
  150.4 3.7 %copy.43 = f32[1,960,768]{2,1,0:T(8,128)} copy(f32[1,960,768]{2,1,0:T(8,128)} %bitcast.33) | data formatting | bytes 5898240
  154.1 0.0 copy-done.1
  154.1 0.7 copy.44
  154.8 0.0 copy-done
  154.8 0.7 copy.45
Async XLA Ops:
  150.4 3.7 %copy-start.1 = (f32[96,768]{1,0:T(8,128)S(1)}, f32[96,768]{1,0:T(8,128)}, u32[]{:S(2)}) copy-start(f32[96,768]{1,0:T(8,128)} %get-tuple-element.74) | copy-start | bytes 884740
  150.4 4.4 %copy-start = (f32[96,768]{1,0:T(8,128)S(1)}, f32[96,768]{1,0:T(8,128)}, u32[]{:S(2)}) copy-start(f32[96,768]{1,0:T(8,128)} %get-tuple-element.30) | copy-start | bytes 884740

commit v3 on v2

--- a/solution.py
+++ b/solution.py
@@ -8,21 +8,22 @@
 from jax.experimental.pallas import tpu as pltpu
 from jax.sharding import PartitionSpec as P
 
+SPANS = 4
 HEADS = 12
 PASS_LEN = 192
 EPSILON = 1e-06
 MASKED = -1000000000.0
 LANES = 128
-MAX_BLOCKS = 32
 MIB = 2**20
+PAIRS = 100
 
 F32 = jnp.float32
 BF16 = jnp.bfloat16
 ID = pl.DeviceIdType.MESH
 
-CK, CV, CO, CQ, SO, SQ, SK, SV = range(8)
-GATHER = ((CK, 2, False), (SO, 4, False), (CO, 2, True))
-REDUCE = ((CO, 1), (CQ, 2), (SQ, 3), (CK, 2))
+CK, CV, CO, CQ, SO, SK, SQ, SV = range(8)
+GATHER = ((CK, 2, False), (SK, 3, False), (SO, 1, True), (CQ, 1, True), (CO, 1, False))
+REDUCE = ((CO, 1, True), (CQ, 2, True), (SK, 3, True), (CK, 1, False), (CV, 1, False))
 
 
 def nn(former, latter):
@@ -226,6 +227,17 @@
         v_buf=full(4, 8, width),
         v_recv=full(3 + spans, 8, width),
         cots=low(2, tokens, width),
+        dec_here=low(tokens, width),
+        enc_here=low(length, width),
+        block_here=low(*quad, width),
+        grad_dec_here=full(*whole),
+        grad_enc_here=full(length, width),
+        g_attn_here=full(8, owned, width),
+        g_in_here=full(width // batch, hidden),
+        g_out_here=full(width // batch, hidden),
+        g_vec_here=full(8, owned),
+        load=dma((3,)),
+        store=dma((16,)),
         key=low(length, width),
         val=low(length, width),
         c_probs=low(pairs, 2 * tokens, length),
@@ -264,9 +276,7 @@
         hp_to=low(3, share, width),
         hp_got=low(3, share, width),
         grad_rows=full(share, width),
-        dmixed=low(*quad, width),
         dcross=low(*quad, width),
-        dots=full(*quad, LANES),
         dq_part=low(*quad, width),
         dq_core=low(2, share, width),
         dq_to=low(share, width),
@@ -289,36 +299,37 @@
         t_recv=full(3 + spans, 8, width),
         f_swap=low(2, width // batch, hidden // 2),
         f_swapped=low(2, width // batch, hidden // 2),
-        f_came=low(spans, 2, width // spans, hidden // 2),
+        f_came=low(3, 2, width // spans, hidden // 2),
         f_sum=full(2, width // spans, hidden // 2),
-        r_sum=full(max(count for _, count in REDUCE), band, half),
-        one_send=dma((96,)),
-        one_recv=dma((96,)),
-        a_recv=dma((runs, psg * batch)),
-        a_up=dma((runs, spans)),
-        a_down=dma((runs, spans)),
-        a_y=dma((runs, spans)),
-        a_x=dma((runs, batch)),
-        a_c=dma((runs, 2 * batch)),
+        one_send=dma((PAIRS,)),
+        one_recv=dma((PAIRS,)),
+        a_recv=dma((runs, 2 * batch)),
+        a_send=dma((runs, 4)),
+        a_core=dma((runs,)),
         w_recv=dma((spans,)),
-        w_up=dma((spans,)),
-        w_down=dma((spans,)),
+        w_send=dma((3,)),
         v_sems=dma((2, spans)),
         t_sems=dma((2, spans)),
-        f_line=dma((2, spans)),
-    )
-    for number, (_, count) in enumerate(REDUCE):
-        out[f"r{number}_y"] = low(spans, count, band, half)
-        out[f"r{number}_came"] = low(spans, count, band, half)
-        out[f"r{number}_swap"] = low(count, owned, half)
-        out[f"r{number}_swapped"] = low(count, owned, half)
-        out[f"r{number}_sems"] = dma((4, spans))
+        f_line=dma((6,)),
+    )
+    for number, (_, count, y_first) in enumerate(REDUCE):
+        rows = -(-count * owned // 16) * 16
+        if y_first:
+            out[f"r{number}_y"] = low(2, count, band, width)
+            out[f"r{number}_one"] = low(count, band, width)
+            out[f"r{number}_own"] = full(count * owned, width)
+        else:
+            out[f"r{number}_one"] = low(2 * band, width)
+            out[f"r{number}_two_to"] = low(band, width)
+            out[f"r{number}_two"] = low(band, width)
+            out[f"r{number}_own"] = full(band, width)
+        out[f"r{number}_last_to"] = low(rows, width)
+        out[f"r{number}_last"] = low(rows, width)
     return out
 
 
 def block_kernel(names, psg, batch, *refs):
     r = types.SimpleNamespace(**dict(zip(names, refs, strict=True)))
-    spans = batch // 2
     index, question = lax.axis_index("psg"), lax.axis_index("batch")
     far, near = question // 2, question % 2
     side, core = index // 2, index % 2
@@ -326,13 +337,15 @@
     c_peer = (side * 2 + 1 - core, question)
     y_peer = (index, far * 2 + 1 - near)
     d_peer = ((1 - side) * 2 + core, far * 2 + 1 - near)
-    column = [(index, lax.rem(far + hop, spans) * 2 + near) for hop in range(1, spans)]
-    tokens, width = r.dec.shape
+    places = [far, far + 1 - 2 * (far % 2), lax.rem(far + 2, SPANS), SPANS - 1 - far]
+    column = [(index, z * 2 + near) for z in places[1:]]
+    one_peer, two_peer = column[0], column[1]
+    tokens, width = r.dec_here.shape
     owned = r.sq.shape[0]
     band, quarter, half = 2 * owned, batch * owned, width // 2
     share = tokens // psg
     fan = width // batch
-    shards = (r.ck, r.cv, r.co, r.cq, r.so, r.sq, r.sk, r.sv)
+    shards = (r.ck, r.cv, r.co, r.cq, r.so, r.sk, r.sq, r.sv)
     pairs = HEADS // 2
 
     def aligned(value, to):
@@ -346,25 +359,36 @@
 
     sent = []
 
-    def go(copy, when=None):
-        if when is None:
-            copy.start()
-        else:
-            pl.when(when)(copy.start)
-        sent.append((copy, when))
+    def go(copy):
+        copy.start()
+        sent.append(copy)
 
     def remote(src, dst, send, recv, device):
         return pltpu.make_async_remote_copy(
             src_ref=src, dst_ref=dst, send_sem=send, recv_sem=recv, device_id=device, device_id_type=ID
         )
 
-    numbers = iter(range(96))
+    numbers = iter(range(PAIRS))
 
     def pair(src, dst, device):
         number = next(numbers)
         copy = remote(src, dst, r.one_send.at[number], r.one_recv.at[number], device)
         go(copy)
         return copy
+
+    loads = [
+        pltpu.make_async_copy(r.cot, r.cots.at[near], r.load.at[0]),
+        pltpu.make_async_copy(r.dec, r.dec_here, r.load.at[1]),
+        pltpu.make_async_copy(r.enc, r.enc_here, r.load.at[2]),
+    ]
+    for copy in loads:
+        copy.start()
+    stores = []
+
+    def store(src, dst):
+        copy = pltpu.make_async_copy(src, dst, r.store.at[len(stores)])
+        copy.start()
+        stores.append(copy)
 
     barrier = pltpu.get_barrier_semaphore()
     greeted = column + [y_peer, x_peer, c_peer, d_peer]
@@ -398,68 +422,63 @@
         return r.w.at[first : first + count, slice(None) if joined else x, rows, lanes(h)]
 
     def landing(run, x, c, z, h):
-        place = 0 if GATHER[run][2] else x
-        return r.a_recv.at[run, (place * 2 + c) * batch + z * 2 + h]
-
-    def hand(run, x, c, z, h, sem, device, when=None):
+        return r.a_recv.at[run, (0 if GATHER[run][2] else x) * batch + z * 2 + h]
+
+    def hand(run, x, c, z, h, kind, device, recv=None):
         spot = unit(run, x, c, z, h)
-        go(remote(spot, spot, sem, landing(run, x, c, z, h), device), when)
-
-    def landed(run, x, c, z, h, when=None):
+        remote(spot, spot, r.a_send.at[run, kind], landing(run, x, c, z, h) if recv is None else recv, device).start()
+
+    def landed(run, x, c, z, h):
         spot = unit(run, x, c, z, h)
-        copy = remote(spot, spot, r.a_up.at[0, 0], landing(run, x, c, z, h), c_peer)
-        if when is None:
-            copy.wait_recv()
-        else:
-            pl.when(when)(copy.wait_recv)
-
-    def wide(run, z, h, when=None):
+        remote(spot, spot, r.a_send.at[run, 0], landing(run, x, c, z, h), c_peer).wait_recv()
+
+    def wide(run, z, h):
         if not GATHER[run][2]:
-            hand(run, side, core, z, h, r.a_x.at[run, z * 2 + h], x_peer, when)
-        hand(run, side, core, z, h, r.a_c.at[run, z * 2 + h], c_peer, when)
+            hand(run, side, core, z, h, 2, x_peer)
+        hand(run, side, core, z, h, 3, c_peer, r.a_core.at[run])
 
     def offer(run):
-        hand(run, side, core, far, near, r.a_up.at[run, far], (index, question + 2), far < spans - 1)
-        hand(run, side, core, far, near, r.a_down.at[run, far], (index, question - 2), far > 0)
-        hand(run, side, core, far, near, r.a_y.at[run, far], y_peer)
+        hand(run, side, core, far, near, 0, two_peer)
+        hand(run, side, core, far, near, 0, one_peer)
+        hand(run, side, core, far, near, 1, y_peer)
         wide(run, far, near)
 
-    def inside(z):
-        return (z >= 0) & (z < spans)
-
     def from_y(run, step):
-        for sign in (-1, 1) if 0 < step < spans else (1,) if step == 0 else ():
-            z = far + sign * step
-            valid = inside(z) if step else None
-            landed(run, side, core, z, 1 - near, valid)
-            wide(run, z, 1 - near, valid)
+        landed(run, side, core, places[step], 1 - near)
+        wide(run, places[step], 1 - near)
 
     def from_line(run, step):
-        for sign in (-1, 1) if step < spans else ():
-            z = far + sign * step
-            valid = inside(z)
-            landed(run, side, core, z, near, valid)
-            if sign < 0:
-                hand(run, side, core, z, near, r.a_up.at[run, z], (index, question + 2), valid & (far < spans - 1))
-            else:
-                hand(run, side, core, z, near, r.a_down.at[run, z], (index, question - 2), valid & (far > 0))
-            hand(run, side, core, z, near, r.a_y.at[run, z], y_peer, valid)
-            wide(run, z, near, valid)
+        z = places[step]
+        landed(run, side, core, z, near)
+        if step == 2:
+            hand(run, side, core, z, near, 0, one_peer)
+        hand(run, side, core, z, near, 1, y_peer)
+        wide(run, z, near)
 
     def from_x(run, step):
-        for sign in (-1, 1) if 0 < step < spans else (1,) if step == 0 else ():
-            z = far + sign * step
-            valid = inside(z) if step else None
-            for h in (near, 1 - near):
-                landed(run, 1 - side, core, z, h, valid)
-                hand(run, 1 - side, core, z, h, r.a_c.at[run, batch + z * 2 + h], c_peer, valid)
+        z = places[step]
+        for h in (near, 1 - near):
+            landed(run, 1 - side, core, z, h)
+            hand(run, 1 - side, core, z, h, 3, c_peer, r.a_core.at[run])
+
+    def sent_of(run):
+        first, count, joined = GATHER[run]
+        lower = r.w.at[first : first + count, slice(None) if joined else 0]
+        quarters = (slice(None),) * (2 if joined else 1)
+        sizes = [
+            lower.at[(*quarters, pl.ds(0, 3 * band), pl.ds(0, half))],
+            lower.at[(*quarters, pl.ds(0, quarter), pl.ds(0, half))],
+            None if joined else lower.at[(*quarters, pl.ds(0, quarter), slice(None))],
+            r.w.at[first : first + count, :, pl.ds(0, quarter), :],
+        ]
+        for kind, size in enumerate(sizes):
+            if size is not None:
+                remote(size, size, r.a_send.at[run, kind], r.a_core.at[run], c_peer).wait_send()
 
     def complete(run):
-        for z in range(spans):
-            for h in range(2):
-                landed(run, side, 1 - core, z, h)
-                if not GATHER[run][2]:
-                    landed(run, 1 - side, 1 - core, z, h)
+        first, count, _ = GATHER[run]
+        all_of = r.w.at[first : first + count, :, span((1 - core) * quarter, quarter, 16), :]
+        remote(all_of, all_of, r.a_send.at[run, 0], r.a_core.at[run], c_peer).wait_recv()
 
     def matrix(number):
         return r.w[number].reshape(width, width)
@@ -485,14 +504,12 @@
         def fourth(copy):
             copy.wait_recv()
             buf[3] = (buf[2].astype(F32) + recv[2].astype(F32)).astype(buf.dtype)
-            for hop in range(1, spans):
-                z = lax.rem(far + hop, spans)
+            for z in places[1:]:
                 go(remote(buf.at[3], recv.at[3 + far], sems.at[0, z], sems.at[1, far], (index, z * 2 + near)))
 
         def last():
             total = buf[3].astype(F32)
-            for hop in range(1, spans):
-                z = lax.rem(far + hop, spans)
+            for z in places[1:]:
                 remote(buf.at[3], recv.at[3 + z], sems.at[0, z], sems.at[1, z], c_peer).wait_recv()
                 total = total + recv[3 + z].astype(F32)
             return total
@@ -522,7 +539,7 @@
     offer(1)
     m_tail.wait_recv()
     join(1)
-    own_tail = r.w.at[CO : CO + 2, side, span(row, band, 16), lanes(near)]
+    own_tail = r.w.at[CQ : CQ + 2, side, span(row, band, 16), lanes(near)]
     x_tail = pair(own_tail, own_tail, x_peer)
     v_copy = v_second(v_copy)
 
@@ -530,75 +547,71 @@
     other_cols = span((1 - near) * cut, cut, LANES)
     own_cols = span(near * cut, cut, LANES)
     own_fan = span(question * fan, fan, 16)
+    r.f[0, own_fan] = r.h_in[:, own_cols]
+    r.f[1, own_fan] = r.h_out[:, own_cols]
+
+    def f_unit(z):
+        return r.f.at[:, span(z * 2 * fan, 2 * fan, 16), :]
+
+    def f_hand(z, sem, device):
+        go(remote(f_unit(z), f_unit(z), sem, r.w_recv.at[z], device))
+
+    def f_landed(step):
+        z = places[step]
+        remote(f_unit(z), f_unit(z), r.w_send.at[0], r.w_recv.at[z], c_peer).wait_recv()
+        if step == 2:
+            f_hand(z, r.w_send.at[2], one_peer)
+
+    def near_units(run):
+        from_y(run, 0)
+        from_line(run, 2)
+        from_line(run, 1)
+
+    def far_units(run):
+        from_line(run, 3)
+        from_y(run, 1)
+        from_y(run, 2)
+
+    near_units(0)
+    near_units(1)
+    x_tail.wait_recv()
+    offer(2)
+    far_units(0)
+    far_units(1)
+    offer(3)
+    near_units(2)
+    from_y(0, 3)
+    from_y(1, 3)
+    offer(4)
+    from_x(0, 0)
+    from_x(1, 0)
+    v_copy = v_third(v_copy)
+    far_units(2)
+    from_x(0, 1)
+    from_x(1, 1)
+    near_units(3)
+    v_fourth(v_copy)
+    from_x(0, 2)
+    from_x(1, 2)
+    from_y(2, 3)
     h_copies = [
         pair(r.h_in.at[:, other_cols], r.f.at[0, own_fan], y_peer),
         pair(r.h_out.at[:, other_cols], r.f.at[1, own_fan], y_peer),
     ]
-    r.f[0, own_fan] = r.h_in[:, own_cols]
-    r.f[1, own_fan] = r.h_out[:, own_cols]
-    r.cots[near] = r.cot[...]
-
-    def f_unit(z):
-        return r.f.at[:, span(z * 2 * fan, 2 * fan, 16), :]
-
-    def f_hand(z, sem, device, when):
-        go(remote(f_unit(z), f_unit(z), sem, r.w_recv.at[z], device), when)
-
-    def f_landed(step):
-        for sign in (-1, 1) if step < spans else ():
-            z = far + sign * step
-            pl.when(inside(z))(remote(f_unit(z), f_unit(z), r.w_up.at[0], r.w_recv.at[z], c_peer).wait_recv)
-            if sign < 0:
-                f_hand(z, r.w_up.at[z], (index, question + 2), inside(z) & (far < spans - 1))
-            else:
-                f_hand(z, r.w_down.at[z], (index, question - 2), inside(z) & (far > 0))
-
-    from_y(0, 0)
-    from_y(1, 0)
-    from_line(0, 1)
-    from_line(1, 1)
-    x_tail.wait_recv()
-    offer(2)
-    from_y(0, 1)
-    from_y(1, 1)
-    v_copy = v_third(v_copy)
-    from_x(0, 0)
-    from_x(1, 0)
-    from_line(0, 2)
-    from_line(1, 2)
-    from_y(2, 0)
-    from_line(2, 1)
+    far_units(3)
+    loads[0].wait()
+    loads[1].wait()
+    from_x(0, 3)
+    from_x(1, 3)
+    from_y(3, 3)
+    near_units(4)
     for copy in h_copies:
         copy.wait_recv()
-    f_hand(far, r.w_up.at[far], (index, question + 2), far < spans - 1)
-    f_hand(far, r.w_down.at[far], (index, question - 2), far > 0)
-    from_y(0, 2)
-    from_y(1, 2)
-    from_x(0, 1)
-    v_fourth(v_copy)
-    from_line(0, 3)
-    from_line(1, 3)
-    from_line(2, 2)
-    from_y(2, 1)
-    from_x(1, 1)
-    from_y(0, 3)
-    from_y(1, 3)
-    from_x(0, 2)
-    from_line(2, 3)
-    from_y(2, 2)
-    f_landed(1)
-    cot_copy = pair(r.cot, r.cots.at[near], y_peer)
-    from_x(1, 2)
-    from_x(0, 3)
-    from_y(2, 3)
-    complete(0)
+    f_hand(far, r.w_send.at[0], two_peer)
+    f_hand(far, r.w_send.at[1], one_peer)
+    for run in range(3):
+        complete(run)
     vectors = v_last()
-    for cols in column_tiles(width):
-        r.key[:, cols] = nn(r.enc[...], r.w[CK, :, :, cols].reshape(width, -1)).astype(BF16)
-        r.val[:, cols] = nn(r.enc[...], r.w[CV, :, :, cols].reshape(width, -1)).astype(BF16)
-    f_landed(2)
-    from_x(1, 3)
-    complete(1)
 
     gains = [vectors[3 + i : 4 + i] for i in range(3)]
     chosen = r.tid[0]
@@ -607,14 +620,24 @@
     )
     r.gains[0:3] = vectors[3:6]
     self_forward(
-        r.dec[...].astype(F32), row_embed, gains[0], matrix(SQ), matrix(SK), matrix(SV), matrix(SO), gains[1],
+        r.dec_here[...].astype(F32), row_embed, gains[0], matrix(SQ), matrix(SK), matrix(SV), matrix(SO), gains[1],
         r.res, r.n1, r.q, r.k, r.v, r.s_probs, r.mix, r.after, r.n2,
     )
-    complete(2)
+    far_units(4)
+    loads[2].wait()
+    for cols in column_tiles(width):
+        r.key[:, cols] = nn(r.enc_here[...], r.w[CK, :, :, cols].reshape(width, -1)).astype(BF16)
+        r.val[:, cols] = nn(r.enc_here[...], r.w[CV, :, :, cols].reshape(width, -1)).astype(BF16)
+    complete(3)
     r.qc[...] = nn(r.n2[...], matrix(CQ)).astype(BF16)
 
     cross_attend(r.qc, r.key, r.val, r.c_probs, r.o_stat, r.o_part)
     first = [pair(r.o_part.at[:, 1 - core], r.o_core, c_peer), pair(r.o_stat.at[:, 1 - core], r.o_core_stat, c_peer)]
+    from_y(4, 3)
+    for step in range(SPANS):
+        from_x(4, step)
+    f_landed(2)
+    f_landed(1)
     for copy in first:
         copy.wait_recv()
     join_parts(
@@ -622,9 +645,11 @@
         r.o_to, r.o_to_stat,
     )
     second = [pair(r.o_to, r.o_x, x_peer), pair(r.o_to_stat, r.o_x_stat, x_peer)]
+    cot_copy = pair(r.cots.at[near], r.cots.at[near], y_peer)
     join_parts(
         r.o_part[side, core], r.o_stat[side, core], r.o_core[side], r.o_core_stat[side], r.o_mid, r.o_mid_stat
     )
+    complete(4)
     for copy in second:
         copy.wait_recv()
     join_parts(r.o_mid[...], r.o_mid_stat[...], r.o_x[...], r.o_x_stat[...], r.mixed_rows, r.stat_rows)
@@ -658,18 +683,17 @@
 
     mine = block8(near, side, core)
     to_y, to_x, to_d, to_c = [pair(mine, mine, peer) for peer in (y_peer, x_peer, d_peer, c_peer)]
-    log_then = spread4(r.log_total)
-    mixc_then = spread4(r.mixc)
     onward = [to_c]
     for copy, h, x in ((to_y, 1 - near, side), (to_x, near, 1 - side), (to_d, 1 - near, 1 - side)):
         copy.wait_recv()
         onward.append(pair(block8(h, x, core), block8(h, x, core), c_peer))
-    log_end = log_then()
     f_landed(3)
     cot_copy.wait_recv()
     for copy in onward:
         copy.wait_recv()
 
+    log_then = spread4(r.log_total)
+    mixc_then = spread4(r.mixc)
     x = r.n3[...].reshape(2 * tokens, width)
     top = r.cots[...].reshape(2 * tokens, width)
     act, dpre = feed_forward(x, top, r.f[0], r.f[1])
@@ -709,102 +733,143 @@
     r.gf[0] = nn(x.T, dpre).astype(BF16)
     r.gf[1] = nn(top.T, act).astype(BF16)
 
-    others = [lax.rem(far + hop, spans) for hop in range(1, spans)]
-
     def line_kit(came, src, sems):
-        def copy(z, slot):
-            return remote(src(z), came.at[slot], sems.at[0, z], sems.at[1, slot], (index, z * 2 + near))
-
-        def send(z):
-            go(copy(z, far))
+        def over_pair(step):
+            slot = step // 2
+            return remote(src(places[step]), came.at[slot], sems.at[slot], sems.at[3 + slot], one_peer)
+
+        def over_pairs():
+            return remote(src(places[2]), came.at[2], sems.at[2], sems.at[5], two_peer)
+
+        def first():
+            go(over_pair(3))
+            go(over_pair(1))
+
+        def second(value):
+            over_pair(3).wait_recv()
+            src(places[2])[...] = (value + came[1].astype(F32)).astype(BF16)
+            go(over_pairs())
 
         def total(value, out):
-            out[...] = value
-            for z in others:
-                copy(far, z).wait_recv()
-                out[...] = out[...] + came[z].astype(F32)
-
-        return send, total
+            over_pair(1).wait_recv()
+            both = value + came[0].astype(F32)
+            over_pairs().wait_recv()
+            out[...] = both + came[2].astype(F32)
+
+        return first, second, total
 
     def f_piece(z):
         return r.gf.at[:, span(z * 2 * fan, 2 * fan, 16), :]
 
-    f_send, f_total = line_kit(r.f_came, f_piece, r.f_line)
-    for z in others:
-        f_send(z)
+    f_first, f_second, f_total = line_kit(r.f_came, f_piece, r.f_line)
+    f_first()
+    log_end = log_then()
+    mixc_end = mixc_then()
 
     upstream = dn_last()
     y = r.after_rows[...]
     factor = rms_factor(y)
     scales = r.gains[2:3]
     gain_three = jnp.sum(upstream * y * factor, 0, keepdims=True)
-    grad = r.cot[my_rows, :].astype(F32) + norm_back(y, factor, scales, upstream)
+    grad = r.cots[near, my_rows, :].astype(F32) + norm_back(y, factor, scales, upstream)
     r.grad_rows[...] = grad
     low = grad.astype(BF16)
     r.dcross[side, core] = low
-    dmixed = nt(low, matrix(CO)).astype(BF16)
-    r.dmixed[side, core] = dmixed
-    dmixed_then = spread4(r.dmixed)
-    r.dots[side, core] = head_sums(dmixed.astype(F32) * r.mixed_rows[...])
-    dots_then = spread4(r.dots)
     dcross_then = spread4(r.dcross)
-    mixc_end = mixc_then()
     hp_last = hp_second()
-    dmixed_end = dmixed_then()
-    dots_end = dots_then()
+    log_end()
+    mixc_end()
     dcross_end = dcross_then()
-    for end in (log_end, mixc_end, dmixed_end, dots_end, dcross_end):
-        end()
+    dcross_end()
 
     def rows_of(ref):
         return ref[...].reshape(tokens, ref.shape[-1])
 
-    def reduce_kit(number):
-        first, count = REDUCE[number]
-        got_y, sems = getattr(r, f"r{number}_y"), getattr(r, f"r{number}_sems")
-
-        def piece(z, h):
-            return r.g.at[first : first + count, span(z * band, band, 16), lanes(h)]
-
-        def y_copy(z):
-            return remote(piece(z, 1 - near), got_y.at[z], sems.at[0, z], sems.at[1, z], y_peer)
-
-        send, total = line_kit(getattr(r, f"r{number}_came"), lambda z: got_y.at[z], sems.at[2:4])
-
-        def begin():
-            for z in others + [far]:
-                go(y_copy(z))
-
-        def value(z):
-            y_copy(z).wait_recv()
-            mine = r.g[first : first + count, span(z * band, band, 16), lanes(near)]
-            return mine.astype(F32) + got_y[z].astype(F32)
+    parity, high = far % 2, far // 2
+
+    def ordered(value, y_first):
+        blocks = [(z, h) for z in range(SPANS) for h in range(2)]
+        if y_first:
+            blocks.sort(key=lambda block: (block[1], block[0] % 2, block[0] // 2))
+        else:
+            blocks.sort(key=lambda block: (block[0] % 2, block[0] // 2, block[1]))
+        parts = [value[(z * 2 + h) * owned : (z * 2 + h + 1) * owned] for z, h in blocks]
+        return jnp.concatenate(parts, 0).astype(BF16)
+
+    def last_step(number, mine, theirs, peer):
+        first, count, _ = REDUCE[number]
+        to, got = getattr(r, f"r{number}_last_to"), getattr(r, f"r{number}_last")
+        if to.shape[0] > theirs.shape[0]:
+            theirs = jnp.concatenate([theirs, jnp.zeros((to.shape[0] - theirs.shape[0], width), F32)], 0)
+        to[...] = theirs.astype(BF16)
+        copy = pair(to, got, peer)
+        r.g_attn_here[first : first + count] = mine.reshape(count, owned, width)
+
+        def end():
+            copy.wait_recv()
+            more = got[...].astype(F32)[: count * owned]
+            r.g_attn_here[first : first + count] = r.g_attn_here[first : first + count] + more.reshape(count, owned, width)
+            store(r.g_attn_here.at[first : first + count], r.g_attn.at[first : first + count])
+
+        return end
+
+    def line_first(number):
+        m = REDUCE[number][0]
+        one, two_to, two, own = [getattr(r, f"r{number}_{name}") for name in ("one", "two_to", "two", "own")]
+        copies = []
 
         def forward():
-            for z in others:
-                got_y[z] = value(z).astype(BF16)
-                send(z)
-
-        swap, swapped = getattr(r, f"r{number}_swap"), getattr(r, f"r{number}_swapped")
-        out = r.g_attn.at[first : first + count]
+            copies.append(pair(r.g.at[m, span((1 - parity) * 2 * band, 2 * band, 16), :], one, one_peer))
+
+        def again():
+            copies[0].wait_recv()
+            total = r.g[m, span(parity * 2 * band, 2 * band, 16), :].astype(F32) + one[...].astype(F32)
+            upper, lower = total[:band], total[band:]
+            two_to[...] = jnp.where(high == 0, lower, upper).astype(BF16)
+            copies.append(pair(two_to, two, two_peer))
+            own[...] = jnp.where(high == 0, upper, lower)
 
         def finish():
-            sums = r.r_sum.at[:count]
-
-            total(value(far), sums)
-            both = sums[...]
-            upper, lower = both[:, :owned], both[:, owned:]
-            swap[...] = jnp.where(near == 0, lower, upper).astype(BF16)
-            copy = pair(swap, swapped, y_peer)
-            out[:, :, lanes(near)] = jnp.where(near == 0, upper, lower)
-
-            def end():
-                copy.wait_recv()
-                out[:, :, lanes(1 - near)] = swapped[...].astype(F32)
-
-            return end
-
-        return begin, forward, finish
+            copies[1].wait_recv()
+            total = own[...] + two[...].astype(F32)
+            upper, lower = total[:owned], total[owned:]
+            return last_step(
+                number, jnp.where(near == 0, upper, lower), jnp.where(near == 0, lower, upper), y_peer
+            )
+
+        return forward, again, finish
+
+    def y_first(number):
+        first, count, _ = REDUCE[number]
+        got_y, one = getattr(r, f"r{number}_y"), getattr(r, f"r{number}_one")
+        copies = {}
+
+        def piece(h, p):
+            return r.g.at[first : first + count, span(h * 2 * band + p * band, band, 16), :]
+
+        def begin(mine):
+            p = parity if mine else 1 - parity
+            copies[mine] = pair(piece(1 - near, p), got_y.at[1 if mine else 0], y_peer)
+
+        def value(mine):
+            copies[mine].wait_recv()
+            return piece(near, parity if mine else 1 - parity)[...].astype(F32) + got_y[1 if mine else 0].astype(F32)
+
+        def forward():
+            got_y[0] = value(False).astype(BF16)
+            copies["one"] = pair(got_y.at[0], one, one_peer)
+
+        def again():
+            total = value(True)
+            copies["one"].wait_recv()
+            total = total + one[...].astype(F32)
+            upper = total[:, :owned].reshape(count * owned, width)
+            lower = total[:, owned:].reshape(count * owned, width)
+            return last_step(
+                number, jnp.where(high == 0, upper, lower), jnp.where(high == 0, lower, upper), two_peer
+            )
+
+        return begin, forward, again
 
     own_rows = span(index * quarter, quarter, 16)
 
@@ -812,16 +877,15 @@
         r.turned[slot] = value.T
         return r.turned[slot, own_rows, :]
 
-    co_begin, co_forward, co_finish = reduce_kit(0)
-    so_begin, so_forward, so_finish = reduce_kit(1)
-    late_begin, late_forward, late_finish = reduce_kit(2)
-    kv_begin, kv_forward, kv_finish = reduce_kit(3)
-    r.g[CO] = nn(turn(0, rows_of(r.mixc)), rows_of(r.dcross)).astype(BF16)
-    co_begin()
+    co_begin, co_forward, co_again = y_first(0)
+    so_begin, so_forward, so_again = y_first(1)
+    late_begin, late_forward, late_again = y_first(2)
+    k_forward, k_again, k_finish = line_first(3)
+    v_forward, v_again, v_finish = line_first(4)
 
     ratio = jnp.exp(rows_of(r.o_stat)[:, :LANES] - rows_of(r.log_total))
-    dots = rows_of(r.dots)
-    dmixed = rows_of(r.dmixed)
+    dmixed = nt(rows_of(r.dcross), matrix(CO)).astype(BF16)
+    dots = head_sums(dmixed.astype(F32) * rows_of(r.mixc).astype(F32))
     for number in range(pairs):
         cross_backward(
             number, r.qc, dmixed, r.key, r.val, r.c_probs, ratio, dots, r.dq_part
@@ -831,9 +895,28 @@
     q_first.wait_recv()
     r.dq_to[...] = (r.dq_part[1 - side, core].astype(F32) + r.dq_core[1 - side].astype(F32)).astype(BF16)
     q_second = pair(r.dq_to, r.dq_x, x_peer)
-    r.c_probs[:, :LANES] = r.enc[...].T.reshape(pairs, LANES, -1)
-    for cols in column_tiles(width):
-        r.gkv[0, :, :, cols] = nn(r.c_probs[:, :LANES].reshape(width, -1), r.key[:, cols]).astype(BF16).reshape(2, 2 * quarter, -1)
+    r.c_probs[:, :LANES] = r.enc_here[...].T.reshape(pairs, LANES, -1)
+    kv_other, kv_own = span((1 - core) * quarter, quarter, 16), span(core * quarter, quarter, 16)
+
+    def kv_first(part, ref):
+        for cols in column_tiles(width):
+            product = nn(r.c_probs[:, :LANES].reshape(width, -1), ref[:, cols])
+            r.gkv[part, :, :, cols] = product.astype(BF16).reshape(2, 2 * quarter, -1)
+        return pair(r.gkv.at[part, :, kv_other, :], r.kv_core.at[part], c_peer)
+
+    def kv_second(part, copy):
+        copy.wait_recv()
+        total = r.gkv[part, 1 - side, kv_own, :].astype(F32) + r.kv_core[part, 1 - side].astype(F32)
+        r.kv_to[part] = total.astype(BF16)
+        return pair(r.kv_to.at[part], r.kv_x.at[part], x_peer)
+
+    def kv_third(part, copy):
+        copy.wait_recv()
+        total = r.gkv[part, side, kv_own, :].astype(F32) + r.kv_core[part, side].astype(F32)
+        r.g[CK + part] = ordered(total + r.kv_x[part].astype(F32), False)
+
+    f_second(f_piece(places[2])[...].astype(F32))
+    k_copy = kv_first(0, r.key)
     q_second.wait_recv()
     dq_rows = (
         r.dq_part[side, core].astype(F32) + r.dq_core[side].astype(F32) + r.dq_x[...].astype(F32)
@@ -848,41 +931,58 @@
     r.dself[side, core] = low
     dself_then = spread4(r.dself)
     r.dself_rest[side, core] = (grad - low.astype(F32)).astype(BF16)
+    dqc_then = spread4(r.dqc)
+    r.g[CO] = ordered(nn(turn(0, rows_of(r.mixc)), rows_of(r.dcross)), True)
+    co_begin(False)
+    co_begin(True)
+    r.val[...] = r.c_probs[:, LANES:].reshape(width, -1).T
+    dself_end = dself_then()
+    k_copy = kv_second(0, k_copy)
+    v_copy = kv_first(1, r.val)
+    dself_end()
+    dqc_end = dqc_then()
+
+    dself = rows_of(r.dself)
+    r.g[SO] = ordered(nn(turn(1, r.mix[...]), dself), True)
+    dmixed = nt(dself, matrix(SO)).astype(BF16)
+    dqc_end()
+    r.g[CQ] = ordered(nn(turn(2, r.n2[...]), rows_of(r.dqc)), True)
+    so_begin(False)
+    v_copy = kv_second(1, v_copy)
     rest_then = spread4(r.dself_rest)
-    dqc_then = spread4(r.dqc)
-    r.val[...] = r.c_probs[:, LANES:].reshape(width, -1).T
-    for cols in column_tiles(width):
-        r.gkv[1, :, :, cols] = nn(r.c_probs[:, :LANES].reshape(width, -1), r.val[:, cols]).astype(BF16).reshape(2, 2 * quarter, -1)
-    kv_first = pair(r.gkv.at[:, :, span((1 - core) * quarter, quarter, 16), :], r.kv_core, c_peer)
-    dself_end = dself_then()
-    dqc_end = dqc_then()
-    rest_end = rest_then()
+    self_backward(dmixed, r.q, r.k, r.v, r.s_probs, r.dq, r.dk, r.dv)
     co_forward()
-    kv_first.wait_recv()
-    kv_own = span(core * quarter, quarter, 16)
-    r.kv_to[...] = (
-        r.gkv[:, 1 - side, kv_own, :].astype(F32) + r.kv_core[:, 1 - side].astype(F32)
-    ).astype(BF16)
-    kv_second = pair(r.kv_to, r.kv_x, x_peer)
-    dself_end()
-    dqc_end()
-
-    dself = rows_of(r.dself)
-    r.g[SO] = nn(turn(1, r.mix[...]), dself).astype(BF16)
-    r.g[CQ] = nn(turn(2, r.n2[...]), rows_of(r.dqc)).astype(BF16)
-    so_begin()
-    dmixed = nt(dself, matrix(SO)).astype(BF16)
-    self_backward(dmixed, r.q, r.k, r.v, r.s_probs, r.dq, r.dk, r.dv)
+    kv_third(0, k_copy)
+    k_forward()
     normed = turn(3, r.n1[...])
     for number, ref in ((SQ, r.dq), (SK, r.dk), (SV, r.dv)):
-        r.g[number] = nn(normed, ref[...]).astype(BF16)
-    late_begin()
-    rest_end()
+        r.g[number] = ordered(nn(normed, ref[...]), True)
+    late_begin(False)
+    so_begin(True)
+    co_end = co_again()
+    so_forward()
+    late_begin(True)
+
+    f_total(f_piece(far)[...].astype(F32), r.f_sum)
+    both = r.f_sum[...]
+    upper, lower = both[:, :fan], both[:, fan:]
+    r.f_swap[...] = jnp.where(near == 0, lower, upper).astype(BF16)
+    f_copy = pair(r.f_swap, r.f_swapped, y_peer)
+    kept = jnp.where(near == 0, upper, lower)
+    r.g_in_here[:, own_cols] = kept[0]
+    r.g_out_here[:, own_cols] = kept[1]
+
     upstream = nt(r.dq[...], matrix(SQ)) + nt(r.dk[...], matrix(SK)) + nt(r.dv[...], matrix(SV))
+    kv_third(1, v_copy)
+    k_again()
+    v_forward()
+    late_forward()
+    rest_then()()
     x = r.res[...]
     factor = rms_factor(x)
     grad = dself.astype(F32) + rows_of(r.dself_rest).astype(F32) + norm_back(x, factor, r.gains[0:1], upstream)
-    r.grad_dec[...] = grad
+    r.grad_dec_here[...] = grad
+    store(r.grad_dec_here, r.grad_dec)
     mine = lax.broadcasted_iota(jnp.int32, (tokens, 1), 0) // share == index
     task = jnp.sum(jnp.where(mine, grad, 0.0), 0, keepdims=True)
     r.t_buf[0, 0:3] = jnp.concatenate([task * jnp.where(chosen == i, 1.0, 0.0).astype(F32) for i in range(3)], 0)
@@ -892,54 +992,79 @@
     r.t_buf[0, 6:8] = jnp.zeros((2, width), F32)
     t_first, t_second, t_third, t_fourth, t_last = ladder(r.t_buf, r.t_recv, r.t_sems)
     t_copy = t_first()
+    so_end = so_again()
     hidden = hp_last()
-    r.block_out[side, core] = (r.after_rows[...] + hidden).astype(BF16)
-    out_then = spread4(r.block_out)
-    so_forward()
+    r.block_here[side, core] = (r.after_rows[...] + hidden).astype(BF16)
+    out_then = spread4(r.block_here)
     t_copy = t_second(t_copy)
-    for cols in column_tiles(width):
-        r.grad_enc[:, cols] = nt(r.key[...], matrix(CK)[cols]) + nt(r.val[...], matrix(CV)[cols])
-    late_forward()
-    kv_second.wait_recv()
-    r.g[CK : CK + 2] = (
-        r.gkv[:, side, kv_own, :].astype(F32) + r.kv_core[:, side].astype(F32) + r.kv_x[...].astype(F32)
-    ).astype(BF16)
-    kv_begin()
+    def encoded_columns(cols):
+        r.grad_enc_here[:, cols] = nt(r.key[...], matrix(CK)[cols]) + nt(r.val[...], matrix(CV)[cols])
+
+    tiles = column_tiles(width)
+    encoded_columns(tiles[0])
     t_copy = t_third(t_copy)
     out_end = out_then()
-
-    f_total(f_piece(far)[...].astype(F32), r.f_sum)
-    both = r.f_sum[...]
-    upper, lower = both[:, :fan], both[:, fan:]
-    r.f_swap[...] = jnp.where(near == 0, lower, upper).astype(BF16)
-    f_copy = pair(r.f_swap, r.f_swapped, y_peer)
-    kept = jnp.where(near == 0, upper, lower)
-    r.g_in[:, own_cols] = kept[0]
-    r.g_out[:, own_cols] = kept[1]
-    co_end = co_finish()
-    so_end = so_finish()
+    v_again()
+    k_end = k_finish()
     t_fourth(t_copy)
-    kv_forward()
-    late_end = late_finish()
-    f_copy.wait_recv()
-    r.g_in[:, other_cols] = r.f_swapped[0].astype(F32)
-    r.g_out[:, other_cols] = r.f_swapped[1].astype(F32)
-    kv_end = kv_finish()
-    r.g_vec[...] = t_last()
-    out_end()
+    for cols in tiles[1:-1]:
+        encoded_columns(cols)
+    late_end = late_again()
+    encoded_columns(tiles[-1])
+    store(r.grad_enc_here, r.grad_enc)
     co_end()
     so_end()
+    v_end = v_finish()
+    out_end()
+    for p in range(psg):
+        store(r.block_here.at[p // 2, p % 2], r.block_out.at[p])
+    f_copy.wait_recv()
+    r.g_in_here[:, other_cols] = r.f_swapped[0].astype(F32)
+    r.g_out_here[:, other_cols] = r.f_swapped[1].astype(F32)
+    store(r.g_in_here, r.g_in)
+    store(r.g_out_here, r.g_out)
+    r.g_vec_here[...] = lax.dot_general(
+        t_last(), place.astype(F32), (((1,), (1,)), ((), ())), precision=lax.Precision.HIGHEST
+    )
+    store(r.g_vec_here, r.g_vec)
+    k_end()
+    v_end()
     late_end()
-    kv_end()
-    for copy, when in sent:
-        if when is None:
-            copy.wait_send()
-        else:
-            pl.when(when)(copy.wait_send)
+    for copy in stores:
+        copy.wait()
+    for run in range(len(GATHER)):
+        sent_of(run)
+    for copy in sent:
+        copy.wait_send()
+
+
+def settle_kernel(block_out, grad_dec, grad_enc, g_attn, g_in, g_out, g_vec, *rest):
+    outs, vectors, here, sems = rest[:13], rest[13:17], rest[17:23], rest[23]
+    sources = [grad_enc, block_out, grad_dec, g_attn, g_in, g_out]
+    arrivals = [
+        pltpu.make_async_copy(source, spot, sems.at[0, number])
+        for number, (source, spot) in enumerate(zip(sources, here, strict=True))
+    ]
+    for copy in arrivals:
+        copy.start()
+    first = 0
+    for out in vectors:
+        out[...] = g_vec[first : first + out.shape[0]]
+        first += out.shape[0]
+    spots = [[outs[2]], [outs[0]], [outs[1]], outs[3:11], [outs[11]], [outs[12]]]
+    departures = []
+    for copy, spot, places in zip(arrivals, here, spots, strict=True):
+        copy.wait()
+        for number, out in enumerate(places):
+            source = spot if len(places) == 1 else spot.at[number]
+            departures.append(pltpu.make_async_copy(source, out, sems.at[1, len(departures)]))
+            departures[-1].start()
+    for copy in departures:
+        copy.wait()
 
 
 def regular(owned, psg, batch, tokens, width):
-    return psg == 4 and batch in (4, 6, 8) and owned % 8 == 0 and tokens % 128 == 0 and (width // 2) % LANES == 0
+    return psg == 4 and batch == 2 * SPANS and owned % 8 == 0 and tokens % 128 == 0 and (width // 2) % LANES == 0
 
 
 def fused(psg, batch, decoder_in, encoded, cotangent, task_ids, task_embed, gain_self, self_query, self_key, self_value,
@@ -951,44 +1076,66 @@
     scratch = buffers(psg, batch, tokens, length, width, owned, hidden)
     names = INPUTS + OUTPUTS + list(scratch)
     vmem = pl.BlockSpec(memory_space=pltpu.VMEM)
-    quad = (2, 2, tokens // psg, width)
+    hbm = pl.BlockSpec(memory_space=pl.ANY)
     block_out, grad_decoder, grad_encoded, g_attn, g_in, g_out, g_vec = pl.pallas_call(
         functools.partial(block_kernel, names, psg, batch),
         out_shape=(
-            jax.ShapeDtypeStruct(quad, BF16),
+            jax.ShapeDtypeStruct((psg,) + (tokens // psg, width), BF16),
             jax.ShapeDtypeStruct((tokens, width), F32),
             jax.ShapeDtypeStruct((length, width), F32),
             jax.ShapeDtypeStruct((8, owned, width), F32),
             jax.ShapeDtypeStruct((width // batch, hidden), F32),
             jax.ShapeDtypeStruct((width // batch, hidden), F32),
-            jax.ShapeDtypeStruct((8, width), F32),
+            jax.ShapeDtypeStruct((8, owned), F32),
         ),
-        in_specs=[pl.BlockSpec(memory_space=pltpu.SMEM)] + [vmem] * (len(INPUTS) - 1),
-        out_specs=[vmem] * len(OUTPUTS),
+        in_specs=[pl.BlockSpec(memory_space=pltpu.SMEM)] + [hbm] * 3 + [vmem] * (len(INPUTS) - 4),
+        out_specs=[hbm] * len(OUTPUTS),
         scratch_shapes=list(scratch.values()),
         compiler_params=pltpu.CompilerParams(collective_id=0, has_side_effects=True, vmem_limit_bytes=56 * MIB),
         name="decoder_block",
     )(task_ids, decoder_in[0], cotangent[0], encoded[0], task_embed, gain_self[None],
       gain_cross[None], gain_hidden[None], self_query, self_key, self_value, self_output,
       cross_query, cross_output, cross_key, cross_value, hidden_in, hidden_out.T)
-    first = (lax.axis_index("psg") * batch + lax.axis_index("batch")) * owned
-    mine = lax.dynamic_slice_in_dim(g_vec, first, owned, 1)
+    shapes = [(tokens, width), (tokens, width), (length, width)] + [(owned, width)] * 8 + [(width // batch, hidden)] * 2
+    small = [(groups, owned)] + [(1, owned)] * 3
+    outs = pl.pallas_call(
+        settle_kernel,
+        out_shape=tuple(
+            jax.ShapeDtypeStruct(shape, F32 if number else BF16) for number, shape in enumerate(shapes + small)
+        ),
+        in_specs=[hbm] * 6 + [vmem],
+        out_specs=[hbm] * len(shapes) + [vmem] * len(small),
+        scratch_shapes=[
+            pltpu.VMEM((length, width), F32),
+            pltpu.VMEM((tokens, width), BF16),
+            pltpu.VMEM((tokens, width), F32),
+            pltpu.VMEM((8, owned, width), F32),
+            pltpu.VMEM((width // batch, hidden), F32),
+            pltpu.VMEM((width // batch, hidden), F32),
+            pltpu.SemaphoreType.DMA((2, len(shapes))),
+        ],
+        compiler_params=pltpu.CompilerParams(vmem_limit_bytes=60 * MIB),
+        name="settle",
+    )(block_out.reshape(tokens, width), grad_decoder, grad_encoded, g_attn, g_in, g_out, g_vec)
+    block_out, grad_decoder, grad_encoded = outs[:3]
+    g_attn, (g_in, g_out) = outs[3:11], outs[11:13]
+    table, gain_one, gain_two, gain_three = outs[13:]
     return (
-        block_out.reshape(decoder_in.shape),
+        block_out[None],
         grad_decoder[None],
         grad_encoded[None],
-        mine[:groups],
-        mine[groups],
+        table,
+        gain_one[0],
         g_attn[SQ],
         g_attn[SK],
         g_attn[SV],
         g_attn[SO],
-        mine[groups + 1],
+        gain_two[0],
         g_attn[CQ],
         g_attn[CK],
         g_attn[CV],
         g_attn[CO],
-        mine[groups + 2],
+        gain_three[0],
         g_in,
         g_out.T,
     )

time: 156 us -> 142 us (0.910)
  local copies, waits for them, and re-layouts: 12.3 us -> 0 us
  Pallas kernels: 142 us -> 140 us
    unnamed x9 -> x0, local copies, waits for them, and re-layouts: 8.5 us -> none
    pallas_call x1, Pallas kernels: 142 us -> 134 us  [fused(): pl.pallas_call(functools.partial(block_kernel, names, psg, batch), out_sh...]
    pallas_call x0 -> x1, Pallas kernels: none -> 5.5 us  [fused(): pl.pallas_call(settle_kernel, out_shape=tuple((jax.ShapeDtypeStruct(shape...]
    squeeze x2 -> x0, local copies, waits for them, and re-layouts: 2.47 us -> none  [the longest x1 1.95 us: fused(): g_attn[CO]]
where the time goes in v3:
time: 142 us; the launch traced here: 141 us
  Pallas kernels  140 us (99%)
  between operations  1.48 us (1%)
    pallas_call x1, Pallas kernels, fused(): pl.pallas_call(functools.partial(block_kernel, names, psg, batch), out_sh...  134 us
    pallas_call x1, Pallas kernels, fused(): pl.pallas_call(settle_kernel, out_shape=tuple((jax.ShapeDtypeStruct(shape...  5.5 us

profile of v3, /device:TPU:0, one launch (start us, length us, event | category | flops | bytes accessed | tf_op | source)
XLA Modules:
  0.0 141.4 jit_solution(6864732663972240311)
XLA Ops:
  1.3 134.4 %decoder_block.1 = (bf16[4,32,768]{2,1,0:T(8,128)(2,1)}, f32[128,768]{1,0:T(8,128)}, f32[960,768]{1,0:T(8,128)}, f32[8,24,768]{2,1,0:T(8,128)}, f32[96,768]{1,0:...) custom-call(s32[1]{0:T(128)S(6)} %copy.35.refs_0_, bf16[128,768]{1,0:T(8,128)(2,1)} %bitcast.16, bf16[128,768]{1,0:T(8,128)(2,1)} %bitcast.17, ...), custom_call_target="tpu_custom_call" | custom-call | tf_op jit(solution)/shard_map/decoder_block/pallas_call | solution.py:1080
  135.7 5.5 %settle.1 = (bf16[128,768]{1,0:T(8,128)(2,1)}, f32[128,768]{1,0:T(8,128)}, f32[960,768]{1,0:T(8,128)}, f32[24,768]{1,0:T(8,128)}, f32[24,768]{1,0:T(8,128)}, /*i...) custom-call(bf16[128,768]{1,0:T(8,128)(2,1)} %bitcast.18, ...), custom_call_target="tpu_custom_call" | custom-call | tf_op jit(solution)/shard_map/settle/pallas_call | solution.py:1101

commit v4 on v3

--- a/solution.py
+++ b/solution.py
@@ -15,14 +15,16 @@
 MASKED = -1000000000.0
 LANES = 128
 MIB = 2**20
-PAIRS = 100
+ENCODED_PARTS = 3
+PAIRS = 80
+LEAVING = 24
 
 F32 = jnp.float32
 BF16 = jnp.bfloat16
 ID = pl.DeviceIdType.MESH
 
 CK, CV, CO, CQ, SO, SK, SQ, SV = range(8)
-GATHER = ((CK, 2, False), (SK, 3, False), (SO, 1, True), (CQ, 1, True), (CO, 1, False))
+GATHER = ((CK, 2, False), (SK, 3, False), (SO, 1, True), (CQ, 1, True), (CO, 1, True))
 REDUCE = ((CO, 1, True), (CQ, 2, True), (SK, 3, True), (CK, 1, False), (CV, 1, False))
 
 
@@ -301,7 +303,7 @@
         f_swapped=low(2, width // batch, hidden // 2),
         f_came=low(3, 2, width // spans, hidden // 2),
         f_sum=full(2, width // spans, hidden // 2),
-        one_send=dma((PAIRS,)),
+        one_send=dma((LEAVING,)),
         one_recv=dma((PAIRS,)),
         a_recv=dma((runs, 2 * batch)),
         a_send=dma((runs, 4)),
@@ -369,11 +371,15 @@
         )
 
     numbers = iter(range(PAIRS))
+    leaving = []
 
     def pair(src, dst, device):
         number = next(numbers)
-        copy = remote(src, dst, r.one_send.at[number], r.one_recv.at[number], device)
-        go(copy)
+        if number >= LEAVING:
+            leaving[number - LEAVING].wait_send()
+        copy = remote(src, dst, r.one_send.at[number % LEAVING], r.one_recv.at[number], device)
+        copy.start()
+        leaving.append(copy)
         return copy
 
     loads = [
@@ -432,9 +438,14 @@
         spot = unit(run, x, c, z, h)
         remote(spot, spot, r.a_send.at[run, 0], landing(run, x, c, z, h), c_peer).wait_recv()
 
-    def wide(run, z, h):
-        if not GATHER[run][2]:
-            hand(run, side, core, z, h, 2, x_peer)
+    held = []
+
+    def wide(run, z, h, hold=False):
+        to_x = functools.partial(hand, run, side, core, z, h, 2, x_peer)
+        if hold:
+            held.append(to_x)
+        elif not GATHER[run][2]:
+            to_x()
         hand(run, side, core, z, h, 3, c_peer, r.a_core.at[run])
 
     def offer(run):
@@ -443,17 +454,17 @@
         hand(run, side, core, far, near, 1, y_peer)
         wide(run, far, near)
 
-    def from_y(run, step):
+    def from_y(run, step, hold=False):
         landed(run, side, core, places[step], 1 - near)
-        wide(run, places[step], 1 - near)
-
-    def from_line(run, step):
+        wide(run, places[step], 1 - near, hold)
+
+    def from_line(run, step, hold=False):
         z = places[step]
         landed(run, side, core, z, near)
         if step == 2:
             hand(run, side, core, z, near, 0, one_peer)
         hand(run, side, core, z, near, 1, y_peer)
-        wide(run, z, near)
+        wide(run, z, near, hold)
 
     def from_x(run, step):
         z = places[step]
@@ -539,7 +550,7 @@
     offer(1)
     m_tail.wait_recv()
     join(1)
-    own_tail = r.w.at[CQ : CQ + 2, side, span(row, band, 16), lanes(near)]
+    own_tail = r.w.at[CO : CO + 3, side, span(row, band, 16), lanes(near)]
     x_tail = pair(own_tail, own_tail, x_peer)
     v_copy = v_second(v_copy)
 
@@ -562,10 +573,10 @@
         if step == 2:
             f_hand(z, r.w_send.at[2], one_peer)
 
-    def near_units(run):
-        from_y(run, 0)
-        from_line(run, 2)
-        from_line(run, 1)
+    def near_units(run, hold=False):
+        from_y(run, 0, hold)
+        from_line(run, 2, hold)
+        from_line(run, 1, hold)
 
     def far_units(run):
         from_line(run, 3)
@@ -573,44 +584,51 @@
         from_y(run, 2)
 
     near_units(0)
-    near_units(1)
+    far_units(0)
+    near_units(1, True)
     x_tail.wait_recv()
     offer(2)
-    far_units(0)
+    from_y(0, 3)
+    for to_x in held:
+        to_x()
     far_units(1)
+    near_units(2)
     offer(3)
-    near_units(2)
-    from_y(0, 3)
+    v_copy = v_third(v_copy)
+    for step in range(3):
+        from_x(0, step)
     from_y(1, 3)
-    offer(4)
-    from_x(0, 0)
-    from_x(1, 0)
-    v_copy = v_third(v_copy)
-    far_units(2)
-    from_x(0, 1)
-    from_x(1, 1)
-    near_units(3)
-    v_fourth(v_copy)
-    from_x(0, 2)
-    from_x(1, 2)
-    from_y(2, 3)
     h_copies = [
         pair(r.h_in.at[:, other_cols], r.f.at[0, own_fan], y_peer),
         pair(r.h_out.at[:, other_cols], r.f.at[1, own_fan], y_peer),
     ]
+    far_units(2)
+    from_x(1, 0)
+    offer(4)
+    from_x(0, 3)
+    near_units(3)
+    complete(0)
+    loads[2].wait()
+    for cols in column_tiles(width):
+        r.key[:, cols] = nn(r.enc_here[...], r.w[CK, :, :, cols].reshape(width, -1)).astype(BF16)
+        r.val[:, cols] = nn(r.enc_here[...], r.w[CV, :, :, cols].reshape(width, -1)).astype(BF16)
+    v_fourth(v_copy)
+    from_y(2, 3)
     far_units(3)
-    loads[0].wait()
-    loads[1].wait()
-    from_x(0, 3)
+    from_x(1, 1)
+    from_x(1, 2)
+    near_units(4)
+    from_y(3, 3)
     from_x(1, 3)
-    from_y(3, 3)
-    near_units(4)
     for copy in h_copies:
         copy.wait_recv()
     f_hand(far, r.w_send.at[0], two_peer)
     f_hand(far, r.w_send.at[1], one_peer)
-    for run in range(3):
-        complete(run)
+    loads[0].wait()
+    loads[1].wait()
+    cot_copy = pair(r.cots.at[near], r.cots.at[near], y_peer)
+    complete(1)
+    complete(2)
     vectors = v_last()
 
     gains = [vectors[3 + i : 4 + i] for i in range(3)]
@@ -624,20 +642,12 @@
         r.res, r.n1, r.q, r.k, r.v, r.s_probs, r.mix, r.after, r.n2,
     )
     far_units(4)
-    loads[2].wait()
-    for cols in column_tiles(width):
-        r.key[:, cols] = nn(r.enc_here[...], r.w[CK, :, :, cols].reshape(width, -1)).astype(BF16)
-        r.val[:, cols] = nn(r.enc_here[...], r.w[CV, :, :, cols].reshape(width, -1)).astype(BF16)
     complete(3)
     r.qc[...] = nn(r.n2[...], matrix(CQ)).astype(BF16)
 
     cross_attend(r.qc, r.key, r.val, r.c_probs, r.o_stat, r.o_part)
     first = [pair(r.o_part.at[:, 1 - core], r.o_core, c_peer), pair(r.o_stat.at[:, 1 - core], r.o_core_stat, c_peer)]
     from_y(4, 3)
-    for step in range(SPANS):
-        from_x(4, step)
-    f_landed(2)
-    f_landed(1)
     for copy in first:
         copy.wait_recv()
     join_parts(
@@ -645,10 +655,11 @@
         r.o_to, r.o_to_stat,
     )
     second = [pair(r.o_to, r.o_x, x_peer), pair(r.o_to_stat, r.o_x_stat, x_peer)]
-    cot_copy = pair(r.cots.at[near], r.cots.at[near], y_peer)
     join_parts(
         r.o_part[side, core], r.o_stat[side, core], r.o_core[side], r.o_core_stat[side], r.o_mid, r.o_mid_stat
     )
+    f_landed(2)
+    f_landed(1)
     complete(4)
     for copy in second:
         copy.wait_recv()
@@ -1034,16 +1045,24 @@
         copy.wait()
     for run in range(len(GATHER)):
         sent_of(run)
-    for copy in sent:
+    for copy in sent + leaving[-LEAVING:]:
         copy.wait_send()
 
 
 def settle_kernel(block_out, grad_dec, grad_enc, g_attn, g_in, g_out, g_vec, *rest):
     outs, vectors, here, sems = rest[:13], rest[13:17], rest[17:23], rest[23]
-    sources = [grad_enc, block_out, grad_dec, g_attn, g_in, g_out]
+    rows = grad_enc.shape[0] // ENCODED_PARTS
+    parts = [pl.ds(number * rows, rows) for number in range(ENCODED_PARTS)]
+    moves = [(grad_enc.at[part], here[0].at[part], [outs[2].at[part]]) for part in parts]
+    moves += [
+        (block_out, here[1], [outs[0]]),
+        (grad_dec, here[2], [outs[1]]),
+        (g_in, here[4], [outs[11]]),
+        (g_out, here[5], [outs[12]]),
+        (g_attn, here[3], outs[3:11]),
+    ]
     arrivals = [
-        pltpu.make_async_copy(source, spot, sems.at[0, number])
-        for number, (source, spot) in enumerate(zip(sources, here, strict=True))
+        pltpu.make_async_copy(source, spot, sems.at[0, number]) for number, (source, spot, _) in enumerate(moves)
     ]
     for copy in arrivals:
         copy.start()
@@ -1051,9 +1070,8 @@
     for out in vectors:
         out[...] = g_vec[first : first + out.shape[0]]
         first += out.shape[0]
-    spots = [[outs[2]], [outs[0]], [outs[1]], outs[3:11], [outs[11]], [outs[12]]]
     departures = []
-    for copy, spot, places in zip(arrivals, here, spots, strict=True):
+    for copy, (_, spot, places) in zip(arrivals, moves, strict=True):
         copy.wait()
         for number, out in enumerate(places):
             source = spot if len(places) == 1 else spot.at[number]
@@ -1112,7 +1130,7 @@
             pltpu.VMEM((8, owned, width), F32),
             pltpu.VMEM((width // batch, hidden), F32),
             pltpu.VMEM((width // batch, hidden), F32),
-            pltpu.SemaphoreType.DMA((2, len(shapes))),
+            pltpu.SemaphoreType.DMA((2, len(shapes) + ENCODED_PARTS)),
         ],
         compiler_params=pltpu.CompilerParams(vmem_limit_bytes=60 * MIB),
         name="settle",

time: 142 us -> 136 us (0.958)
  Pallas kernels: 140 us -> 135 us
    pallas_call x1, Pallas kernels: 134 us -> 129 us  [fused(): pl.pallas_call(functools.partial(block_kernel, names, psg, batch), out_sh...]
where the time goes in v4:
time: 136 us
  Pallas kernels  135 us (99%)
  between operations  1.48 us (1%)
    pallas_call x1, Pallas kernels, fused(): pl.pallas_call(functools.partial(block_kernel, names, psg, batch), out_sh...  129 us
    pallas_call x1, Pallas kernels, fused(): pl.pallas_call(settle_kernel, out_shape=tuple((jax.ShapeDtypeStruct(shape...  5.15 us

profile of v4, /device:TPU:0, one launch (start us, length us, event | category | flops | bytes accessed | tf_op | source)
XLA Modules:
  0.0 136.1 jit_solution(2536533730307950759)
XLA Ops:
  1.3 129.4 %decoder_block.1 = (bf16[4,32,768]{2,1,0:T(8,128)(2,1)}, f32[128,768]{1,0:T(8,128)}, f32[960,768]{1,0:T(8,128)}, f32[8,24,768]{2,1,0:T(8,128)}, f32[96,768]{1,0:...) custom-call(s32[1]{0:T(128)S(6)} %copy.35.refs_0_, bf16[128,768]{1,0:T(8,128)(2,1)} %bitcast.16, bf16[128,768]{1,0:T(8,128)(2,1)} %bitcast.17, ...), custom_call_target="tpu_custom_call" | custom-call | tf_op jit(solution)/shard_map/decoder_block/pallas_call | solution.py:1098
  130.7 5.1 %settle.1 = (bf16[128,768]{1,0:T(8,128)(2,1)}, f32[128,768]{1,0:T(8,128)}, f32[960,768]{1,0:T(8,128)}, f32[24,768]{1,0:T(8,128)}, f32[24,768]{1,0:T(8,128)}, /*i...) custom-call(bf16[128,768]{1,0:T(8,128)(2,1)} %bitcast.18, ...), custom_call_target="tpu_custom_call" | custom-call | tf_op jit(solution)/shard_map/settle/pallas_call | solution.py:1119

commit v5 on v4

--- a/solution.py
+++ b/solution.py
@@ -626,7 +626,6 @@
     f_hand(far, r.w_send.at[1], one_peer)
     loads[0].wait()
     loads[1].wait()
-    cot_copy = pair(r.cots.at[near], r.cots.at[near], y_peer)
     complete(1)
     complete(2)
     vectors = v_last()
@@ -642,6 +641,7 @@
         r.res, r.n1, r.q, r.k, r.v, r.s_probs, r.mix, r.after, r.n2,
     )
     far_units(4)
+    cot_copy = pair(r.cots.at[near], r.cots.at[near], y_peer)
     complete(3)
     r.qc[...] = nn(r.n2[...], matrix(CQ)).astype(BF16)
 
@@ -787,11 +787,11 @@
     low = grad.astype(BF16)
     r.dcross[side, core] = low
     dcross_then = spread4(r.dcross)
-    hp_last = hp_second()
     log_end()
     mixc_end()
     dcross_end = dcross_then()
     dcross_end()
+    hp_last = hp_second()
 
     def rows_of(ref):
         return ref[...].reshape(tokens, ref.shape[-1])
@@ -902,6 +902,9 @@
             number, r.qc, dmixed, r.key, r.val, r.c_probs, ratio, dots, r.dq_part
         )
     q_first = pair(r.dq_part.at[:, 1 - core], r.dq_core, c_peer)
+    r.g[CO] = ordered(nn(turn(0, rows_of(r.mixc)), rows_of(r.dcross)), True)
+    co_begin(False)
+    co_begin(True)
     r.key[...] = r.c_probs[:, :LANES].reshape(width, -1).T
     q_first.wait_recv()
     r.dq_to[...] = (r.dq_part[1 - side, core].astype(F32) + r.dq_core[1 - side].astype(F32)).astype(BF16)
@@ -943,11 +946,9 @@
     dself_then = spread4(r.dself)
     r.dself_rest[side, core] = (grad - low.astype(F32)).astype(BF16)
     dqc_then = spread4(r.dqc)
-    r.g[CO] = ordered(nn(turn(0, rows_of(r.mixc)), rows_of(r.dcross)), True)
-    co_begin(False)
-    co_begin(True)
     r.val[...] = r.c_probs[:, LANES:].reshape(width, -1).T
     dself_end = dself_then()
+    co_forward()
     k_copy = kv_second(0, k_copy)
     v_copy = kv_first(1, r.val)
     dself_end()
@@ -961,8 +962,8 @@
     so_begin(False)
     v_copy = kv_second(1, v_copy)
     rest_then = spread4(r.dself_rest)
+    co_end = co_again()
     self_backward(dmixed, r.q, r.k, r.v, r.s_probs, r.dq, r.dk, r.dv)
-    co_forward()
     kv_third(0, k_copy)
     k_forward()
     normed = turn(3, r.n1[...])
@@ -970,7 +971,6 @@
         r.g[number] = ordered(nn(normed, ref[...]), True)
     late_begin(False)
     so_begin(True)
-    co_end = co_again()
     so_forward()
     late_begin(True)
 
@@ -1021,11 +1021,11 @@
     for cols in tiles[1:-1]:
         encoded_columns(cols)
     late_end = late_again()
+    v_end = v_finish()
     encoded_columns(tiles[-1])
     store(r.grad_enc_here, r.grad_enc)
     co_end()
     so_end()
-    v_end = v_finish()
     out_end()
     for p in range(psg):
         store(r.block_here.at[p // 2, p % 2], r.block_out.at[p])

time: 136 us -> 136 us (level)
  no operation moved by 1% of the time
where the time goes in v5:
time: 136 us
  Pallas kernels  134 us (99%)
  between operations  1.48 us (1%)
    pallas_call x1, Pallas kernels, fused(): pl.pallas_call(functools.partial(block_kernel, names, psg, batch), out_sh...  129 us
    pallas_call x1, Pallas kernels, fused(): pl.pallas_call(settle_kernel, out_shape=tuple((jax.ShapeDtypeStruct(shape...  5.15 us

profile of v5, /device:TPU:0, one launch (start us, length us, event | category | flops | bytes accessed | tf_op | source)
XLA Modules:
  0.0 135.8 jit_solution(17740798937317071543)
XLA Ops:
  1.3 129.2 %decoder_block.1 = (bf16[4,32,768]{2,1,0:T(8,128)(2,1)}, f32[128,768]{1,0:T(8,128)}, f32[960,768]{1,0:T(8,128)}, f32[8,24,768]{2,1,0:T(8,128)}, f32[96,768]{1,0:...) custom-call(s32[1]{0:T(128)S(6)} %copy.35.refs_0_, bf16[128,768]{1,0:T(8,128)(2,1)} %bitcast.16, bf16[128,768]{1,0:T(8,128)(2,1)} %bitcast.17, ...), custom_call_target="tpu_custom_call" | custom-call | tf_op jit(solution)/shard_map/decoder_block/pallas_call | solution.py:1098
  130.5 5.1 %settle.1 = (bf16[128,768]{1,0:T(8,128)(2,1)}, f32[128,768]{1,0:T(8,128)}, f32[960,768]{1,0:T(8,128)}, f32[24,768]{1,0:T(8,128)}, f32[24,768]{1,0:T(8,128)}, /*i...) custom-call(bf16[128,768]{1,0:T(8,128)(2,1)} %bitcast.18, ...), custom_call_target="tpu_custom_call" | custom-call | tf_op jit(solution)/shard_map/settle/pallas_call | solution.py:1119

commit v6 on v5

--- a/solution.py
+++ b/solution.py
@@ -16,8 +16,8 @@
 LANES = 128
 MIB = 2**20
 ENCODED_PARTS = 3
-PAIRS = 80
-LEAVING = 24
+PAIRS = 78
+LEAVING = 16
 
 F32 = jnp.float32
 BF16 = jnp.bfloat16
@@ -112,7 +112,7 @@
     sums = jnp.ones((tokens, LANES), F32)
     for pair in range(HEADS // 2):
         cols = pair_lanes(pair)
-        scores = nt(stack_heads(qc[:, cols]), key[:, cols]) * scale
+        scores = nt(stack_heads(qc[:, cols] * scale), key[:, cols])
         top = jnp.max(scores, -1, keepdims=True)
         expo = jnp.exp(scores - top)
         total = jnp.sum(expo, -1, keepdims=True)
@@ -239,7 +239,7 @@
         g_out_here=full(width // batch, hidden),
         g_vec_here=full(8, owned),
         load=dma((3,)),
-        store=dma((16,)),
+        store=dma((14,)),
         key=low(length, width),
         val=low(length, width),
         c_probs=low(pairs, 2 * tokens, length),
@@ -305,7 +305,7 @@
         f_sum=full(2, width // spans, hidden // 2),
         one_send=dma((LEAVING,)),
         one_recv=dma((PAIRS,)),
-        a_recv=dma((runs, 2 * batch)),
+        a_recv=dma((sum(1 if joined else 2 for _, _, joined in GATHER) * batch,)),
         a_send=dma((runs, 4)),
         a_core=dma((runs,)),
         w_recv=dma((spans,)),
@@ -428,7 +428,7 @@
         return r.w.at[first : first + count, slice(None) if joined else x, rows, lanes(h)]
 
     def landing(run, x, c, z, h):
-        return r.a_recv.at[run, (0 if GATHER[run][2] else x) * batch + z * 2 + h]
+        return r.a_recv.at[sum(1 if joined else 2 for _, _, joined in GATHER[:run]) * batch + (0 if GATHER[run][2] else x) * batch + z * 2 + h]
 
     def hand(run, x, c, z, h, kind, device, recv=None):
         spot = unit(run, x, c, z, h)

time: 136 us -> 136 us (level)
  no operation moved by 1% of the time
where the time goes in v6:
time: 136 us; the launch traced here: 135 us
  Pallas kernels  134 us (99%)
  between operations  1.48 us (1%)
    pallas_call x1, Pallas kernels, fused(): pl.pallas_call(functools.partial(block_kernel, names, psg, batch), out_sh...  129 us
    pallas_call x1, Pallas kernels, fused(): pl.pallas_call(settle_kernel, out_shape=tuple((jax.ShapeDtypeStruct(shape...  5.15 us

profile of v6, /device:TPU:0, one launch (start us, length us, event | category | flops | bytes accessed | tf_op | source)
XLA Modules:
  0.0 135.5 jit_solution(16393573373176435589)
XLA Ops:
  1.3 128.9 %decoder_block.1 = (bf16[4,32,768]{2,1,0:T(8,128)(2,1)}, f32[128,768]{1,0:T(8,128)}, f32[960,768]{1,0:T(8,128)}, f32[8,24,768]{2,1,0:T(8,128)}, f32[96,768]{1,0:...) custom-call(s32[1]{0:T(128)S(6)} %copy.35.refs_0_, bf16[128,768]{1,0:T(8,128)(2,1)} %bitcast.16, bf16[128,768]{1,0:T(8,128)(2,1)} %bitcast.17, ...), custom_call_target="tpu_custom_call" | custom-call | tf_op jit(solution)/shard_map/decoder_block/pallas_call | solution.py:1098
  130.2 5.1 %settle.1 = (bf16[128,768]{1,0:T(8,128)(2,1)}, f32[128,768]{1,0:T(8,128)}, f32[960,768]{1,0:T(8,128)}, f32[24,768]{1,0:T(8,128)}, f32[24,768]{1,0:T(8,128)}, /*i...) custom-call(bf16[128,768]{1,0:T(8,128)(2,1)} %bitcast.18, ...), custom_call_target="tpu_custom_call" | custom-call | tf_op jit(solution)/shard_map/settle/pallas_call | solution.py:1119
